TPU v7x, 32 devices: a whole 2x2x4 slice. The times are simulated.
32 devices in a mesh: dp: 4 (over y, x), noise: 8 (over z, core).
Axes of the slice: x: 2, y: 2, z: 4, core: 2. Of those that a mesh axis runs over, the one named last changes fastest.
Arguments:
- prefix_rows: bfloat16 [2, 32, 816, 640], P(None, ('dp', 'noise')), may hold values from -6 to 6
- action_rows: bfloat16 [2, 32, 50, 1024], P(None, ('dp', 'noise')), may hold values from -6 to 6
- segment_item: int32 [2, 32], P(None, ('dp', 'noise')), may hold values from 0 to 7
- segment_time: int32 [2, 32], P(None, ('dp', 'noise')), may hold values from 0 to 15
- item_weight: int32 [2, 32], P(None, 'dp'), may hold values from 0 to 15
- prefix_len: int32 [2, 32], P(None, 'dp'), may hold values from 204 to 816, as said below
- vlm_prenorm: bfloat16 [640], P(('dp', 'noise')), may hold values from 0.5 to 1.5
- vlm_query: bfloat16 [640, 1024], P(('dp', 'noise')), may hold values from -0.25 to 0.25
- vlm_key: bfloat16 [640, 256], P(('dp', 'noise')), may hold values from -0.25 to 0.25
- vlm_value: bfloat16 [640, 256], P(('dp', 'noise')), may hold values from -0.25 to 0.25
- vlm_mixer: bfloat16 [1024, 640], P(('dp', 'noise')), may hold values from -1.5 to 1.5
- vlm_midnorm: bfloat16 [640], P(('dp', 'noise')), may hold values from 0.5 to 1.5
- vlm_gate: bfloat16 [640, 2048], P(('dp', 'noise')), may hold values from -0.25 to 0.25
- vlm_expand: bfloat16 [640, 2048], P(('dp', 'noise')), may hold values from -0.25 to 0.25
- vlm_down: bfloat16 [2048, 640], P(('dp', 'noise')), may hold values from -0.125 to 0.125
- act_prenorm: bfloat16 [1024], P(('dp', 'noise')), may hold values from 0.5 to 1.5
- act_query: bfloat16 [1024, 1024], P(('dp', 'noise')), may hold values from -0.1875 to 0.1875
- act_key: bfloat16 [1024, 256], P(('dp', 'noise')), may hold values from -0.1875 to 0.1875
- act_value: bfloat16 [1024, 256], P(('dp', 'noise')), may hold values from -0.1875 to 0.1875
- act_mixer: bfloat16 [1024, 1024], P(('dp', 'noise')), may hold values from -1.5 to 1.5
- act_midnorm: bfloat16 [1024], P(('dp', 'noise')), may hold values from 0.5 to 1.5
- act_gate: bfloat16 [1024, 4096], P(('dp', 'noise')), may hold values from -0.1875 to 0.1875
- act_expand: bfloat16 [1024, 4096], P(('dp', 'noise')), may hold values from -0.1875 to 0.1875
- act_down: bfloat16 [4096, 1024], P(('dp', 'noise')), may hold values from -0.09375 to 0.09375
- time_scales: bfloat16 [2048, 16], P(('dp', 'noise')), may hold values from 0.099609375 to 1.8984375
- cot_prefix: bfloat16 [2, 32, 816, 640], P(None, ('dp', 'noise')), may hold values from -6 to 6
- cot_action: bfloat16 [2, 32, 50, 1024], P(None, ('dp', 'noise')), may hold values from -6 to 6
Outputs:
- prefix_out: bfloat16 [2, 32, 816, 640], P(None, ('dp', 'noise'))
- action_out: bfloat16 [2, 32, 50, 1024], P(None, ('dp', 'noise'))
- prefix_grad: float32 [2, 32, 816, 640], P(None, ('dp', 'noise'))
- action_grad: float32 [2, 32, 50, 1024], P(None, ('dp', 'noise'))
- prefgrad_prenorm: float32 [640], P(('dp', 'noise'))
- prefgrad_query: float32 [640, 1024], P(('dp', 'noise'))
- prefgrad_key: float32 [640, 256], P(('dp', 'noise'))
- prefgrad_value: float32 [640, 256], P(('dp', 'noise'))
- prefgrad_mixer: float32 [1024, 640], P(('dp', 'noise'))
- prefgrad_midnorm: float32 [640], P(('dp', 'noise'))
- prefgrad_gate: float32 [640, 2048], P(('dp', 'noise'))
- prefgrad_expand: float32 [640, 2048], P(('dp', 'noise'))
- prefgrad_down: float32 [2048, 640], P(('dp', 'noise'))
- actgrad_prenorm: float32 [1024], P(('dp', 'noise'))
- actgrad_query: float32 [1024, 1024], P(('dp', 'noise'))
- actgrad_key: float32 [1024, 256], P(('dp', 'noise'))
- actgrad_value: float32 [1024, 256], P(('dp', 'noise'))
- actgrad_mixer: float32 [1024, 1024], P(('dp', 'noise'))
- actgrad_midnorm: float32 [1024], P(('dp', 'noise'))
- actgrad_gate: float32 [1024, 4096], P(('dp', 'noise'))
- actgrad_expand: float32 [1024, 4096], P(('dp', 'noise'))
- actgrad_down: float32 [4096, 1024], P(('dp', 'noise'))
- scales_grad: float32 [2048, 16], P(('dp', 'noise'))
Inputs may be any that keep to these rules, and one draw needn't show every extreme that they name: `segment_item`: numbers the segment's item within its data group of 8 items. `prefix_len`: prefix keys at positions of len or later are never attended.
All inputs are finite; a program needn't handle non-finite values.
Results may differ from a plain program's by a relative error of at most 0.015.
Values may be sent and summed in bfloat16 or wider, within the bound.
No kernel may reach another device: no remote copies, remote signals or barrier semaphores. Data moves between devices by JAX's collectives and lax.ppermute only.
A program may use at most 448 MiB of HBM per device.

v0:
```python
import jax
import jax.numpy as jnp
from jax import lax
from jax.sharding import PartitionSpec as P

EPS = 1e-06
HIGH = lax.Precision.HIGHEST


def normed(rows):
    factor = lax.rsqrt(jnp.mean(rows * rows, axis=-1, keepdims=True) + EPS)
    return (rows * factor, factor)


def norm_back(grad_hidden, normal, factor, gain_mod):
    grad_normal = grad_hidden * gain_mod
    centred = jnp.mean(grad_normal * normal, axis=-1, keepdims=True)
    return factor * (grad_normal - normal * centred)


def flatten(array):
    return array.reshape(-1, array.shape[-1])


def weight_grad(inputs, grads):
    return jnp.einsum(
        "ra,rb->ab", flatten(inputs), flatten(grads), preferred_element_type=jnp.float32
    )


def back_through(grads, weight):
    return jnp.einsum("...b,ab->...a", grads, weight, preferred_element_type=jnp.float32)


def scores_of(queries, keys, valid):
    batch, rows, width = queries.shape
    depth = keys.shape[-1]
    split = queries.reshape(batch, rows, width // depth, depth)
    scores = jnp.einsum(
        "bnhd,bmd->bhnm", split, keys, preferred_element_type=jnp.float32
    ) * depth ** (-0.5)
    return (split, jnp.where(valid[:, None, None, :], scores, -1e30))


def attend(queries, keys, values, valid):
    split, scores = scores_of(queries, keys, valid)
    top = jnp.max(scores, axis=-1, keepdims=True)
    total = top + jnp.log(jnp.sum(jnp.exp(scores - top), axis=-1, keepdims=True))
    probs = jnp.exp(scores - total).astype(jnp.bfloat16)
    mixed = jnp.einsum("bhnm,bmd->bnhd", probs, values, preferred_element_type=jnp.float32)
    return (mixed.reshape(queries.shape).astype(jnp.bfloat16), total)


def attend_back(queries, keys, values, valid, total, grad_mixed):
    split, scores = scores_of(queries, keys, valid)
    depth = keys.shape[-1]
    probs = jnp.exp(scores - total)
    grad_split = grad_mixed.reshape(split.shape)
    grad_values = jnp.einsum(
        "bhnm,bnhd->bmd", probs.astype(jnp.bfloat16), grad_split, preferred_element_type=jnp.float32
    )
    grad_probs = jnp.einsum(
        "bnhd,bmd->bhnm", grad_split, values, preferred_element_type=jnp.float32
    )
    centred = jnp.sum(probs * grad_probs, axis=-1, keepdims=True)
    grad_scores = (probs * (grad_probs - centred) * depth ** (-0.5)).astype(jnp.bfloat16)
    grad_queries = jnp.einsum(
        "bhnm,bmd->bnhd", grad_scores, keys, preferred_element_type=jnp.float32
    )
    grad_keys = jnp.einsum("bhnm,bnhd->bmd", grad_scores, split, preferred_element_type=jnp.float32)
    return (grad_queries.reshape(queries.shape).astype(jnp.bfloat16), grad_keys, grad_values)


def feed(hidden, w_gate, w_up, w_down):
    gate = jnp.dot(hidden, w_gate, preferred_element_type=jnp.float32)
    upward = jnp.dot(hidden, w_up, preferred_element_type=jnp.float32)
    middle = (jax.nn.gelu(gate) * upward).astype(jnp.bfloat16)
    return (jnp.dot(middle, w_down, preferred_element_type=jnp.float32), gate, upward, middle)


def feed_back(grad_rows, hidden, gate, upward, middle, w_gate, w_up, w_down):
    inner_width = middle.shape[-1]
    grad_out = flatten(grad_rows.astype(jnp.bfloat16))
    flat_mid = flatten(middle)
    flat_hidden = flatten(hidden)
    grad_mid = jnp.einsum("rd,fd->rf", grad_out, w_down, preferred_element_type=jnp.float32)
    activated, pullback = jax.vjp(jax.nn.gelu, gate.reshape(-1, inner_width))
    grad_gate = pullback(grad_mid * upward.reshape(-1, inner_width))[0].astype(jnp.bfloat16)
    grad_upward = (grad_mid * activated).astype(jnp.bfloat16)
    grad_hidden = jnp.einsum("rf,df->rd", grad_gate, w_gate, preferred_element_type=jnp.float32)
    grad_hidden = grad_hidden + jnp.einsum(
        "rf,df->rd", grad_upward, w_up, preferred_element_type=jnp.float32
    )
    return (
        grad_hidden.reshape(hidden.shape),
        [(flat_hidden, grad_gate), (flat_hidden, grad_upward), (flat_mid, grad_out)],
    )


def assemble(mats, smalls, depth):
    (
        pre_dquery,
        pre_djoint,
        pre_dmixer,
        pre_dgate,
        pre_dexpand,
        pre_ddown,
        suf_dquery,
        suf_djoint,
        suf_dmixer,
        suf_dgate,
        suf_dexpand,
        suf_ddown,
    ) = mats
    pre_dgain, pre_dmid, suf_dgain, suf_dmid, time_dtable = smalls
    return (
        pre_dgain,
        pre_dquery,
        pre_djoint[:, :depth],
        pre_djoint[:, depth:],
        pre_dmixer,
        pre_dmid,
        pre_dgate,
        pre_dexpand,
        pre_ddown,
        suf_dgain,
        suf_dquery,
        suf_djoint[:, :depth],
        suf_djoint[:, depth:],
        suf_dmixer,
        suf_dmid,
        suf_dgate,
        suf_dexpand,
        suf_ddown,
        time_dtable,
    )


def per_device(
    prefix_rows,
    action_rows,
    segment_item,
    segment_time,
    item_weight,
    prefix_len,
    vlm_prenorm,
    vlm_query,
    vlm_key,
    vlm_value,
    vlm_mixer,
    vlm_midnorm,
    vlm_gate,
    vlm_expand,
    vlm_down,
    act_prenorm,
    act_query,
    act_key,
    act_value,
    act_mixer,
    act_midnorm,
    act_gate,
    act_expand,
    act_down,
    time_scales,
    cot_prefix,
    cot_action,
):
    micro, items, prefix, width = prefix_rows.shape
    segments, seg_len, suf_width = (
        action_rows.shape[1],
        action_rows.shape[2],
        action_rows.shape[3],
    )
    group = prefix_len.shape[1]
    depth = vlm_key.shape[1]
    levels = time_scales.shape[1]
    place = lax.axis_index("noise") * items
    positions = jnp.arange(prefix, dtype=jnp.int32)
    group_ids = jnp.arange(group, dtype=jnp.int32)
    prefix_outs = []
    action_outs = []
    prefix_grads = []
    action_grads = []
    shards = None
    small_totals = None
    pair_lists = None
    whole = (
        lax.all_gather(vlm_prenorm, ("dp", "noise"), axis=0, tiled=True),
        lax.all_gather(vlm_query, ("dp", "noise"), axis=0, tiled=True),
        lax.all_gather(vlm_key, ("dp", "noise"), axis=0, tiled=True),
        lax.all_gather(vlm_value, ("dp", "noise"), axis=0, tiled=True),
        lax.all_gather(vlm_mixer, ("dp", "noise"), axis=0, tiled=True),
        lax.all_gather(vlm_midnorm, ("dp", "noise"), axis=0, tiled=True),
        lax.all_gather(vlm_gate, ("dp", "noise"), axis=0, tiled=True),
        lax.all_gather(vlm_expand, ("dp", "noise"), axis=0, tiled=True),
        lax.all_gather(vlm_down, ("dp", "noise"), axis=0, tiled=True),
        lax.all_gather(act_prenorm, ("dp", "noise"), axis=0, tiled=True),
        lax.all_gather(act_query, ("dp", "noise"), axis=0, tiled=True),
        lax.all_gather(act_key, ("dp", "noise"), axis=0, tiled=True),
        lax.all_gather(act_value, ("dp", "noise"), axis=0, tiled=True),
        lax.all_gather(act_mixer, ("dp", "noise"), axis=0, tiled=True),
        lax.all_gather(act_midnorm, ("dp", "noise"), axis=0, tiled=True),
        lax.all_gather(act_gate, ("dp", "noise"), axis=0, tiled=True),
        lax.all_gather(act_expand, ("dp", "noise"), axis=0, tiled=True),
        lax.all_gather(act_down, ("dp", "noise"), axis=0, tiled=True),
        lax.all_gather(time_scales, ("dp", "noise"), axis=0, tiled=True),
    )
    (
        pre_gain,
        pre_query,
        pre_key,
        pre_value,
        pre_mixer,
        pre_midgain,
        pre_gate,
        pre_expand,
        pre_down,
        suf_gain,
        suf_query,
        suf_key,
        suf_value,
        suf_mixer,
        suf_midgain,
        suf_gate,
        suf_expand,
        suf_down,
        time_table,
    ) = whole
    pre_joint = jnp.concatenate([pre_key, pre_value], axis=1)
    suf_joint = jnp.concatenate([suf_key, suf_value], axis=1)
    for step in range(micro):
        prefix_in = prefix_rows[step].astype(jnp.float32)
        first_normal, first_scale = normed(prefix_in)
        first_hidden = (first_normal * pre_gain).astype(jnp.bfloat16)
        prefix_queries = jnp.dot(
            first_hidden, pre_query, preferred_element_type=jnp.float32
        ).astype(jnp.bfloat16)
        prefix_kv = jnp.dot(first_hidden, pre_joint, preferred_element_type=jnp.float32).astype(
            jnp.bfloat16
        )
        group_kv = lax.all_gather(prefix_kv, "noise", axis=0, tiled=True)
        own_len = lax.dynamic_slice_in_dim(prefix_len[step], place, items)
        prefix_valid = positions[None, :] < own_len[:, None]
        prefix_keys = prefix_kv[..., :depth]
        prefix_values = prefix_kv[..., depth:]
        prefix_attn, prefix_total = attend(prefix_queries, prefix_keys, prefix_values, prefix_valid)
        prefix_resid = prefix_in + jnp.dot(
            prefix_attn, pre_mixer, preferred_element_type=jnp.float32
        )
        second_normal, second_scale = normed(prefix_resid)
        second_hidden = (second_normal * pre_midgain).astype(jnp.bfloat16)
        prefix_branch, prefix_gate, prefix_upward, prefix_mid = feed(
            second_hidden, pre_gate, pre_expand, pre_down
        )
        prefix_outs.append((prefix_resid + prefix_branch).astype(jnp.bfloat16))
        action_in = action_rows[step].astype(jnp.float32)
        item_match = segment_item[step][:, None] == group_ids[None, :]
        item_hot = item_match.astype(jnp.float32)
        time_hot = (segment_time[step][:, None] == jnp.arange(levels)[None, :]).astype(jnp.float32)
        modulation = jnp.einsum(
            "ct,jt->cj", time_hot, time_table.astype(jnp.float32), precision=HIGH
        )
        first_mod = modulation[:, None, :suf_width]
        second_mod = modulation[:, None, suf_width:]
        seg_length = jnp.sum(jnp.where(item_match, prefix_len[step][None, :], 0), axis=1)
        seg_weight = (
            jnp.sum(jnp.where(item_match, item_weight[step][None, :], 0), axis=1) + 1
        ).astype(jnp.float32) / 8.0
        action_normal, action_scale = normed(action_in)
        action_hidden = (action_normal * suf_gain * first_mod).astype(jnp.bfloat16)
        action_queries = jnp.dot(
            action_hidden, suf_query, preferred_element_type=jnp.float32
        ).astype(jnp.bfloat16)
        action_kv = jnp.dot(action_hidden, suf_joint, preferred_element_type=jnp.float32).astype(
            jnp.bfloat16
        )
        joined_kv = jnp.concatenate([group_kv[segment_item[step]], action_kv], axis=1)
        action_keys = joined_kv[..., :depth]
        action_values = joined_kv[..., depth:]
        action_valid = jnp.concatenate(
            [positions[None, :] < seg_length[:, None], jnp.ones((segments, seg_len), dtype=bool)],
            axis=1,
        )
        action_attn, action_total = attend(action_queries, action_keys, action_values, action_valid)
        action_resid = action_in + jnp.dot(
            action_attn, suf_mixer, preferred_element_type=jnp.float32
        )
        late_normal, late_scale = normed(action_resid)
        late_hidden = (late_normal * suf_midgain * second_mod).astype(jnp.bfloat16)
        action_branch, action_gate, action_upward, action_mid = feed(
            late_hidden, suf_gate, suf_expand, suf_down
        )
        action_outs.append((action_resid + action_branch).astype(jnp.bfloat16))
        grad_action = cot_action[step].astype(jnp.float32) * seg_weight[:, None, None]
        grad_late, suf_ffpairs = feed_back(
            grad_action,
            late_hidden,
            action_gate,
            action_upward,
            action_mid,
            suf_gate,
            suf_expand,
            suf_down,
        )
        late_back = grad_late * late_normal
        suf_dmid = jnp.sum(late_back * second_mod, axis=(0, 1))
        second_dmod = jnp.sum(late_back * suf_midgain, axis=1)
        action_dresid = grad_action + norm_back(
            grad_late, late_normal, late_scale, suf_midgain * second_mod
        )
        action_dmixed = action_dresid.astype(jnp.bfloat16)
        action_dattn = back_through(action_dmixed, suf_mixer).astype(jnp.bfloat16)
        action_dq, action_dkeys, action_dvalues = attend_back(
            action_queries, action_keys, action_values, action_valid, action_total, action_dattn
        )
        segment_dkv = jnp.concatenate(
            [action_dkeys[:, :prefix], action_dvalues[:, :prefix]], axis=-1
        )
        own_dkv = jnp.concatenate(
            [action_dkeys[:, prefix:], action_dvalues[:, prefix:]], axis=-1
        ).astype(jnp.bfloat16)
        group_dkv = jnp.einsum("cg,cpe->gpe", item_hot, segment_dkv, precision=HIGH)
        mine_dkv = lax.psum_scatter(
            group_dkv.astype(jnp.bfloat16), "noise", scatter_dimension=0, tiled=True
        ).astype(jnp.float32)
        action_dhidden = back_through(action_dq, suf_query) + back_through(own_dkv, suf_joint)
        first_back = action_dhidden * action_normal
        suf_dgain = jnp.sum(first_back * first_mod, axis=(0, 1))
        first_dmod = jnp.sum(first_back * suf_gain, axis=1)
        action_grads.append(
            action_dresid
            + norm_back(action_dhidden, action_normal, action_scale, suf_gain * first_mod)
        )
        time_dtable = jnp.einsum(
            "cj,ct->jt",
            jnp.concatenate([first_dmod, second_dmod], axis=-1),
            time_hot,
            precision=HIGH,
        )
        grad_prefix = cot_prefix[step].astype(jnp.float32)
        grad_second, pre_ffpairs = feed_back(
            grad_prefix,
            second_hidden,
            prefix_gate,
            prefix_upward,
            prefix_mid,
            pre_gate,
            pre_expand,
            pre_down,
        )
        pre_dmid = jnp.sum(grad_second * second_normal, axis=(0, 1))
        prefix_dresid = grad_prefix + norm_back(
            grad_second, second_normal, second_scale, pre_midgain
        )
        prefix_dmixed = prefix_dresid.astype(jnp.bfloat16)
        prefix_dattn = back_through(prefix_dmixed, pre_mixer).astype(jnp.bfloat16)
        prefix_dq, prefix_dkeys, prefix_dvalues = attend_back(
            prefix_queries, prefix_keys, prefix_values, prefix_valid, prefix_total, prefix_dattn
        )
        prefix_dkv = (jnp.concatenate([prefix_dkeys, prefix_dvalues], axis=-1) + mine_dkv).astype(
            jnp.bfloat16
        )
        prefix_dhidden = back_through(prefix_dq, pre_query) + back_through(prefix_dkv, pre_joint)
        pre_dgain = jnp.sum(prefix_dhidden * first_normal, axis=(0, 1))
        prefix_grads.append(
            prefix_dresid + norm_back(prefix_dhidden, first_normal, first_scale, pre_gain)
        )
        pairs = [
            (flatten(first_hidden), flatten(prefix_dq)),
            (flatten(first_hidden), flatten(prefix_dkv)),
            (flatten(prefix_attn), flatten(prefix_dmixed)),
        ] + pre_ffpairs
        pairs = (
            pairs
            + [
                (flatten(action_hidden), flatten(action_dq)),
                (flatten(action_hidden), flatten(own_dkv)),
                (flatten(action_attn), flatten(action_dmixed)),
            ]
            + suf_ffpairs
        )
        smalls = (pre_dgain, pre_dmid, suf_dgain, suf_dmid, time_dtable)
        small_totals = (
            smalls
            if small_totals is None
            else tuple((left + right for left, right in zip(small_totals, smalls)))
        )
        pair_lists = (
            [[pair] for pair in pairs]
            if pair_lists is None
            else [kept + [pair] for kept, pair in zip(pair_lists, pairs)]
        )
    mats = tuple(
        (
            weight_grad(
                jnp.concatenate([pair[0] for pair in kept], axis=0),
                jnp.concatenate([pair[1] for pair in kept], axis=0),
            )
            for kept in pair_lists
        )
    )
    grads = assemble(mats, small_totals, depth)
    shards = (
        lax.psum_scatter(grads[0], ("dp", "noise"), scatter_dimension=0, tiled=True),
        lax.psum_scatter(grads[1], ("dp", "noise"), scatter_dimension=0, tiled=True),
        lax.psum_scatter(grads[2], ("dp", "noise"), scatter_dimension=0, tiled=True),
        lax.psum_scatter(grads[3], ("dp", "noise"), scatter_dimension=0, tiled=True),
        lax.psum_scatter(grads[4], ("dp", "noise"), scatter_dimension=0, tiled=True),
        lax.psum_scatter(grads[5], ("dp", "noise"), scatter_dimension=0, tiled=True),
        lax.psum_scatter(grads[6], ("dp", "noise"), scatter_dimension=0, tiled=True),
        lax.psum_scatter(grads[7], ("dp", "noise"), scatter_dimension=0, tiled=True),
        lax.psum_scatter(grads[8], ("dp", "noise"), scatter_dimension=0, tiled=True),
        lax.psum_scatter(grads[9], ("dp", "noise"), scatter_dimension=0, tiled=True),
        lax.psum_scatter(grads[10], ("dp", "noise"), scatter_dimension=0, tiled=True),
        lax.psum_scatter(grads[11], ("dp", "noise"), scatter_dimension=0, tiled=True),
        lax.psum_scatter(grads[12], ("dp", "noise"), scatter_dimension=0, tiled=True),
        lax.psum_scatter(grads[13], ("dp", "noise"), scatter_dimension=0, tiled=True),
        lax.psum_scatter(grads[14], ("dp", "noise"), scatter_dimension=0, tiled=True),
        lax.psum_scatter(grads[15], ("dp", "noise"), scatter_dimension=0, tiled=True),
        lax.psum_scatter(grads[16], ("dp", "noise"), scatter_dimension=0, tiled=True),
        lax.psum_scatter(grads[17], ("dp", "noise"), scatter_dimension=0, tiled=True),
        lax.psum_scatter(grads[18], ("dp", "noise"), scatter_dimension=0, tiled=True),
    )
    return (
        jnp.stack(prefix_outs),
        jnp.stack(action_outs),
        jnp.stack(prefix_grads),
        jnp.stack(action_grads),
        shards[0],
        shards[1],
        shards[2],
        shards[3],
        shards[4],
        shards[5],
        shards[6],
        shards[7],
        shards[8],
        shards[9],
        shards[10],
        shards[11],
        shards[12],
        shards[13],
        shards[14],
        shards[15],
        shards[16],
        shards[17],
        shards[18],
    )


def solution(mesh):
    return jax.shard_map(
        per_device,
        mesh=mesh,
        in_specs=(
            P(None, ("dp", "noise"), None, None),
            P(None, ("dp", "noise"), None, None),
            P(None, ("dp", "noise")),
            P(None, ("dp", "noise")),
            P(None, "dp"),
            P(None, "dp"),
            P(("dp", "noise")),
            P(("dp", "noise"), None),
            P(("dp", "noise"), None),
            P(("dp", "noise"), None),
            P(("dp", "noise"), None),
            P(("dp", "noise")),
            P(("dp", "noise"), None),
            P(("dp", "noise"), None),
            P(("dp", "noise"), None),
            P(("dp", "noise")),
            P(("dp", "noise"), None),
            P(("dp", "noise"), None),
            P(("dp", "noise"), None),
            P(("dp", "noise"), None),
            P(("dp", "noise")),
            P(("dp", "noise"), None),
            P(("dp", "noise"), None),
            P(("dp", "noise"), None),
            P(("dp", "noise"), None),
            P(None, ("dp", "noise"), None, None),
            P(None, ("dp", "noise"), None, None),
        ),
        out_specs=(
            P(None, ("dp", "noise"), None, None),
            P(None, ("dp", "noise"), None, None),
            P(None, ("dp", "noise"), None, None),
            P(None, ("dp", "noise"), None, None),
            P(("dp", "noise")),
            P(("dp", "noise"), None),
            P(("dp", "noise"), None),
            P(("dp", "noise"), None),
            P(("dp", "noise"), None),
            P(("dp", "noise")),
            P(("dp", "noise"), None),
            P(("dp", "noise"), None),
            P(("dp", "noise"), None),
            P(("dp", "noise")),
            P(("dp", "noise"), None),
            P(("dp", "noise"), None),
            P(("dp", "noise"), None),
            P(("dp", "noise"), None),
            P(("dp", "noise")),
            P(("dp", "noise"), None),
            P(("dp", "noise"), None),
            P(("dp", "noise"), None),
            P(("dp", "noise"), None),
        ),
        check_vma=False,
    )
```

profile of v0, /device:TPU:0, one launch (start us, length us, event | category | flops | bytes accessed | tf_op | source)
XLA Modules:
  0.0 2581.9 jit_solution(1534238184578053595)
XLA Ops:
  11.4 42.1 %all-reduce.21 = (bf16[640]{0:T(1024)(128)(2,1)S(1)}, bf16[640]{0:T(1024)(128)(2,1)}, bf16[1024]{0:T(1024)(128)(2,1)S(1)}, bf16[1024]{0:T(1024)(128)(2,1)S(1)}) all-reduce(bf16[640]{0:T(1024)(128)(2,1)S(1)} %dynamic-update-slice.2, bf16[640]{0:T(1024)(128)(2,1)S(1)} %dynamic-update-slice.3, ...), channel_id=1, replica_groups=mesh['dp'=4,'noise'=8] {'dp','noise'}, use_global_device_ids=true, to_apply=%add.2 | all-reduce | flops 3328 | bytes 13312
  53.5 42.4 %all-gather.2 = bf16[32,20,256]{2,1,0:T(8,128)(2,1)S(1)} all-gather(bf16[1,20,256]{2,1,0:T(8,128)(2,1)} %bitcast.762), channel_id=1, replica_groups=mesh['dp'=4,'noise'=8] {'dp','noise'}, dimensions={0}, use_global_device_ids=true | all-gather | bytes 337920 | tf_op jit(solution)/shard_map/all_gather | solution.py:190
  95.9 38.6 %all-gather.3 = bf16[32,20,256]{2,1,0:T(8,128)(2,1)S(1)} all-gather(bf16[1,20,256]{2,1,0:T(8,128)(2,1)} %bitcast.763), channel_id=1, replica_groups=mesh['dp'=4,'noise'=8] {'dp','noise'}, dimensions={0}, use_global_device_ids=true | all-gather | bytes 337920 | tf_op jit(solution)/shard_map/all_gather | solution.py:191
  151.3 39.8 %all-gather.7 = bf16[32,64,16]{1,2,0:T(8,128)(2,1)S(1)} all-gather(bf16[1,64,16]{1,2,0:T(8,128)(2,1)S(1)} %bitcast.764), channel_id=1, replica_groups=mesh['dp'=4,'noise'=8] {'dp','noise'}, dimensions={0}, use_global_device_ids=true | all-gather | bytes 67584 | tf_op jit(solution)/shard_map/all_gather | solution.py:206
  202.1 39.0 %all_gather.75 = bf16[1024,256]{1,0:T(8,128)(2,1)S(1)} all-gather(bf16[32,256]{1,0:T(8,128)(2,1)S(1)} %copy-done.188), channel_id=1, replica_groups=mesh['dp'=4,'noise'=8] {'dp','noise'}, dimensions={0}, use_global_device_ids=true | all-gather | bytes 540672 | tf_op jit(solution)/shard_map/all_gather | solution.py:199
  241.2 41.0 %all_gather.76 = bf16[1024,256]{1,0:T(8,128)(2,1)S(1)} all-gather(bf16[32,256]{1,0:T(8,128)(2,1)S(1)} %copy-done.189), channel_id=1, replica_groups=mesh['dp'=4,'noise'=8] {'dp','noise'}, dimensions={0}, use_global_device_ids=true | all-gather | bytes 540672 | tf_op jit(solution)/shard_map/all_gather | solution.py:200
  293.9 41.1 %all-gather.37.cloned.1.call-done = bf16[6528,512]{1,0:T(8,128)(2,1)} async-done(((bf16[816,512]{1,0:T(8,128)(2,1)}), bf16[6528,512]{1,0:T(8,128)(2,1)}) %all-gather.37.cloned.1.call-update) | async-done | bytes 6684688 | tf_op jit(solution)/shard_map/all_gather | solution.py:241
  339.2 74.6 %all-gather.31.cloned.1.call-done = bf16[1024,4096]{1,0:T(8,128)(2,1)} async-done(((bf16[32,4096]{1,0:T(8,128)(2,1)}), bf16[1024,4096]{1,0:T(8,128)(2,1)}) %all-gather.31.cloned.1.call-update) | async-done | bytes 8388624 | tf_op jit(solution)/shard_map/all_gather | solution.py:204
  413.9 5.9 fusion.329
  419.8 72.9 %all-gather.29.cloned.1.call-done = bf16[1024,4096]{1,0:T(8,128)(2,1)} async-done(((bf16[32,4096]{1,0:T(8,128)(2,1)}), bf16[1024,4096]{1,0:T(8,128)(2,1)}) %all-gather.29.cloned.1.call-update) | async-done | bytes 8388624 | tf_op jit(solution)/shard_map/all_gather | solution.py:203
  492.7 6.0 fusion.328
  503.9 67.7 %all-gather.33.cloned.1.call-done = bf16[4096,1024]{1,0:T(8,128)(2,1)} async-done(((bf16[128,1024]{1,0:T(8,128)(2,1)}), bf16[4096,1024]{1,0:T(8,128)(2,1)}) %all-gather.33.cloned.1.call-update) | async-done | bytes 8388624 | tf_op jit(solution)/shard_map/all_gather | solution.py:205
  571.6 7.7 multiply_convert_fusion.9
  580.1 7.5 fusion.334
  587.6 5.6 multiply_convert_fusion.8
  625.1 4.9 multiply_convert_fusion.1
  657.2 5.1 multiply_convert_fusion
  664.8 6.0 fusion.48
  676.1 8.5 all-gather.21.cloned.1.call-done
  684.6 4.8 multiply_reduce_fusion.4
  693.5 52.0 %all-gather.41.cloned.1.call-done = bf16[32,20,2048]{2,1,0:T(8,128)(2,1)} async-done(((bf16[1,20,2048]{2,1,0:T(8,128)(2,1)}), bf16[32,20,2048]{2,1,0:T(8,128)(2,1)}) %all-gather.41.cloned.1.call-update) | async-done | bytes 2621456 | tf_op jit(solution)/shard_map/all_gather | solution.py:194
  745.5 5.2 reshape.1527
  750.7 55.8 %all-gather.43.cloned.1.call-done = bf16[32,20,2048]{2,1,0:T(8,128)(2,1)} async-done(((bf16[1,20,2048]{2,1,0:T(8,128)(2,1)}), bf16[32,20,2048]{2,1,0:T(8,128)(2,1)}) %all-gather.43.cloned.1.call-update) | async-done | bytes 2621456 | tf_op jit(solution)/shard_map/all_gather | solution.py:195
  811.7 6.0 fusion.325
  817.7 4.7 fusion.324
  822.4 43.9 %all-gather.23.cloned.1.call-done = bf16[2048,640]{1,0:T(8,128)(2,1)} async-done(((bf16[64,640]{1,0:T(8,128)(2,1)}), bf16[2048,640]{1,0:T(8,128)(2,1)}) %all-gather.23.cloned.1.call-update) | async-done | bytes 2621456 | tf_op jit(solution)/shard_map/all_gather | solution.py:196
  866.3 12.6 multiply_convert_fusion.3
  878.9 6.0 fusion.332
  888.3 4.7 fusion.327
  892.9 4.6 fusion.326
  897.6 11.9 multiply_convert_fusion.2
  909.5 6.0 fusion.335
  922.0 4.6 fusion.55
  928.6 9.4 fusion.41
  949.5 8.1 fusion.175
  958.8 8.2 fusion.171
  968.2 8.2 fusion.179
  981.8 7.4 fusion.9
  990.1 5.3 fusion.49
  995.3 5.5 fusion.117
  1006.1 5.1 fusion.5
  1011.2 5.5 fusion.50
  1016.7 5.5 fusion.118
  1038.6 4.5 fusion.51
  1055.0 6.7 fusion.37
  1061.7 6.9 fusion.33
  1079.0 69.5 %reduce-scatter.27.cloned.1.call-done = bf16[1,816,512]{2,1,0:T(8,128)(2,1)} async-done(((bf16[8,816,512]{2,1,0:T(8,128)(2,1)}), bf16[1,816,512]{2,1,0:T(8,128)(2,1)}) %reduce-scatter.27.cloned.1.call-update) | async-done | bytes 835600 | tf_op jit(solution)/shard_map/reduce_scatter | solution.py:323
  1154.5 248.1 %fusion.311 = (f32[24,1024]{1,0:T(8,128)S(1)}, f32[24,256]{1,0:T(8,128)S(1)}, f32[24,256]{1,0:T(8,128)S(1)}, f32[24,2048]{1,0:T(8,128)S(1)}, f32[24,2048]{1,0:T(8,128)S(1)}) fusion(f32[640,1024]{1,0:T(8,128)} %fusion.51, f32[640,256]{1,0:T(8,128)} %get-tuple-element.195, f32[640,256]{1,0:T(8,128)} %get-tuple-element.194, f32[640,2048]{1,0:T(8,128)} %fusion.33, ...), kind=kCustom, calls=%all-reduce-scatter.5 | all-reduce-scatter fusion | flops 4325377 | bytes 14958592
  1403.9 7.2 collective-permute-start.9
  1411.1 4.2 collective-permute-start.17
  1425.0 5.6 collective-permute-start.8
  1435.0 4.6 collective-permute-start.16
  1469.9 5.8 collective-permute-start.21
  1477.1 8.9 collective-permute-start.19
  1489.8 42.4 %all-reduce.20 = (f32[640]{0:T(1024)S(1)}, f32[640]{0:T(1024)S(1)}, f32[1024]{0:T(1024)S(1)}, f32[1024]{0:T(1024)S(1)}) all-reduce(f32[640]{0:T(1024)S(1)} %add.364, f32[640]{0:T(1024)S(1)} %add.365, f32[1024]{0:T(1024)S(1)} %copy-done.190, f32[1024]{0:T(1024)S(1)} %add.367), channel_id=6, replica_groups=mesh['dp'=4,'noise'=8] {'dp','noise'}, use_global_device_ids=true, to_apply=%region_36.37.clone | all-reduce | flops 3328 | bytes 26624
  1538.1 4.8 collective-permute-start.27
  1546.4 5.6 collective-permute-start.25
  1565.6 26.2 %reduce-scatter.37.cloned.1.call-done = f32[32,256]{1,0:T(8,128)} async-done(((f32[1024,256]{1,0:T(8,128)}), f32[32,256]{1,0:T(8,128)}) %reduce-scatter.37.cloned.1.call-update) | async-done | bytes 32784 | tf_op jit(solution)/shard_map/reduce_scatter | solution.py:416
  1591.8 137.2 %reduce-scatter.35.cloned.1.call-done = f32[32,256]{1,0:T(8,128)} async-done(((f32[1024,256]{1,0:T(8,128)}), f32[32,256]{1,0:T(8,128)}) %reduce-scatter.35.cloned.1.call-update) | async-done | bytes 32784 | tf_op jit(solution)/shard_map/reduce_scatter | solution.py:415
  1729.1 141.8 %reduce-scatter.33.cloned.1.call-done = f32[32,1024]{1,0:T(8,128)} async-done(((f32[1024,1024]{1,0:T(8,128)}), f32[32,1024]{1,0:T(8,128)}) %reduce-scatter.33.cloned.1.call-update) | async-done | bytes 131088 | tf_op jit(solution)/shard_map/reduce_scatter | solution.py:414
  1870.9 142.7 %reduce-scatter.39.cloned.1.call-done = f32[32,1024]{1,0:T(8,128)} async-done(((f32[1024,1024]{1,0:T(8,128)}), f32[32,1024]{1,0:T(8,128)}) %reduce-scatter.39.cloned.1.call-update) | async-done | bytes 131088 | tf_op jit(solution)/shard_map/reduce_scatter | solution.py:417
  2013.5 186.6 %reduce-scatter.43.cloned.1.call-done = f32[32,4096]{1,0:T(8,128)} async-done(((f32[1024,4096]{1,0:T(8,128)}), f32[32,4096]{1,0:T(8,128)}) %reduce-scatter.43.cloned.1.call-update) | async-done | bytes 524304 | tf_op jit(solution)/shard_map/reduce_scatter | solution.py:420
  2200.2 187.4 %reduce-scatter.41.cloned.1.call-done = f32[32,4096]{1,0:T(8,128)} async-done(((f32[1024,4096]{1,0:T(8,128)}), f32[32,4096]{1,0:T(8,128)}) %reduce-scatter.41.cloned.1.call-update) | async-done | bytes 524304 | tf_op jit(solution)/shard_map/reduce_scatter | solution.py:419
  2387.6 187.2 %reduce-scatter.45.cloned.1.call-done = f32[128,1024]{1,0:T(8,128)} async-done(((f32[4096,1024]{1,0:T(8,128)}), f32[128,1024]{1,0:T(8,128)}) %reduce-scatter.45.cloned.1.call-update) | async-done | bytes 524304 | tf_op jit(solution)/shard_map/reduce_scatter | solution.py:421
  (858 shorter events, 276.8 us)
Async XLA Ops:
  7.2 127.5 %copy-start.18 = (bf16[2,1,816,640]{3,2,1,0:T(8,128)(2,1)S(1)}, bf16[2,1,816,640]{3,2,1,0:T(8,128)(2,1)}, u32[]{:S(2)}) copy-start(bf16[2,1,816,640]{3,2,1,0:T(8,128)(2,1)} %param.27) | copy-start | bytes 6266884
  7.2 278.5 %all-gather.25.cloned.1.call-start = ((), (), s32[]{:S(2)}) async-start(), calls=%async_computation.14 | async-start | bytes 2162688 | tf_op jit(solution)/shard_map/all_gather | solution.py:198
  7.9 280.7 %all-gather.35.cloned.1.call-start = ((), (), s32[]{:S(2)}) async-start(), calls=%async_computation.30 | async-start | bytes 7520256 | tf_op jit(solution)/shard_map/all_gather | solution.py:241
  139.5 152.2 %all-gather.27.cloned.1.call-start = ((), (), s32[]{:S(2)}) async-start(), calls=%async_computation.15 | async-start | bytes 2162688 | tf_op jit(solution)/shard_map/all_gather | solution.py:201
  140.2 194.8 %all-gather.37.cloned.1.call-start = ((), (), s32[]{:S(2)}) async-start(), calls=%async_computation.31 | async-start | bytes 7520256 | tf_op jit(solution)/shard_map/all_gather | solution.py:241
  142.1 271.7 %all-gather.31.cloned.1.call-start = ((), (), s32[]{:S(2)}) async-start(), calls=%async_computation.17 | async-start | bytes 8650752 | tf_op jit(solution)/shard_map/all_gather | solution.py:204
  142.7 350.0 %all-gather.29.cloned.1.call-start = ((), (), s32[]{:S(2)}) async-start(), calls=%async_computation.16 | async-start | bytes 8650752 | tf_op jit(solution)/shard_map/all_gather | solution.py:203
  143.3 428.3 %all-gather.33.cloned.1.call-start = ((), (), s32[]{:S(2)}) async-start(), calls=%async_computation.18 | async-start | bytes 8650752 | tf_op jit(solution)/shard_map/all_gather | solution.py:205
  144.1 489.8 %all-gather.39.cloned.1.call-start = ((), (), s32[]{:S(2)}) async-start(), calls=%async_computation.32 | async-start | bytes 1622016 | tf_op jit(solution)/shard_map/all_gather | solution.py:189
  144.8 539.8 %all-gather.21.cloned.1.call-start = ((), (), s32[]{:S(2)}) async-start(), calls=%async_computation.12 | async-start | bytes 1351680 | tf_op jit(solution)/shard_map/all_gather | solution.py:192
  145.5 600.0 %all-gather.41.cloned.1.call-start = ((), (), s32[]{:S(2)}) async-start(), calls=%async_computation.33 | async-start | bytes 3244032 | tf_op jit(solution)/shard_map/all_gather | solution.py:194
  146.1 660.4 %all-gather.43.cloned.1.call-start = ((), (), s32[]{:S(2)}) async-start(), calls=%async_computation.34 | async-start | bytes 3244032 | tf_op jit(solution)/shard_map/all_gather | solution.py:195
  146.9 719.4 %all-gather.23.cloned.1.call-start = ((), (), s32[]{:S(2)}) async-start(), calls=%async_computation.13 | async-start | bytes 2703360 | tf_op jit(solution)/shard_map/all_gather | solution.py:196
  147.4 927.7 %reduce-scatter.47.cloned.1.call-start = ((), (), s32[]{:S(2)}) async-start(), calls=%async_computation.35 | async-start | bytes 1081344
  201.8 136.3 %copy-start.58 = (bf16[1,1,50,1024]{3,2,1,0:T(8,128)(2,1)}, bf16[1,1,50,1024]{3,2,1,0:T(8,128)(2,1)S(1)}, u32[]{:S(2)}) copy-start(bf16[1,1,50,1024]{3,2,1,0:T(8,128)(2,1)S(1)} %get-tuple-element.173) | copy-start | bytes 307204
  282.2 337.4 %copy-start.170 = (f32[1024]{0:T(1024)}, f32[1024]{0:T(1024)S(1)}, u32[]{:S(2)}) copy-start(f32[1024]{0:T(1024)S(1)} %get-tuple-element.210) | copy-start | bytes 12292
  282.2 337.4 %copy-start.172 = (f32[1024]{0:T(1024)}, f32[1024]{0:T(1024)S(1)}, u32[]{:S(2)}) copy-start(f32[1024]{0:T(1024)S(1)} %get-tuple-element.209) | copy-start | bytes 12292
  285.6 286.0 %copy-start.108 = (bf16[50,1024]{1,0:T(8,128)(2,1)}, bf16[50,1024]{1,0:T(8,128)(2,1)S(1)}, u32[]{:S(2)}) copy-start(bf16[50,1024]{1,0:T(8,128)(2,1)S(1)} %bitcast_convert_fusion.1) | copy-start | bytes 307204
  339.2 153.5 %copy-start.42 = (bf16[50,1024]{1,0:T(8,128)(2,1)}, bf16[50,1024]{1,0:T(8,128)(2,1)S(1)}, u32[]{:S(2)}) copy-start(bf16[50,1024]{1,0:T(8,128)(2,1)S(1)} %get-tuple-element.205) | copy-start | bytes 307204
  339.2 162.0 %copy-start.44 = (bf16[50,1024]{1,0:T(8,128)(2,1)}, bf16[50,1024]{1,0:T(8,128)(2,1)S(1)}, u32[]{:S(2)}) copy-start(bf16[50,1024]{1,0:T(8,128)(2,1)S(1)} %get-tuple-element.206) | copy-start | bytes 307204
  625.0 451.5 %reduce-scatter.25.cloned.1.call-start = ((), (), s32[]{:S(2)}) async-start(), calls=%async_computation.19 | async-start | bytes 7520256 | tf_op jit(solution)/shard_map/reduce_scatter | solution.py:323
  630.0 518.5 %reduce-scatter.27.cloned.1.call-start = ((), (), s32[]{:S(2)}) async-start(), calls=%async_computation.20 | async-start | bytes 7520256 | tf_op jit(solution)/shard_map/reduce_scatter | solution.py:323
  631.8 286.9 %copy-start.147 = (f32[640]{0:T(1024)}, f32[640]{0:T(1024)S(1)}, u32[]{:S(2)}) copy-start(f32[640]{0:T(1024)S(1)} %convert_element_type.535) | copy-start | bytes 7684
  662.3 903.3 %reduce-scatter.29.cloned.1.call-start = ((), (), s32[]{:S(2)}) async-start(), calls=%async_computation.21 | async-start | bytes 2703360 | tf_op jit(solution)/shard_map/reduce_scatter | solution.py:408
  689.4 229.4 %copy-start.162 = (f32[816]{0:T(1024)}, f32[816]{0:T(1024)S(1)}, u32[]{:S(2)}) copy-start(f32[816]{0:T(1024)S(1)} %add_rsqrt_fusion) | copy-start | bytes 9796
  691.0 227.7 %copy-start.158 = (f32[816]{0:T(1024)}, f32[816]{0:T(1024)S(1)}, u32[]{:S(2)}) copy-start(f32[816]{0:T(1024)S(1)} %add_rsqrt_fusion.2) | copy-start | bytes 9796
  926.6 639.1 %reduce-scatter.31.cloned.1.call-start = ((), (), s32[]{:S(2)}) async-start(), calls=%async_computation.22 | async-start | bytes 5406720 | tf_op jit(solution)/shard_map/reduce_scatter | solution.py:412
  938.1 653.8 %reduce-scatter.37.cloned.1.call-start = ((), (), s32[]{:S(2)}) async-start(), calls=%async_computation.25 | async-start | bytes 1081344 | tf_op jit(solution)/shard_map/reduce_scatter | solution.py:416
  941.0 788.1 %reduce-scatter.35.cloned.1.call-start = ((), (), s32[]{:S(2)}) async-start(), calls=%async_computation.24 | async-start | bytes 1081344 | tf_op jit(solution)/shard_map/reduce_scatter | solution.py:415
  941.7 929.2 %reduce-scatter.33.cloned.1.call-start = ((), (), s32[]{:S(2)}) async-start(), calls=%async_computation.23 | async-start | bytes 4325376 | tf_op jit(solution)/shard_map/reduce_scatter | solution.py:414
  944.5 1069.0 %reduce-scatter.39.cloned.1.call-start = ((), (), s32[]{:S(2)}) async-start(), calls=%async_computation.26 | async-start | bytes 4325376 | tf_op jit(solution)/shard_map/reduce_scatter | solution.py:417
  948.3 1251.9 %reduce-scatter.43.cloned.1.call-start = ((), (), s32[]{:S(2)}) async-start(), calls=%async_computation.28 | async-start | bytes 17301504 | tf_op jit(solution)/shard_map/reduce_scatter | solution.py:420
  957.7 1429.9 %reduce-scatter.41.cloned.1.call-start = ((), (), s32[]{:S(2)}) async-start(), calls=%async_computation.27 | async-start | bytes 17301504 | tf_op jit(solution)/shard_map/reduce_scatter | solution.py:419
  967.0 1607.7 %reduce-scatter.45.cloned.1.call-start = ((), (), s32[]{:S(2)}) async-start(), calls=%async_computation.29 | async-start | bytes 17301504 | tf_op jit(solution)/shard_map/reduce_scatter | solution.py:421
  1402.6 32.4 %collective-permute-start.10 = (f32[24,256]{1,0:T(8,128)S(1)}, f32[24,256]{1,0:T(8,128)S(1)}, u32[]{:S(2)}, u32[]{:S(2)}) collective-permute-start(f32[24,256]{1,0:T(8,128)S(1)} %get-tuple-element.162), channel_id=1, source_target_pairs={{0,5},{1,6},{2,7},{3,8},{4,9},{5,10},{6,11},{7,12},{8,13},{9,14},{... | collective-permute-start | bytes 73736
  1403.9 35.7 %collective-permute-start.9 = (f32[24,256]{1,0:T(8,128)S(1)}, f32[24,256]{1,0:T(8,128)S(1)}, u32[]{:S(2)}, u32[]{:S(2)}) collective-permute-start(f32[24,256]{1,0:T(8,128)S(1)} %get-tuple-element.162), channel_id=1, source_target_pairs={{0,4},{1,5},{2,6},{3,7},{4,8},{5,9},{6,10},{7,11},{8,12},{9,13},{1... | collective-permute-start | bytes 73736
  1411.1 13.9 collective-permute-start.17
  1415.3 15.3 collective-permute-start.11
  1417.3 15.6 collective-permute-start.5
  1425.0 17.5 collective-permute-start.8
  1430.6 14.7 collective-permute-start.7
  1432.9 15.2 collective-permute-start.6
  1435.0 15.2 collective-permute-start.16
  1439.7 13.5 collective-permute-start.15
  1442.4 12.7 collective-permute-start.14
  1445.3 11.1 collective-permute-start.13
  1448.1 10.9 collective-permute-start.12
  1450.2 11.3 collective-permute-start.29
  1453.2 10.0 collective-permute-start.23
  1455.1 11.8 collective-permute-start.4
  1456.5 13.5 collective-permute-start.3
  1459.0 16.7 collective-permute-start.2
  1461.5 15.6 collective-permute-start.1
  1463.2 22.8 collective-permute-start
  1466.9 69.9 %collective-permute-start.22 = (f32[24,2048]{1,0:T(8,128)S(1)}, f32[24,2048]{1,0:T(8,128)S(1)}, u32[]{:S(2)}, u32[]{:S(2)}) collective-permute-start(f32[24,2048]{1,0:T(8,128)S(1)} %get-tuple-element.164), channel_id=1, source_target_pairs={{0,5},{1,6},{2,7},{3,8},{4,9},{5,10},{6,11},{7,12},{8,13},{9,14},{... | collective-permute-start | bytes 589832
  1469.9 68.2 %collective-permute-start.21 = (f32[24,2048]{1,0:T(8,128)S(1)}, f32[24,2048]{1,0:T(8,128)S(1)}, u32[]{:S(2)}, u32[]{:S(2)}) collective-permute-start(f32[24,2048]{1,0:T(8,128)S(1)} %get-tuple-element.164), channel_id=1, source_target_pairs={{0,4},{1,5},{2,6},{3,7},{4,8},{5,9},{6,10},{7,11},{8,12},{9,13},{1... | collective-permute-start | bytes 589832
  1475.8 67.2 %collective-permute-start.20 = (f32[24,2048]{1,0:T(8,128)S(1)}, f32[24,2048]{1,0:T(8,128)S(1)}, u32[]{:S(2)}, u32[]{:S(2)}) collective-permute-start(f32[24,2048]{1,0:T(8,128)S(1)} %get-tuple-element.164), channel_id=1, source_target_pairs={{0,3},{1,4},{2,5},{3,6},{4,7},{5,8},{6,9},{7,10},{8,11},{9,12},{10... | collective-permute-start | bytes 589832
  1477.1 69.3 %collective-permute-start.19 = (f32[24,2048]{1,0:T(8,128)S(1)}, f32[24,2048]{1,0:T(8,128)S(1)}, u32[]{:S(2)}, u32[]{:S(2)}) collective-permute-start(f32[24,2048]{1,0:T(8,128)S(1)} %get-tuple-element.164), channel_id=1, source_target_pairs={{0,2},{1,3},{2,4},{3,5},{4,6},{5,7},{6,8},{7,9},{8,10},{9,11},{10,... | collective-permute-start | bytes 589832
  1486.0 66.0 %collective-permute-start.18 = (f32[24,2048]{1,0:T(8,128)S(1)}, f32[24,2048]{1,0:T(8,128)S(1)}, u32[]{:S(2)}, u32[]{:S(2)}) collective-permute-start(f32[24,2048]{1,0:T(8,128)S(1)} %get-tuple-element.164), channel_id=1, source_target_pairs={{0,1},{1,2},{2,3},{3,4},{4,5},{5,6},{6,7},{7,8},{8,9},{9,10},{10,1... | collective-permute-start | bytes 589832
  1536.8 23.0 collective-permute-start.28
  1538.1 21.7 collective-permute-start.27
  1543.0 16.8 collective-permute-start.26
  1546.4 13.4 collective-permute-start.25
  1552.0 8.5 collective-permute-start.24
  (252 other events, 2806.0 us)
Sparse Core Ops, SparseCore 0:
  11.0 59.4 all-gather.24
  139.6 67.3 all-gather.34
  210.0 56.1 all-gather.26
  267.7 67.3 all-gather.36
  337.8 75.9 all-gather.30
  416.7 75.9 all-gather.28
  495.7 75.8 all-gather.32
  574.6 53.7 all-gather.38
  631.2 53.3 all-gather.20
  687.4 58.0 all-gather.40
  748.6 57.9 all-gather.42
  809.3 56.9 all-gather.22
  868.5 133.6 reduce-scatter.46
  1004.5 69.8 reduce-scatter.24
  1076.6 71.8 reduce-scatter.26
  1151.3 147.1 reduce-scatter.28
  1301.3 152.9 reduce-scatter.30
  1457.1 134.7 reduce-scatter.36
  1594.7 134.3 reduce-scatter.34
  1731.9 138.9 reduce-scatter.32
  1873.8 139.6 reduce-scatter.38
  2016.5 183.6 reduce-scatter.42
  2203.2 184.3 reduce-scatter.40
  2390.4 184.3 reduce-scatter.44
where the time goes:
time: 2590 us; the launch traced here: 2580 us
  waiting for transfers between devices  1500 us (58%)
  blocking collectives  534 us (21%)
  matrix products  277 us (11%)
  starting transfers between devices  94.8 us (4%)
  local copies, waits for them, and re-layouts  83 us (3%)
  other arithmetic  67 us (3%)
    unnamed x3, blocking collectives  333 us
    reduce_scatter x1, waiting for transfers between devices, per_device(): lax.psum_scatter(grads[15], ('dp', 'noise'), scatter_dimension=0, tiled=T...  187 us
    reduce_scatter x1, waiting for transfers between devices, per_device(): lax.psum_scatter(grads[17], ('dp', 'noise'), scatter_dimension=0, tiled=T...  187 us
    reduce_scatter x1, waiting for transfers between devices, per_device(): lax.psum_scatter(grads[16], ('dp', 'noise'), scatter_dimension=0, tiled=T...  187 us
    reduce_scatter x1, waiting for transfers between devices, per_device(): lax.psum_scatter(grads[13], ('dp', 'noise'), scatter_dimension=0, tiled=T...  143 us
    reduce_scatter x1, waiting for transfers between devices, per_device(): lax.psum_scatter(grads[10], ('dp', 'noise'), scatter_dimension=0, tiled=T...  142 us
    reduce_scatter x1, waiting for transfers between devices, per_device(): lax.psum_scatter(grads[11], ('dp', 'noise'), scatter_dimension=0, tiled=T...  137 us
    unnamed x31, starting transfers between devices  93.9 us
  transfers between devices with their start and end apart: 54, of which 16 were waited for; matrix products, arithmetic and copies ran while one was open for 25% of the time, Pallas kernels for 0%

commit v1 on v0

v1 whole, which is shorter than its diff:
```python
import jax
import jax.numpy as jnp
from jax import lax
from jax.sharding import PartitionSpec as P

EPS = 1e-06
HIGH = lax.Precision.HIGHEST


def normed(rows):
    factor = lax.rsqrt(jnp.mean(rows * rows, axis=-1, keepdims=True) + EPS)
    return (rows * factor, factor)


def norm_back(grad_hidden, normal, factor, gain_mod):
    grad_normal = grad_hidden * gain_mod
    centred = jnp.mean(grad_normal * normal, axis=-1, keepdims=True)
    return factor * (grad_normal - normal * centred)


def flatten(array):
    return array.reshape(-1, array.shape[-1])


def weight_grad(inputs, grads):
    return jnp.einsum(
        "ra,rb->ab", flatten(inputs), flatten(grads), preferred_element_type=jnp.float32
    )


def back_through(grads, weight):
    return jnp.einsum("...b,ab->...a", grads, weight, preferred_element_type=jnp.float32)


def scores_of(queries, keys, valid):
    batch, rows, width = queries.shape
    depth = keys.shape[-1]
    split = queries.reshape(batch, rows, width // depth, depth)
    scores = jnp.einsum(
        "bnhd,bmd->bhnm", split, keys, preferred_element_type=jnp.float32
    ) * depth ** (-0.5)
    return (split, jnp.where(valid[:, None, None, :], scores, -1e30))


def attend(queries, keys, values, valid):
    split, scores = scores_of(queries, keys, valid)
    top = jnp.max(scores, axis=-1, keepdims=True)
    total = top + jnp.log(jnp.sum(jnp.exp(scores - top), axis=-1, keepdims=True))
    probs = jnp.exp(scores - total).astype(jnp.bfloat16)
    mixed = jnp.einsum("bhnm,bmd->bnhd", probs, values, preferred_element_type=jnp.float32)
    return (mixed.reshape(queries.shape).astype(jnp.bfloat16), total)


def attend_back(queries, keys, values, valid, total, grad_mixed):
    split, scores = scores_of(queries, keys, valid)
    depth = keys.shape[-1]
    probs = jnp.exp(scores - total)
    grad_split = grad_mixed.reshape(split.shape)
    grad_values = jnp.einsum(
        "bhnm,bnhd->bmd", probs.astype(jnp.bfloat16), grad_split, preferred_element_type=jnp.float32
    )
    grad_probs = jnp.einsum(
        "bnhd,bmd->bhnm", grad_split, values, preferred_element_type=jnp.float32
    )
    centred = jnp.sum(probs * grad_probs, axis=-1, keepdims=True)
    grad_scores = (probs * (grad_probs - centred) * depth ** (-0.5)).astype(jnp.bfloat16)
    grad_queries = jnp.einsum(
        "bhnm,bmd->bnhd", grad_scores, keys, preferred_element_type=jnp.float32
    )
    grad_keys = jnp.einsum("bhnm,bnhd->bmd", grad_scores, split, preferred_element_type=jnp.float32)
    return (grad_queries.reshape(queries.shape).astype(jnp.bfloat16), grad_keys, grad_values)


ALL = ("dp", "noise")


def gelu_parts(gate):
    c = 0.7978845608028654
    inner = c * (gate + 0.044715 * gate * gate * gate)
    t = jnp.tanh(inner)
    half = 0.5 * (1.0 + t)
    slope = half + 0.5 * gate * (1.0 - t * t) * c * (1.0 + 3 * 0.044715 * gate * gate)
    return gate * half, slope


def swap_bit(x, bit, total):
    return lax.ppermute(x, ALL, [(i, i ^ (1 << bit)) for i in range(total)])


def scatter_sum(x, order, total):
    me = lax.axis_index("dp") * lax.axis_size("noise") + lax.axis_index("noise")
    live = list(range(total.bit_length() - 2, -1, -1))
    rest = x.shape[1:]
    for bit in order:
        at = live.index(bit)
        high, low = 1 << at, 1 << (len(live) - at - 1)
        x = x.reshape((high, 2, low) + rest)
        mine = (me >> bit) & 1
        keep = lax.dynamic_index_in_dim(x, mine, 1, keepdims=False)
        send = lax.dynamic_index_in_dim(x, 1 - mine, 1, keepdims=False)
        x = keep + swap_bit(send, bit, total)
        live.remove(bit)
    return x.reshape(rest)


def orders(total):
    bits = list(range(1, total.bit_length() - 1))
    high = bits[::-1]
    third = len(bits) // 2
    return ([0] + high, [0] + high[1:] + high[:1], [0] + bits)


def own_attend(q, k, v, keys, values, valid):
    depth = keys.shape[-1]
    scale = depth ** (-0.5)
    far = jnp.einsum("nmqhd,mkd->mhnqk", q, keys, preferred_element_type=jnp.float32) * scale
    far = jnp.where(valid[:, None, None, None, :], far, -1e30)
    near = jnp.einsum("nmqhd,nmkd->mhnqk", q, k, preferred_element_type=jnp.float32) * scale
    top = jnp.maximum(jnp.max(far, -1, keepdims=True), jnp.max(near, -1, keepdims=True))
    efar, enear = jnp.exp(far - top), jnp.exp(near - top)
    total = jnp.sum(efar, -1, keepdims=True) + jnp.sum(enear, -1, keepdims=True)
    pfar, pnear = efar / total, enear / total
    mixed = jnp.einsum("mhnqk,mkd->nmqhd", pfar.astype(jnp.bfloat16), values, preferred_element_type=jnp.float32)
    mixed = mixed + jnp.einsum("mhnqk,nmkd->nmqhd", pnear.astype(jnp.bfloat16), v, preferred_element_type=jnp.float32)
    return mixed, pfar, pnear


def own_attend_back(q, k, v, keys, values, pfar, pnear, dout):
    depth = keys.shape[-1]
    scale = depth ** (-0.5)
    dvalues = jnp.einsum("mhnqk,nmqhd->mkd", pfar.astype(jnp.bfloat16), dout, preferred_element_type=jnp.float32)
    dv = jnp.einsum("mhnqk,nmqhd->nmkd", pnear.astype(jnp.bfloat16), dout, preferred_element_type=jnp.float32)
    dfar = jnp.einsum("nmqhd,mkd->mhnqk", dout, values, preferred_element_type=jnp.float32)
    dnear = jnp.einsum("nmqhd,nmkd->mhnqk", dout, v, preferred_element_type=jnp.float32)
    centre = jnp.sum(pfar * dfar, -1, keepdims=True) + jnp.sum(pnear * dnear, -1, keepdims=True)
    sfar = (pfar * (dfar - centre) * scale).astype(jnp.bfloat16)
    snear = (pnear * (dnear - centre) * scale).astype(jnp.bfloat16)
    dq = jnp.einsum("mhnqk,mkd->nmqhd", sfar, keys, preferred_element_type=jnp.float32)
    dq = dq + jnp.einsum("mhnqk,nmkd->nmqhd", snear, k, preferred_element_type=jnp.float32)
    dkeys = jnp.einsum("mhnqk,nmqhd->mkd", sfar, q, preferred_element_type=jnp.float32)
    dk = jnp.einsum("mhnqk,nmqhd->nmkd", snear, q, preferred_element_type=jnp.float32)
    return dq, dk, dv, dkeys, dvalues


def dot(a, b):
    return jnp.dot(a, b, preferred_element_type=jnp.float32)


def dot_t(a, b):
    return lax.dot_general(a, b, (((1,), (1,)), ((), ())), preferred_element_type=jnp.float32)


def dot_w(a, b):
    return lax.dot_general(a, b, (((0,), (0,)), ((), ())), preferred_element_type=jnp.float32)


def per_device(
    prefix_rows,
    action_rows,
    segment_item,
    segment_time,
    item_weight,
    prefix_len,
    vlm_prenorm,
    vlm_query,
    vlm_key,
    vlm_value,
    vlm_mixer,
    vlm_midnorm,
    vlm_gate,
    vlm_expand,
    vlm_down,
    act_prenorm,
    act_query,
    act_key,
    act_value,
    act_mixer,
    act_midnorm,
    act_gate,
    act_expand,
    act_down,
    time_scales,
    cot_prefix,
    cot_action,
):
    bf = jnp.bfloat16
    micro, items, prefix, width = prefix_rows.shape
    seg_len, wide = action_rows.shape[2:]
    groups, n = lax.axis_size("dp"), lax.axis_size("noise")
    total = groups * n
    depth = vlm_key.shape[1]
    hq = vlm_query.shape[1]
    heads = hq // depth
    ff = vlm_gate.shape[1]
    ffa = act_gate.shape[1]
    levels = time_scales.shape[1]
    rows_p, rows_a = vlm_query.shape[0], act_query.shape[0]
    here = lax.axis_index("noise")
    live = micro * seg_len
    pad = -live % 16 if -live % 16 >= micro else -live % 16 + 16
    block = live + pad

    def padded(x):
        return jnp.pad(x.reshape(live, x.shape[-1]), ((0, pad), (0, 0)))

    extra = jnp.zeros((rows_p, 128), bf)
    extra = extra.at[:, 0].set(vlm_prenorm).at[:, 1].set(vlm_midnorm)
    pre_a = lax.all_gather(
        jnp.concatenate([vlm_query, vlm_key, vlm_value, extra], axis=1), ALL, axis=0, tiled=True
    )
    extra = jnp.concatenate(
        [
            act_prenorm[:, None],
            act_midnorm[:, None],
            time_scales.reshape(rows_a, -1),
            jnp.zeros((rows_a, 128 - 2 - time_scales.size // rows_a), bf),
        ],
        axis=1,
    )
    act_a = lax.all_gather(
        jnp.concatenate([act_query, act_key, act_value, act_mixer, extra], axis=1),
        ALL,
        axis=0,
        tiled=True,
    )
    pre_b = lax.all_gather(jnp.concatenate([vlm_gate, vlm_expand], axis=1), ALL, axis=0, tiled=True)
    pre_c = lax.all_gather(jnp.concatenate([vlm_mixer, vlm_down], axis=0), ALL, axis=0)
    unit = act_down.shape[0]
    cols = jnp.stack([act_gate, act_expand]).reshape(2, rows_a, groups, n, unit)
    cols = lax.all_to_all(
        cols.transpose(3, 0, 1, 2, 4).reshape(n, 2, rows_a, groups * unit), "noise", 0, 0, tiled=True
    )
    hidden_w = lax.all_gather(
        jnp.concatenate(
            [
                cols.transpose(0, 2, 1, 3).reshape(n * rows_a, 2 * groups * unit),
                act_down.reshape(-1, 2 * groups * unit),
            ],
            axis=0,
        ),
        "dp",
        axis=0,
    )
    part = groups * unit
    gu_w = hidden_w[:, : n * rows_a].reshape(groups * n * rows_a, 2 * part)
    down_w = hidden_w[:, n * rows_a :].reshape(part, wide)

    pre_qkv = pre_a[:, : hq + 2 * depth]
    pre_gain = pre_a[:, hq + 2 * depth].astype(jnp.float32)
    pre_midgain = pre_a[:, hq + 2 * depth + 1].astype(jnp.float32)
    pre_mixer = pre_c[:, : vlm_mixer.shape[0]].reshape(hq, width)
    pre_down = pre_c[:, vlm_mixer.shape[0] :].reshape(ff, width)
    suf_qkv = act_a[:, : hq + 2 * depth]
    suf_mixer = act_a[:, hq + 2 * depth : hq + 2 * depth + wide]
    small = act_a[:, hq + 2 * depth + wide :].astype(jnp.float32)
    suf_gain, suf_midgain = small[:, 0], small[:, 1]
    table = small[:, 2 : 2 + time_scales.size // rows_a].reshape(2 * wide, levels)

    item = segment_item[:, 0]
    time_hot = (segment_time[:, 0][:, None] == jnp.arange(levels)[None, :]).astype(jnp.float32)
    mods = jnp.einsum("mt,jt->mj", time_hot, table, precision=HIGH)
    mod1, mod2 = mods[:, None, :wide], mods[:, None, wide:]
    hot = item[:, None] == jnp.arange(prefix_len.shape[1])[None, :]
    weight = (jnp.sum(jnp.where(hot, item_weight, 0), axis=1) + 1).astype(jnp.float32) / 8.0
    grad_action = cot_action[:, 0].astype(jnp.float32) * weight[:, None, None]
    dy_own = padded(grad_action.astype(bf))
    dy_all = lax.all_gather(dy_own, "noise", axis=0, tiled=True)
    action_in = action_rows[:, 0].astype(jnp.float32)
    an1, as1 = normed(action_in)
    ah1 = padded((an1 * suf_gain * mod1).astype(bf))
    aqkv = dot(ah1, suf_qkv).astype(bf)
    tags = jnp.zeros((block, hq + 2 * depth), bf).at[live : live + micro, 0].set(item.astype(bf))
    gathered = lax.all_gather(aqkv + tags, "noise", axis=0)
    owned = gathered[:, live : live + micro, 0] == here.astype(bf)
    gathered = gathered[:, :live].reshape(n, micro, seg_len, hq + 2 * depth)
    qs = gathered[..., :hq].reshape(n, micro, seg_len, heads, depth)
    ks, vs = gathered[..., hq : hq + depth], gathered[..., hq + depth :]

    prefix_in = prefix_rows[:, 0].astype(jnp.float32)
    n1, s1 = normed(prefix_in)
    h1 = (n1 * pre_gain).astype(bf)
    qkv = jnp.einsum("mra,ab->mrb", h1, pre_qkv, preferred_element_type=jnp.float32).astype(bf)
    queries, keys, values = qkv[..., :hq], qkv[..., hq : hq + depth], qkv[..., hq + depth :]
    own_len = lax.dynamic_slice_in_dim(prefix_len, here, 1, axis=1)
    valid = jnp.arange(prefix, dtype=jnp.int32)[None, :] < own_len

    mixed, pfar, pnear = own_attend(qs, ks, vs, keys, values, valid)
    mixed = jnp.where(owned[:, :, None, None, None], mixed, 0.0).astype(bf).reshape(n, live, hq)
    mixed = jnp.pad(mixed, ((0, 0), (0, pad), (0, 0)))
    oa = lax.psum_scatter(mixed, "noise", scatter_dimension=0)
    a1 = action_in + dot(oa, suf_mixer)[:live].reshape(action_in.shape)
    an2, as2 = normed(a1)
    ah2 = padded((an2 * suf_midgain * mod2).astype(bf))
    h_all = lax.all_gather(ah2, "noise", axis=0, tiled=True)
    gu = dot(h_all, gu_w)
    gate_a, up_a = gu[:, :part], gu[:, part:]
    act_g, slope_g = gelu_parts(gate_a)
    mid_a = (act_g * up_a).astype(bf)
    out_part = dot(mid_a, down_w)
    dmid_a = dot_t(dy_all, down_w)
    dgu = jnp.concatenate(
        [(dmid_a * up_a * slope_g).astype(bf), (dmid_a * act_g).astype(bf)], axis=1
    )
    dh_part = dot_t(dgu, gu_w)
    both = jnp.concatenate([out_part, dh_part], axis=1).astype(bf).reshape(n, block, 2 * wide)
    both = lax.psum_scatter(both, "noise", scatter_dimension=0)[:live].astype(jnp.float32)
    action_out = (a1 + both[:, :wide].reshape(a1.shape)).astype(bf)
    grad_late = both[:, wide:].reshape(a1.shape)
    dgu_w = dot_w(h_all, dgu).astype(bf)
    ddown_w = dot_w(mid_a, dy_all).astype(bf)
    dff = lax.psum_scatter(
        jnp.concatenate(
            [
                dgu_w.reshape(groups, n * rows_a, 2 * part),
                ddown_w.reshape(groups, -1, 2 * part),
            ],
            axis=1,
        ),
        "dp",
        scatter_dimension=0,
    )
    ddown_a = dff[n * rows_a :].reshape(unit, wide)
    dgu_a = lax.all_to_all(
        dff[: n * rows_a].reshape(n, rows_a, 2 * part), "noise", 0, 0, tiled=True
    )
    dgu_a = dgu_a.reshape(n, rows_a, 2, groups, unit).transpose(2, 1, 3, 0, 4)
    dgu_a = dgu_a.reshape(2, rows_a, ffa)

    late_back = grad_late * an2
    suf_dmid = jnp.sum(late_back * mod2, axis=(0, 1))
    dmod2 = jnp.sum(late_back * suf_midgain, axis=1)
    da1 = grad_action + norm_back(grad_late, an2, as2, suf_midgain * mod2)
    dmixed_a = padded(da1.astype(bf))
    dattn_a = dot_t(dmixed_a, suf_mixer).astype(bf)
    dattn_all = lax.all_gather(dattn_a, "noise", axis=0)
    dattn_all = dattn_all[:, :live].reshape(n, micro, seg_len, hq)
    dattn_all = jnp.where(owned[:, :, None, None], dattn_all, 0).reshape(qs.shape)
    dqs, dks, dvs, far_dk, far_dv = own_attend_back(
        qs, ks, vs, keys, values, pfar, pnear, dattn_all
    )
    back = jnp.concatenate([dqs.reshape(n, live, hq), dks.reshape(n, live, depth), dvs.reshape(n, live, depth)], axis=-1)
    back = jnp.pad(back.astype(bf), ((0, 0), (0, pad), (0, 0)))
    daqkv = lax.psum_scatter(back, "noise", scatter_dimension=0)
    dah1 = dot_t(daqkv, suf_qkv)[:live].reshape(action_in.shape)
    first_back = dah1 * an1
    suf_dgain = jnp.sum(first_back * mod1, axis=(0, 1))
    dmod1 = jnp.sum(first_back * suf_gain, axis=1)
    action_grad = da1 + norm_back(dah1, an1, as1, suf_gain * mod1)
    dtable = jnp.einsum(
        "mj,mt->jt", jnp.concatenate([dmod1, dmod2], axis=-1), time_hot, precision=HIGH
    )
    dact_a = jnp.concatenate([dot_w(ah1, daqkv), dot_w(oa, dmixed_a)], axis=1).astype(bf)

    outs = [attend(queries[m : m + 1], keys[m : m + 1], values[m : m + 1], valid[m : m + 1]) for m in range(micro)]
    o = jnp.concatenate([x[0] for x in outs])
    x1 = prefix_in + jnp.einsum("mra,ab->mrb", o, pre_mixer, preferred_element_type=jnp.float32)
    n2, s2 = normed(x1)
    h2 = flatten((n2 * pre_midgain).astype(bf))
    gate = dot(h2, pre_b[:, :ff])
    up = dot(h2, pre_b[:, ff:])
    act, slope = gelu_parts(gate)
    mid = (act * up).astype(bf)
    prefix_out = (x1 + dot(mid, pre_down).reshape(x1.shape)).astype(bf)
    dy = flatten(cot_prefix[:, 0])
    dmid = dot_t(dy, pre_down)
    dgate = (dmid * up * slope).astype(bf)
    dup = (dmid * act).astype(bf)
    dh2 = (dot_t(dgate, pre_b[:, :ff]) + dot_t(dup, pre_b[:, ff:])).reshape(x1.shape)
    one, two, three = orders(total)
    ddown = scatter_sum(dot_w(mid, dy).astype(bf).reshape(total, -1, width), one, total)
    dgate_w = scatter_sum(dot_w(h2, dgate).astype(bf).reshape(total, rows_p, ff), two, total)
    dup_w = scatter_sum(dot_w(h2, dup).astype(bf).reshape(total, rows_p, ff), three, total)
    pre_dmid = jnp.sum(dh2 * n2, axis=(0, 1))
    dx1 = cot_prefix[:, 0].astype(jnp.float32) + norm_back(dh2, n2, s2, pre_midgain)
    dmixed = dx1.astype(bf)
    dattn = jnp.einsum("mrb,ab->mra", dmixed, pre_mixer, preferred_element_type=jnp.float32).astype(bf)
    dmixer = scatter_sum(dot_w(flatten(o), flatten(dmixed)).astype(bf).reshape(total, -1, width), one, total)
    dact_a = scatter_sum(dact_a.reshape(total, rows_a, -1), two, total)
    grads = [
        attend_back(queries[m : m + 1], keys[m : m + 1], values[m : m + 1], valid[m : m + 1], outs[m][1], dattn[m : m + 1])
        for m in range(micro)
    ]
    dk = jnp.concatenate([g[1] for g in grads]) + far_dk
    dv = jnp.concatenate([g[2] for g in grads]) + far_dv
    dqkv = jnp.concatenate([jnp.concatenate([g[0] for g in grads]), dk.astype(bf), dv.astype(bf)], axis=-1)
    dqkv_w = scatter_sum(dot_w(flatten(h1), flatten(dqkv)).astype(bf).reshape(total, rows_p, -1), three, total)
    dh1 = jnp.einsum("mrb,ab->mra", dqkv, pre_qkv, preferred_element_type=jnp.float32)
    pre_dgain = jnp.sum(dh1 * n1, axis=(0, 1))
    prefix_grad = dx1 + norm_back(dh1, n1, s1, pre_gain)
    smalls = jnp.concatenate(
        [
            dtable.reshape(total, -1),
            pre_dgain.reshape(total, rows_p),
            pre_dmid.reshape(total, rows_p),
            suf_dgain.reshape(total, rows_a),
            suf_dmid.reshape(total, rows_a),
        ],
        axis=1,
    )
    cut = smalls.shape[1]
    smalls = jnp.pad(smalls, ((0, 0), (0, -cut % 128))).reshape(total, -1, 128)
    smalls = scatter_sum(smalls, one, total).reshape(-1)
    f32 = jnp.float32
    at = dtable.size // total
    dact_a = dact_a.astype(f32)
    dqkv_w = dqkv_w.astype(f32)
    return (
        prefix_out[:, None],
        action_out[:, None],
        prefix_grad[:, None],
        action_grad[:, None],
        smalls[at : at + rows_p],
        dqkv_w[:, :hq],
        dqkv_w[:, hq : hq + depth],
        dqkv_w[:, hq + depth :],
        dmixer.astype(f32),
        smalls[at + rows_p : at + 2 * rows_p],
        dgate_w.astype(f32),
        dup_w.astype(f32),
        ddown.astype(f32),
        smalls[at + 2 * rows_p : at + 2 * rows_p + rows_a],
        dact_a[:, :hq],
        dact_a[:, hq : hq + depth],
        dact_a[:, hq + depth : hq + 2 * depth],
        dact_a[:, hq + 2 * depth :],
        smalls[at + 2 * rows_p + rows_a : at + 2 * rows_p + 2 * rows_a],
        dgu_a[0].astype(f32),
        dgu_a[1].astype(f32),
        ddown_a.astype(f32),
        smalls[:at].reshape(-1, levels),
    )


def solution(mesh):
    return jax.shard_map(
        per_device,
        mesh=mesh,
        in_specs=(
            P(None, ("dp", "noise"), None, None),
            P(None, ("dp", "noise"), None, None),
            P(None, ("dp", "noise")),
            P(None, ("dp", "noise")),
            P(None, "dp"),
            P(None, "dp"),
            P(("dp", "noise")),
            P(("dp", "noise"), None),
            P(("dp", "noise"), None),
            P(("dp", "noise"), None),
            P(("dp", "noise"), None),
            P(("dp", "noise")),
            P(("dp", "noise"), None),
            P(("dp", "noise"), None),
            P(("dp", "noise"), None),
            P(("dp", "noise")),
            P(("dp", "noise"), None),
            P(("dp", "noise"), None),
            P(("dp", "noise"), None),
            P(("dp", "noise"), None),
            P(("dp", "noise")),
            P(("dp", "noise"), None),
            P(("dp", "noise"), None),
            P(("dp", "noise"), None),
            P(("dp", "noise"), None),
            P(None, ("dp", "noise"), None, None),
            P(None, ("dp", "noise"), None, None),
        ),
        out_specs=(
            P(None, ("dp", "noise"), None, None),
            P(None, ("dp", "noise"), None, None),
            P(None, ("dp", "noise"), None, None),
            P(None, ("dp", "noise"), None, None),
            P(("dp", "noise")),
            P(("dp", "noise"), None),
            P(("dp", "noise"), None),
            P(("dp", "noise"), None),
            P(("dp", "noise"), None),
            P(("dp", "noise")),
            P(("dp", "noise"), None),
            P(("dp", "noise"), None),
            P(("dp", "noise"), None),
            P(("dp", "noise")),
            P(("dp", "noise"), None),
            P(("dp", "noise"), None),
            P(("dp", "noise"), None),
            P(("dp", "noise"), None),
            P(("dp", "noise")),
            P(("dp", "noise"), None),
            P(("dp", "noise"), None),
            P(("dp", "noise"), None),
            P(("dp", "noise"), None),
        ),
        check_vma=False,
    )
```

time: 2590 us -> 1040 us (0.40)
  waiting for transfers between devices: 1500 us -> 385 us
  blocking collectives: 534 us -> 25.4 us
  local copies, waits for them, and re-layouts: 83 us -> 173 us
  starting transfers between devices: 94.8 us -> 39.7 us
  other arithmetic: 67 us -> 120 us
    reduce_scatter x11 -> x3, waiting for transfers between devices: 1080 us -> 8.71 us  [the longest x1 8.69 us: per_device(): oa = lax.psum_scatter(mixed, 'noise', scatter_dimension=0)]
    unnamed x3 -> x0, blocking collectives: 333 us -> none
    all_gather x5 -> x0, blocking collectives: 201 us -> none  [the longest x1 42.4 us: per_device(): lax.all_gather(vlm_key, ('dp', 'noise'), axis=0, tiled=True)]
    all_gather x12 -> x9, waiting for transfers between devices: 417 us -> 239 us  [the longest x1 61.3 us: per_device(): lax.all_gather(jnp.concatenate([act_query, act_key, act_value, act_mixer,...]
    ppermute x0 -> x35, waiting for transfers between devices: none -> 120 us  [swap_bit(): return lax.ppermute(x, ALL, [(i, i ^ 1 << bit) for i in range(total)])]
    unnamed x31 -> x1, starting transfers between devices: 93.9 us -> 0.45 us
    ppermute x0 -> x35, starting transfers between devices: none -> 33.2 us  [swap_bit(): return lax.ppermute(x, ALL, [(i, i ^ 1 << bit) for i in range(total)])]
    add x5 -> x33, other arithmetic: 0.69 us -> 28.7 us  [the longest x29 27 us: scatter_sum(): x = keep + swap_bit(send, bit, total)]
  transfers between devices with their start and end apart: 54 -> 49, of which waited for: 16 -> 22; matrix products, arithmetic and copies ran while one was open for 25% -> 49% of each run, Pallas kernels for 0% -> 0%
where the time goes in v1:
time: 1040 us; the launch traced here: 1030 us
  waiting for transfers between devices  385 us (37%)
  matrix products  271 us (26%)
  local copies, waits for them, and re-layouts  173 us (17%)
  other arithmetic  120 us (12%)
  starting transfers between devices  39.7 us (4%)
  blocking collectives  25.4 us (2%)
  between operations  18.9 us (2%)
    ppermute x35, waiting for transfers between devices, swap_bit(): return lax.ppermute(x, ALL, [(i, i ^ 1 << bit) for i in range(total)])  120 us
    all_gather x1, waiting for transfers between devices, per_device(): lax.all_gather(jnp.concatenate([act_query, act_key, act_value, act_mixer,...  61.3 us
    all_gather x1, waiting for transfers between devices, per_device(): lax.all_gather(jnp.concatenate([vlm_gate, vlm_expand], axis=1), ALL, axis...  57.9 us
    all_gather x1, waiting for transfers between devices, per_device(): lax.all_gather(jnp.concatenate([vlm_query, vlm_key, vlm_value, extra], ax...  50.2 us
    dot_general x7, matrix products, dot_t(): lax.dot_general(a, b, (((1,), (1,)), ((), ())), preferred_element_type=jn...  47.9 us
    all_gather x1, waiting for transfers between devices, per_device(): lax.all_gather(jnp.concatenate([vlm_mixer, vlm_down], axis=0), ALL, axis=0)  46.6 us
    dot_general x9, matrix products, dot_w(): lax.dot_general(a, b, (((0,), (0,)), ((), ())), preferred_element_type=jn...  46.4 us
    dot_general x7, matrix products, dot(): return jnp.dot(a, b, preferred_element_type=jnp.float32)  42.5 us
  transfers between devices with their start and end apart: 49, of which 22 were waited for; matrix products, arithmetic and copies ran while one was open for 49% of the time, Pallas kernels for 0%

profile of v1, /device:TPU:0, one launch (start us, length us, event | category | flops | bytes accessed | tf_op | source)
XLA Modules:
  0.0 1033.3 jit_solution(8945106033654246817)
XLA Ops:
  20.2 61.3 %all-gather.15.cloned.1.call-done = bf16[1024,2688]{1,0:T(8,128)(2,1)} async-done(((bf16[32,2688]{1,0:T(8,128)(2,1)}), bf16[1024,2688]{1,0:T(8,128)(2,1)}) %all-gather.15.cloned.1.call-update) | async-done | bytes 5505040 | tf_op jit(solution)/shard_map/all_gather | solution.py:220
  91.6 50.2 %all-gather.29.cloned.1.call-done = bf16[32,20,1664]{2,1,0:T(8,128)(2,1)} async-done(((bf16[1,20,1664]{2,1,0:T(8,128)(2,1)}), bf16[32,20,1664]{2,1,0:T(8,128)(2,1)}) %all-gather.29.cloned.1.call-update) | async-done | bytes 2129936 | tf_op jit(solution)/shard_map/all_gather | solution.py:208
  141.9 4.1 reshape.945
  147.2 7.4 convolution_convert_fusion
  154.6 23.4 %all-gather.17.cloned.1.call-done = bf16[8,112,1536]{2,1,0:T(8,128)(2,1)} async-done(((bf16[1,112,1536]{2,1,0:T(8,128)(2,1)}), bf16[8,112,1536]{2,1,0:T(8,128)(2,1)}) %all-gather.17.cloned.1.call-update) | async-done | bytes 2752528 | tf_op jit(solution)/shard_map/all_gather | solution.py:273
  186.3 5.1 bitcast_reduce_fusion
  192.0 3.4 fusion.29
  196.3 5.2 fusion.236
  202.4 7.3 fusion.58
  213.0 25.4 %all_to_all.10 = bf16[8,2,32,512]{3,2,1,0:T(8,128)(2,1)S(1)} all-to-all(bf16[8,2,32,512]{3,2,1,0:T(8,128)(2,1)S(1)} %reshape.874), channel_id=1, replica_groups=mesh['dp'=4,'noise'=8] {'noise'}, dimensions={0} | all-to-all | bytes 1048576 | tf_op jit(solution)/shard_map/all_to_all | solution.py:230
  241.8 8.7 reduce-scatter.4.cloned.1.call-done
  271.4 5.9 fusion.23
  280.8 4.0 fusion.119
  289.5 4.0 fusion.120
  300.5 46.6 %all-gather.23.cloned.1.call-done = bf16[3072,640]{1,0:T(8,128)(2,1)} async-done(((bf16[96,640]{1,0:T(8,128)(2,1)}), bf16[3072,640]{1,0:T(8,128)(2,1)}) %all-gather.23.cloned.1.call-update) | async-done | bytes 3932176 | tf_op jit(solution)/shard_map/all_gather | solution.py:227
  351.2 6.0 multiply_reduce_fusion.2
  360.9 57.9 %all-gather.31.cloned.1.call-done = bf16[32,20,4096]{2,1,0:T(8,128)(2,1)} async-done(((bf16[1,20,4096]{2,1,0:T(8,128)(2,1)}), bf16[32,20,4096]{2,1,0:T(8,128)(2,1)}) %all-gather.31.cloned.1.call-update) | async-done | bytes 5242896 | tf_op jit(solution)/shard_map/all_gather | solution.py:226
  418.8 7.8 reshape.947
  426.6 10.5 %fusion.73 = f32[1632,2048]{1,0:T(8,128)} fusion(bf16[1632,640]{1,0:T(8,128)(2,1)} %bitcast.734, bf16[640,4096]{1,0:T(8,128)(2,1)} %reshape.947), kind=kOutput, calls=%fused_computation.124 | convolution fusion | flops 4278190080 | bytes 18079744 | tf_op jit(solution)/shard_map/dot_general | solution.py:146
  437.1 8.4 fusion.77
  445.5 21.8 %fusion.7 = (bf16[1632,2048]{1,0:T(8,128)(2,1)}, bf16[1632,2048]{1,0:T(8,128)(2,1)}, bf16[1632,2048]{1,0:T(8,128)(2,1)}) fusion(f32[1632,2048]{1,0:T(8,128)} %fusion.77, f32[1632,2048]{1,0:T(8,128)} %fusion.73, bf16[2048,640]{1,0:T(8,128)(2,1)S(1)} %bitcast.718, bf16[1632,640]{1,0:T(8,128)(2,1)S(1)} %bitcast.732), kind=kOutput, calls=%fused_computation.11 | convolution fusion | flops 4361748480 | bytes 51503104 | tf_op jit(solution)/shard_map/dot_general | solution.py:150
  467.4 9.5 convolution_convert_fusion.4
  476.9 5.5 fusion.75
  482.4 6.7 convolution_convert_fusion.3
  489.2 5.7 convolution_add_fusion
  497.5 7.7 bitcast_convert_fusion.1
  509.7 3.5 reshape.882
  513.3 5.2 fusion.165
  518.5 8.7 fusion.14
  528.6 5.2 fusion.162
  533.8 8.7 fusion.18
  542.5 5.2 reshape_reshape.27
  547.6 3.5 reshape_reshape.26
  551.2 3.6 constant_dynamic-slice_fusion.11
  561.8 6.5 convolution_convert_fusion.2
  570.2 7.9 fusion.45
  578.2 9.8 fusion.44
  588.0 11.1 %fusion.79 = bf16[2,1,816,640]{3,2,1,0:T(8,128)(2,1)} fusion(f32[2,816,640]{2,1,0:T(8,128)S(1)} %copy-done.7, bf16[2,816,2048]{2,1,0:T(8,128)(2,1)} %bitcast.790, bf16[2048,640,1]{1,0,2:T(8,128)(2,1)S(1)} %bitcast.719), kind=kOutput, calls=%fused_computation.131 | convolution fusion | flops 4280279040 | bytes 15572992 | tf_op jit(solution)/shard_map/dot_general | solution.py:146
  607.2 5.4 fusion.246
  612.6 5.2 fusion.94
  626.1 5.9 fusion.122
  634.5 3.7 fusion.121
  646.7 3.4 collective-permute-done.14
  654.3 3.8 constant_dynamic-slice_fusion.9
  669.0 14.3 %collective-permute-done.21 = bf16[8,1,20,2048]{3,0,2,1:T(8,128)(2,1)} collective-permute-done((bf16[8,1,20,2048]{3,0,2,1:T(8,128)(2,1)}, bf16[8,1,20,2048]{3,0,2,1:T(8,128)(2,1)}, u32[]{:S(2)}, u32[]{:S(2)}) %collective-permute-start.21) | collective-permute-done | bytes 655392 | tf_op jit(solution)/shard_map/ppermute | solution.py:87
  698.4 12.3 %collective-permute-done.22 = bf16[4,1,20,2048]{3,0,2,1:T(4,128)(2,1)S(1)} collective-permute-done((bf16[4,1,20,2048]{3,0,2,1:T(4,128)(2,1)S(1)}, bf16[4,1,20,2048]{3,0,2,1:T(4,128)(2,1)S(1)}, u32[]{:S(2)}, u32[]{:S(2)}) %collective-permute-start.22) | collective-permute-done | bytes 327712 | tf_op jit(solution)/shard_map/ppermute | solution.py:87
  733.6 15.7 %collective-permute-done.18 = bf16[2,1,20,2048]{3,1,2,0:T(2,128)(2,1)S(1)} collective-permute-done((bf16[2,1,20,2048]{3,1,2,0:T(2,128)(2,1)S(1)}, bf16[2,1,20,2048]{3,1,2,0:T(2,128)(2,1)S(1)}, u32[]{:S(2)}, u32[]{:S(2)}) %collective-permute-start.18) | collective-permute-done | bytes 163872 | tf_op jit(solution)/shard_map/ppermute | solution.py:87
  770.9 10.1 fusion.9
  781.0 9.6 fusion.12
  794.1 3.4 fusion.56
  803.3 3.4 reshape.886
  811.1 7.0 fusion.116
  818.2 6.3 fusion.115
  825.4 5.5 bitcast_convert_fusion
  843.7 3.7 all-reduce.11.cloned.1.call-done
  850.0 5.1 all-to-all-start.1
  865.5 12.9 %all-to-all-done.1 = bf16[8,32,1024]{2,1,0:T(8,128)(2,1)} async-done(((bf16[8,32,1024]{2,1,0:T(8,128)(2,1)}), bf16[8,32,1024]{2,1,0:T(8,128)(2,1)}, u32[]{:S(2)}, u32[]{:S(2)}) %all-to-all-start.1) | async-done | bytes 524320 | tf_op jit(solution)/shard_map/all_to_all | solution.py:323
  893.8 8.3 fusion.54
  902.7 3.7 collective-permute-done.7
  922.7 4.3 multiply_reduce_fusion.4
  949.4 25.4 %collective-permute-done.2 = f32[1,4,9,128]{3,2,1,0:T(8,128)S(1)} collective-permute-done((f32[1,4,9,128]{3,2,1,0:T(8,128)S(1)}, f32[1,4,9,128]{3,2,1,0:T(8,128)S(1)}, u32[]{:S(2)}, u32[]{:S(2)}) %collective-permute-start.2) | collective-permute-done | bytes 18464 | tf_op jit(solution)/shard_map/ppermute | solution.py:87
  982.3 26.5 %collective-permute-done.3 = f32[1,2,9,128]{3,2,1,0:T(8,128)S(1)} collective-permute-done((f32[1,2,9,128]{3,2,1,0:T(8,128)S(1)}, f32[1,2,9,128]{3,2,1,0:T(8,128)S(1)}, u32[]{:S(2)}, u32[]{:S(2)}) %collective-permute-start.3) | collective-permute-done | bytes 9248 | tf_op jit(solution)/shard_map/ppermute | solution.py:87
  1013.9 4.9 collective-permute-done.33
  1020.1 4.2 collective-permute-done.34
  (738 shorter events, 312.0 us)
Async XLA Ops:
  8.0 82.8 %copy-start = (s32[2,8]{1,0:T(2,128)S(1)}, s32[2,8]{1,0:T(2,128)}, u32[]{:S(2)}) copy-start(s32[2,8]{1,0:T(2,128)} %param.38) | copy-start | bytes 196
  8.0 76.3 %copy-start.140 = (s32[2,1]{0,1:T(1,128)S(1)}, s32[2,1]{0,1:T(1,128)}, u32[]{:S(2)}) copy-start(s32[2,1]{0,1:T(1,128)} %param.36) | copy-start | bytes 28
  8.1 73.4 %all-gather.15.cloned.1.call-start = ((), (), s32[]{:S(2)}) async-start(), calls=%async_computation.5 | async-start | bytes 5677056 | tf_op jit(solution)/shard_map/all_gather | solution.py:220
  12.2 129.7 %all-gather.29.cloned.1.call-start = ((), (), s32[]{:S(2)}) async-start(), calls=%async_computation.15 | async-start | bytes 2635776 | tf_op jit(solution)/shard_map/all_gather | solution.py:208
  17.8 160.3 %all-gather.17.cloned.1.call-start = ((), (), s32[]{:S(2)}) async-start(), calls=%async_computation.6 | async-start | bytes 3096576 | tf_op jit(solution)/shard_map/all_gather | solution.py:273
  19.6 65.7 %copy-start.21 = (f32[2,1,50,1024]{3,2,0,1:T(8,128)}, f32[2,1,50,1024]{3,2,0,1:T(8,128)S(1)}, u32[]{:S(2)}) copy-start(f32[2,1,50,1024]{3,2,0,1:T(8,128)S(1)} %copy_convert_fusion.1) | copy-start | bytes 1228804
  19.6 65.9 %copy-start.39 = (f32[100,1024]{1,0:T(8,128)}, f32[100,1024]{1,0:T(8,128)S(1)}, u32[]{:S(2)}) copy-start(f32[100,1024]{1,0:T(8,128)S(1)} %reshape.927) | copy-start | bytes 1228804
  20.1 237.1 %copy-start.133 = (f32[2,50]{1,0:T(2,128)}, f32[2,50]{1,0:T(2,128)S(1)}, u32[]{:S(2)}) copy-start(f32[2,50]{1,0:T(2,128)S(1)} %add_rsqrt_fusion.2) | copy-start | bytes 1204
  20.2 68.2 %copy-start.146 = (f32[100]{0:T(128)}, f32[100]{0:T(128)S(1)}, u32[]{:S(2)}) copy-start(f32[100]{0:T(128)S(1)} %rsqrt.43) | copy-start | bytes 1204
  84.3 169.2 %copy-start.117 = (f32[1024]{0:T(1024)}, f32[1024]{0:T(1024)S(1)}, u32[]{:S(2)}) copy-start(f32[1024]{0:T(1024)S(1)} %get-tuple-element.230) | copy-start | bytes 12292
  90.5 160.0 %reduce-scatter.4.cloned.1.call-start = ((), (), s32[]{:S(2)}) async-start(), calls=%async_computation.7 | async-start | bytes 2064384 | tf_op jit(solution)/shard_map/reduce_scatter | solution.py:290
  91.1 166.1 %copy-start.107 = (pred[2,816]{1,0:T(4,128)(4,1)}, pred[2,816]{1,0:T(4,128)(4,1)S(1)}, u32[]{:S(2)}) copy-start(pred[2,816]{1,0:T(4,128)(4,1)S(1)} %iota_compare_fusion) | copy-start | bytes 4900
  91.6 63.0 %copy-start.127 = (f32[2,816]{1,0:T(2,128)}, f32[2,816]{1,0:T(2,128)S(1)}, u32[]{:S(2)}) copy-start(f32[2,816]{1,0:T(2,128)S(1)} %add_rsqrt_fusion.1) | copy-start | bytes 19588
  212.0 83.1 %all-gather.25.cloned.1.call-start = ((), (), s32[]{:S(2)}) async-start(), calls=%async_computation.13 | async-start | bytes 3932160 | tf_op jit(solution)/shard_map/all_gather | solution.py:233
  240.0 107.1 %all-gather.23.cloned.1.call-start = ((), (), s32[]{:S(2)}) async-start(), calls=%async_computation.12 | async-start | bytes 4055040 | tf_op jit(solution)/shard_map/all_gather | solution.py:227
  240.8 178.0 %all-gather.31.cloned.1.call-start = ((), (), s32[]{:S(2)}) async-start(), calls=%async_computation.16 | async-start | bytes 6488064 | tf_op jit(solution)/shard_map/all_gather | solution.py:226
  241.6 365.6 %all-gather.19.cloned.1.call-start = ((), (), s32[]{:S(2)}) async-start(), calls=%async_computation.8 | async-start | bytes 2064384 | tf_op jit(solution)/shard_map/all_gather | solution.py:294
  255.1 357.5 %all-gather.21.cloned.1.call-start = ((), (), s32[]{:S(2)}) async-start(), calls=%async_computation.9 | async-start | bytes 2064384 | tf_op jit(solution)/shard_map/all_gather | solution.py:267
  257.1 462.3 %reduce-scatter.6.cloned.1.call-start = ((), (), s32[]{:S(2)}) async-start(), calls=%async_computation.10 | async-start | bytes 4128768 | tf_op jit(solution)/shard_map/reduce_scatter | solution.py:306
  351.1 94.4 %copy-start.47 = (bf16[32,64,640]{2,1,0:T(8,128)(2,1)}, bf16[32,64,640]{2,1,0:T(8,128)(2,1)S(1)}, u32[]{:S(2)}) copy-start(bf16[32,64,640]{2,1,0:T(8,128)(2,1)S(1)} %slice.320) | copy-start | bytes 7864324
  557.4 46.9 %collective-permute-start.10 = (bf16[16,1,32,640]{3,2,0,1:T(8,128)(2,1)}, bf16[16,1,32,640]{3,2,0,1:T(8,128)(2,1)}, u32[]{:S(2)}, u32[]{:S(2)}) collective-permute-start(bf16[16,1,32,640]{3,2,0,1:T(8,128)(2,1)} %dynamic-slice_bitcast_fusion.4), channel_id=1, source_target_pairs={{0,1},{1,0},{2,3},{3,2},{4,5},{5,4},{6,7},{7,6},{8,9},{9,8},{10,11... | collective-permute-start | bytes 1966088 | tf_op jit(solution)/shard_map/ppermute | solution.py:87
  561.3 89.4 %collective-permute-start.20 = (bf16[16,1,20,2048]{3,0,2,1:T(8,128)(2,1)}, bf16[16,1,20,2048]{3,0,2,1:T(8,128)(2,1)}, u32[]{:S(2)}, u32[]{:S(2)}) collective-permute-start(bf16[16,1,20,2048]{3,0,2,1:T(8,128)(2,1)} %bitcast.676), channel_id=1, source_target_pairs={{0,1},{1,0},{2,3},{3,2},{4,5},{5,4},{6,7},{7,6},{8,9},{9,8},{10,11... | collective-permute-start | bytes 3932168 | tf_op jit(solution)/shard_map/ppermute | solution.py:87
  561.5 97.9 %collective-permute-start.15 = (bf16[16,1,20,2048]{3,0,2,1:T(8,128)(2,1)}, bf16[16,1,20,2048]{3,0,2,1:T(8,128)(2,1)}, u32[]{:S(2)}, u32[]{:S(2)}) collective-permute-start(bf16[16,1,20,2048]{3,0,2,1:T(8,128)(2,1)} %bitcast.677), channel_id=1, source_target_pairs={{0,1},{1,0},{2,3},{3,2},{4,5},{5,4},{6,7},{7,6},{8,9},{9,8},{10,11... | collective-permute-start | bytes 3932168 | tf_op jit(solution)/shard_map/ppermute | solution.py:87
  569.6 96.8 %collective-permute-start.25 = (bf16[16,1,64,640]{3,2,0,1:T(8,128)(2,1)}, bf16[16,1,64,640]{3,2,0,1:T(8,128)(2,1)}, u32[]{:S(2)}, u32[]{:S(2)}) collective-permute-start(bf16[16,1,64,640]{3,2,0,1:T(8,128)(2,1)} %dynamic-slice_bitcast_fusion.1), channel_id=1, source_target_pairs={{0,1},{1,0},{2,3},{3,2},{4,5},{5,4},{6,7},{7,6},{8,9},{9,8},{10,11... | collective-permute-start | bytes 3932168 | tf_op jit(solution)/shard_map/ppermute | solution.py:87
  605.5 19.3 %collective-permute-start.11 = (bf16[1,8,32,640]{3,2,1,0:T(8,128)(2,1)S(1)}, bf16[1,8,32,640]{3,2,1,0:T(8,128)(2,1)S(1)}, u32[]{:S(2)}, u32[]{:S(2)}) collective-permute-start(bf16[1,8,32,640]{3,2,1,0:T(8,128)(2,1)S(1)} %dynamic-slice_bitcast_fusion.6), channel_id=1, source_target_pairs={{0,16},{1,17},{2,18},{3,19},{4,20},{5,21},{6,22},{7,23},{8,24},{9,... | collective-permute-start | bytes 983048 | tf_op jit(solution)/shard_map/ppermute | solution.py:87
  624.6 137.5 %all-gather.27.cloned.1.call-start = ((), (), s32[]{:S(2)}) async-start(), calls=%async_computation.14 | async-start | bytes 2064384 | tf_op jit(solution)/shard_map/all_gather | solution.py:335
  625.0 7.1 collective-permute-start.12
  632.7 11.1 %collective-permute-start.13 = (bf16[1,2,32,640]{3,2,1,0:T(8,128)(2,1)}, bf16[1,2,32,640]{3,2,1,0:T(8,128)(2,1)}, u32[]{:S(2)}, u32[]{:S(2)}) collective-permute-start(bf16[1,2,32,640]{3,2,1,0:T(8,128)(2,1)} %dynamic-slice_bitcast_fusion.11), channel_id=1, source_target_pairs={{0,4},{1,5},{2,6},{3,7},{4,0},{5,1},{6,2},{7,3},{8,12},{9,13},{10,... | collective-permute-start | bytes 245768 | tf_op jit(solution)/shard_map/ppermute | solution.py:87
  644.8 5.3 collective-permute-start.14
  659.4 23.9 %collective-permute-start.21 = (bf16[8,1,20,2048]{3,0,2,1:T(8,128)(2,1)}, bf16[8,1,20,2048]{3,0,2,1:T(8,128)(2,1)}, u32[]{:S(2)}, u32[]{:S(2)}) collective-permute-start(bf16[8,1,20,2048]{3,0,2,1:T(8,128)(2,1)} %bitcast.679), channel_id=1, source_target_pairs={{0,2},{1,3},{2,0},{3,1},{4,6},{5,7},{6,4},{7,5},{8,10},{9,11},{10,... | collective-permute-start | bytes 1966088 | tf_op jit(solution)/shard_map/ppermute | solution.py:87
  665.6 23.7 %collective-permute-start.16 = (bf16[2,4,20,2048]{3,1,2,0:T(4,128)(2,1)}, bf16[2,4,20,2048]{3,1,2,0:T(4,128)(2,1)}, u32[]{:S(2)}, u32[]{:S(2)}) collective-permute-start(bf16[2,4,20,2048]{3,1,2,0:T(4,128)(2,1)} %bitcast.680), channel_id=1, source_target_pairs={{0,8},{1,9},{2,10},{3,11},{4,12},{5,13},{6,14},{7,15},{8,0},{9,1},... | collective-permute-start | bytes 1966088 | tf_op jit(solution)/shard_map/ppermute | solution.py:87
  668.8 26.1 %collective-permute-start.26 = (bf16[1,8,64,640]{3,2,1,0:T(8,128)(2,1)}, bf16[1,8,64,640]{3,2,1,0:T(8,128)(2,1)}, u32[]{:S(2)}, u32[]{:S(2)}) collective-permute-start(bf16[1,8,64,640]{3,2,1,0:T(8,128)(2,1)} %dynamic-slice_bitcast_fusion.3), channel_id=1, source_target_pairs={{0,16},{1,17},{2,18},{3,19},{4,20},{5,21},{6,22},{7,23},{8,24},{9,... | collective-permute-start | bytes 1966088 | tf_op jit(solution)/shard_map/ppermute | solution.py:87
  687.2 23.5 %collective-permute-start.22 = (bf16[4,1,20,2048]{3,0,2,1:T(4,128)(2,1)S(1)}, bf16[4,1,20,2048]{3,0,2,1:T(4,128)(2,1)S(1)}, u32[]{:S(2)}, u32[]{:S(2)}) collective-permute-start(bf16[4,1,20,2048]{3,0,2,1:T(4,128)(2,1)S(1)} %bitcast.772), channel_id=1, source_target_pairs={{0,4},{1,5},{2,6},{3,7},{4,0},{5,1},{6,2},{7,3},{8,12},{9,13},{10,... | collective-permute-start | bytes 983048 | tf_op jit(solution)/shard_map/ppermute | solution.py:87
  694.0 23.8 %collective-permute-start.17 = (bf16[2,2,20,2048]{3,1,2,0:T(2,128)(2,1)}, bf16[2,2,20,2048]{3,1,2,0:T(2,128)(2,1)}, u32[]{:S(2)}, u32[]{:S(2)}) collective-permute-start(bf16[2,2,20,2048]{3,1,2,0:T(2,128)(2,1)} %bitcast.684), channel_id=1, source_target_pairs={{0,4},{1,5},{2,6},{3,7},{4,0},{5,1},{6,2},{7,3},{8,12},{9,13},{10,... | collective-permute-start | bytes 983048 | tf_op jit(solution)/shard_map/ppermute | solution.py:87
  696.9 29.1 %collective-permute-start.27 = (bf16[1,4,64,640]{3,2,1,0:T(8,128)(2,1)}, bf16[1,4,64,640]{3,2,1,0:T(8,128)(2,1)}, u32[]{:S(2)}, u32[]{:S(2)}) collective-permute-start(bf16[1,4,64,640]{3,2,1,0:T(8,128)(2,1)} %dynamic-slice_bitcast_fusion.5), channel_id=1, source_target_pairs={{0,8},{1,9},{2,10},{3,11},{4,12},{5,13},{6,14},{7,15},{8,0},{9,1},... | collective-permute-start | bytes 983048 | tf_op jit(solution)/shard_map/ppermute | solution.py:87
  713.7 16.8 %collective-permute-start.23 = (bf16[2,1,20,2048]{3,0,2,1:T(2,128)(2,1)}, bf16[2,1,20,2048]{3,0,2,1:T(2,128)(2,1)S(1)}, u32[]{:S(2)}, u32[]{:S(2)}) collective-permute-start(bf16[2,1,20,2048]{3,0,2,1:T(2,128)(2,1)} %bitcast.688), channel_id=1, source_target_pairs={{0,8},{1,9},{2,10},{3,11},{4,12},{5,13},{6,14},{7,15},{8,0},{9,1},... | collective-permute-start | bytes 491528 | tf_op jit(solution)/shard_map/ppermute | solution.py:87
  725.2 122.3 %all-reduce.11.cloned.1.call-start = ((), (), s32[]{:S(2)}) async-start(), calls=%async_computation.17 | async-start | bytes 6291456
  726.0 23.3 %collective-permute-start.18 = (bf16[2,1,20,2048]{3,1,2,0:T(2,128)(2,1)S(1)}, bf16[2,1,20,2048]{3,1,2,0:T(2,128)(2,1)S(1)}, u32[]{:S(2)}, u32[]{:S(2)}) collective-permute-start(bf16[2,1,20,2048]{3,1,2,0:T(2,128)(2,1)S(1)} %constant_dynamic-slice_fusion.13), channel_id=1, source_target_pairs={{0,2},{1,3},{2,0},{3,1},{4,6},{5,7},{6,4},{7,5},{8,10},{9,11},{10,... | collective-permute-start | bytes 491528 | tf_op jit(solution)/shard_map/ppermute | solution.py:87
  727.2 26.7 %collective-permute-start.28 = (bf16[1,2,64,640]{3,2,1,0:T(8,128)(2,1)S(1)}, bf16[1,2,64,640]{3,2,1,0:T(8,128)(2,1)S(1)}, u32[]{:S(2)}, u32[]{:S(2)}) collective-permute-start(bf16[1,2,64,640]{3,2,1,0:T(8,128)(2,1)S(1)} %dynamic-slice_bitcast_fusion.8), channel_id=1, source_target_pairs={{0,4},{1,5},{2,6},{3,7},{4,0},{5,1},{6,2},{7,3},{8,12},{9,13},{10,... | collective-permute-start | bytes 491528 | tf_op jit(solution)/shard_map/ppermute | solution.py:87
  732.1 102.8 %collective-permute-start.24 = (bf16[1,1,20,2048]{3,0,2,1:T(2,128)(2,1)}, bf16[1,1,20,2048]{3,0,2,1:T(2,128)(2,1)}, u32[]{:S(2)}, u32[]{:S(2)}) collective-permute-start(bf16[1,1,20,2048]{3,0,2,1:T(2,128)(2,1)} %constant_dynamic-slice_fusion.3), channel_id=1, source_target_pairs={{0,16},{1,17},{2,18},{3,19},{4,20},{5,21},{6,22},{7,23},{8,24},{9,... | collective-permute-start | bytes 245768 | tf_op jit(solution)/shard_map/ppermute | solution.py:87
  751.3 84.9 %collective-permute-start.19 = (bf16[1,1,20,2048]{3,1,2,0:T(2,128)(2,1)}, bf16[1,1,20,2048]{3,1,2,0:T(2,128)(2,1)}, u32[]{:S(2)}, u32[]{:S(2)}) collective-permute-start(bf16[1,1,20,2048]{3,1,2,0:T(2,128)(2,1)} %constant_dynamic-slice_fusion.12), channel_id=1, source_target_pairs={{0,16},{1,17},{2,18},{3,19},{4,20},{5,21},{6,22},{7,23},{8,24},{9,... | collective-permute-start | bytes 245768 | tf_op jit(solution)/shard_map/ppermute | solution.py:87
  754.5 84.3 %collective-permute-start.29 = (bf16[1,1,64,640]{3,2,1,0:T(8,128)(2,1)}, bf16[1,1,64,640]{3,2,1,0:T(8,128)(2,1)}, u32[]{:S(2)}, u32[]{:S(2)}) collective-permute-start(bf16[1,1,64,640]{3,2,1,0:T(8,128)(2,1)} %constant_dynamic-slice_fusion.2), channel_id=1, source_target_pairs={{0,2},{1,3},{2,0},{3,1},{4,6},{5,7},{6,4},{7,5},{8,10},{9,11},{10,... | collective-permute-start | bytes 245768 | tf_op jit(solution)/shard_map/ppermute | solution.py:87
  762.1 147.4 %reduce-scatter.8.cloned.1.call-start = ((), (), s32[]{:S(2)}) async-start(), calls=%async_computation.11 | async-start | bytes 3096576 | tf_op jit(solution)/shard_map/reduce_scatter | solution.py:343
  834.9 20.2 %collective-permute-start.5 = (bf16[16,1,20,1536]{3,0,2,1:T(8,128)(2,1)}, bf16[16,1,20,1536]{3,0,2,1:T(8,128)(2,1)S(1)}, u32[]{:S(2)}, u32[]{:S(2)}) collective-permute-start(bf16[16,1,20,1536]{3,0,2,1:T(8,128)(2,1)} %bitcast.678), channel_id=1, source_target_pairs={{0,1},{1,0},{2,3},{3,2},{4,5},{5,4},{6,7},{7,6},{8,9},{9,8},{10,11... | collective-permute-start | bytes 2949128 | tf_op jit(solution)/shard_map/ppermute | solution.py:87
  850.0 28.4 %all-to-all-start.1 = ((bf16[8,32,1024]{2,1,0:T(8,128)(2,1)}), bf16[8,32,1024]{2,1,0:T(8,128)(2,1)}, u32[]{:S(2)}, u32[]{:S(2)}) async-start(bf16[8,32,1024]{2,1,0:T(8,128)(2,1)} %bitcast.191), calls=%async_computation.4 | async-start | bytes 1048576 | tf_op jit(solution)/shard_map/all_to_all | solution.py:323
  861.0 28.3 %collective-permute-start.6 = (bf16[8,1,20,1536]{3,0,2,1:T(8,128)(2,1)}, bf16[8,1,20,1536]{3,0,2,1:T(8,128)(2,1)}, u32[]{:S(2)}, u32[]{:S(2)}) collective-permute-start(bf16[8,1,20,1536]{3,0,2,1:T(8,128)(2,1)} %bitcast.682), channel_id=1, source_target_pairs={{0,2},{1,3},{2,0},{3,1},{4,6},{5,7},{6,4},{7,5},{8,10},{9,11},{10,... | collective-permute-start | bytes 1474568 | tf_op jit(solution)/shard_map/ppermute | solution.py:87
  893.7 12.7 %collective-permute-start.7 = (bf16[4,1,20,1536]{3,0,2,1:T(4,128)(2,1)S(1)}, bf16[4,1,20,1536]{3,0,2,1:T(4,128)(2,1)S(1)}, u32[]{:S(2)}, u32[]{:S(2)}) collective-permute-start(bf16[4,1,20,1536]{3,0,2,1:T(4,128)(2,1)S(1)} %bitcast.777), channel_id=1, source_target_pairs={{0,4},{1,5},{2,6},{3,7},{4,0},{5,1},{6,2},{7,3},{8,12},{9,13},{10,... | collective-permute-start | bytes 737288 | tf_op jit(solution)/shard_map/ppermute | solution.py:87
  908.0 6.8 collective-permute-start.8
  914.8 22.4 %collective-permute-start.30 = (bf16[16,1,32,2560]{3,2,0,1:T(8,128)(2,1)}, bf16[16,1,32,2560]{3,2,0,1:T(8,128)(2,1)}, u32[]{:S(2)}, u32[]{:S(2)}) collective-permute-start(bf16[16,1,32,2560]{3,2,0,1:T(8,128)(2,1)} %fusion.65), channel_id=1, source_target_pairs={{0,1},{1,0},{2,3},{3,2},{4,5},{5,4},{6,7},{7,6},{8,9},{9,8},{10,11... | collective-permute-start | bytes 7864328 | tf_op jit(solution)/shard_map/ppermute | solution.py:87
  916.0 5.8 collective-permute-start.9
  937.1 6.3 collective-permute-start
  942.8 32.1 %collective-permute-start.31 = (bf16[2,4,32,2560]{3,2,1,0:T(8,128)(2,1)}, bf16[2,4,32,2560]{3,2,1,0:T(8,128)(2,1)}, u32[]{:S(2)}, u32[]{:S(2)}) collective-permute-start(bf16[2,4,32,2560]{3,2,1,0:T(8,128)(2,1)} %dynamic-slice_bitcast_fusion), channel_id=1, source_target_pairs={{0,8},{1,9},{2,10},{3,11},{4,12},{5,13},{6,14},{7,15},{8,0},{9,1},... | collective-permute-start | bytes 3932168 | tf_op jit(solution)/shard_map/ppermute | solution.py:87
  943.4 4.3 collective-permute-start.1
  945.4 34.4 %copy-start.57 = (f32[2,1,50,1024]{3,2,0,1:T(8,128)S(1)}, f32[2,1,50,1024]{3,2,0,1:T(8,128)}, u32[]{:S(2)}) copy-start(f32[2,1,50,1024]{3,2,0,1:T(8,128)} %reshape.885) | copy-start | bytes 1228804
  945.4 34.4 %copy-start.58 = (f32[2,1,50,1024]{3,2,0,1:T(8,128)S(1)}, f32[2,1,50,1024]{3,2,0,1:T(8,128)}, u32[]{:S(2)}) copy-start(f32[2,1,50,1024]{3,2,0,1:T(8,128)} %reshape.878) | copy-start | bytes 1228804
  945.4 34.4 %copy-start.95 = (bf16[2,1,50,1024]{3,0,2,1:T(2,128)(2,1)S(1)}, bf16[2,1,50,1024]{3,0,2,1:T(2,128)(2,1)}, u32[]{:S(2)}) copy-start(bf16[2,1,50,1024]{3,0,2,1:T(2,128)(2,1)} %param.34) | copy-start | bytes 614404
  945.4 34.4 %copy-start.97 = (bf16[2,1,50,1024]{3,0,2,1:T(2,128)(2,1)S(1)}, bf16[2,1,50,1024]{3,0,2,1:T(2,128)(2,1)}, u32[]{:S(2)}) copy-start(bf16[2,1,50,1024]{3,0,2,1:T(2,128)(2,1)} %param.59) | copy-start | bytes 614404
  947.8 27.1 %collective-permute-start.2 = (f32[1,4,9,128]{3,2,1,0:T(8,128)S(1)}, f32[1,4,9,128]{3,2,1,0:T(8,128)S(1)}, u32[]{:S(2)}, u32[]{:S(2)}) collective-permute-start(f32[1,4,9,128]{3,2,1,0:T(8,128)S(1)} %dynamic-slice_bitcast_fusion.13), channel_id=1, source_target_pairs={{0,8},{1,9},{2,10},{3,11},{4,12},{5,13},{6,14},{7,15},{8,0},{9,1},... | collective-permute-start | bytes 55304 | tf_op jit(solution)/shard_map/ppermute | solution.py:87
  976.8 32.1 %collective-permute-start.32 = (bf16[2,2,32,2560]{3,2,1,0:T(8,128)(2,1)S(1)}, bf16[2,2,32,2560]{3,2,1,0:T(8,128)(2,1)S(1)}, u32[]{:S(2)}, u32[]{:S(2)}) collective-permute-start(bf16[2,2,32,2560]{3,2,1,0:T(8,128)(2,1)S(1)} %dynamic-slice_bitcast_fusion.2), channel_id=1, source_target_pairs={{0,4},{1,5},{2,6},{3,7},{4,0},{5,1},{6,2},{7,3},{8,12},{9,13},{10,... | collective-permute-start | bytes 1966088 | tf_op jit(solution)/shard_map/ppermute | solution.py:87
  976.9 32.0 %collective-permute-start.3 = (f32[1,2,9,128]{3,2,1,0:T(8,128)S(1)}, f32[1,2,9,128]{3,2,1,0:T(8,128)S(1)}, u32[]{:S(2)}, u32[]{:S(2)}) collective-permute-start(f32[1,2,9,128]{3,2,1,0:T(8,128)S(1)} %fusion.215), channel_id=1, source_target_pairs={{0,4},{1,5},{2,6},{3,7},{4,0},{5,1},{6,2},{7,3},{8,12},{9,13},{10,... | collective-permute-start | bytes 27656 | tf_op jit(solution)/shard_map/ppermute | solution.py:87
  980.2 45.4 %copy-start.1 = (s32[2,8]{1,0:T(2,128)S(1)}, s32[2,8]{1,0:T(2,128)}, u32[]{:S(2)}) copy-start(s32[2,8]{1,0:T(2,128)} %param.38) | copy-start | bytes 196
  1008.8 3.7 collective-permute-start.4
  1009.0 9.8 collective-permute-start.33
  1018.8 5.4 collective-permute-start.34
  (164 other events, 1433.7 us)
Sparse Core Ops, SparseCore 0:
  12.5 68.9 all-gather.14
  84.9 56.8 all-gather.28
  144.1 33.9 all-gather.16
  212.1 38.2 reduce-scatter.3
  624.7 56.6 reduce-scatter.5
  833.5 44.7 reduce-scatter.7
Sparse Core Ops, SparseCore 1:
  240.1 42.2 all-gather.24
  285.8 61.2 all-gather.22
  350.5 68.2 all-gather.30
  420.4 25.3 all-gather.18
  447.5 26.3 all-gather.20
  725.3 31.1 all-gather.26
  762.1 85.3 all-reduce.10

commit v2 on v1

v2 whole, which is shorter than its diff:
```python
import jax
import jax.numpy as jnp
from jax import lax
from jax.experimental import pallas as pl
from jax.experimental.pallas import tpu as pltpu
from jax.sharding import PartitionSpec as P

EPS = 1e-06
HIGH = lax.Precision.HIGHEST
ALL = ("dp", "noise")
BF = jnp.bfloat16
F32 = jnp.float32
ROOT = 0.7978845608028654
MASKED = -1e30


def normed(rows):
    factor = lax.rsqrt(jnp.mean(rows * rows, axis=-1, keepdims=True) + EPS)
    return (rows * factor, factor)


def norm_back(grad_hidden, normal, factor, gain_mod):
    grad_normal = grad_hidden * gain_mod
    centred = jnp.mean(grad_normal * normal, axis=-1, keepdims=True)
    return factor * (grad_normal - normal * centred)


def flatten(array):
    return array.reshape(-1, array.shape[-1])


def gelu_parts(gate):
    square = gate * gate
    t = jnp.tanh(gate * (ROOT + (ROOT * 0.044715) * square))
    half = 0.5 + 0.5 * t
    slope = half + (gate * (1.0 - t * t)) * ((0.5 * ROOT) + (1.5 * 0.044715 * ROOT) * square)
    return gate * half, slope


def dot(a, b):
    return lax.dot_general(a, b, (((1,), (0,)), ((), ())), preferred_element_type=F32)


def dot_t(a, b):
    return lax.dot_general(a, b, (((1,), (1,)), ((), ())), preferred_element_type=F32)


def dot_w(a, b):
    return lax.dot_general(a, b, (((0,), (0,)), ((), ())), preferred_element_type=F32)


class Line:
    def __init__(self, axes):
        self.axes = axes
        names = (axes,) if isinstance(axes, str) else axes
        self.count, self.me = 1, 0
        for name in names:
            self.count *= lax.axis_size(name)
            self.me = self.me * lax.axis_size(name) + lax.axis_index(name)
        self.bits = list(range(self.count.bit_length() - 1))

    def across(self, x, mask):
        return lax.ppermute(x, self.axes, [(i, i ^ mask) for i in range(self.count)])

    def swap(self, x, bit):
        return self.across(x, 1 << bit)

    def around(self, x, gate=()):
        parts = [self.across(x, far << 1) for far in range(1, self.count // 2)]
        if gate:
            parts = list(after(parts, *gate))
        parts = jnp.stack([x] + parts)
        both = jnp.stack([parts, self.swap(parts, 0)], axis=1)
        return both.reshape((self.count,) + x.shape)

    def home(self, x):
        x = x.reshape((self.count // 2, 2) + x.shape[1:])
        return x[:, 0] + self.swap(x[:, 1], 0)

    def home_end(self, x, gate=()):
        parts = [self.across(x[far], far << 1) for far in range(1, self.count // 2)]
        if gate:
            parts = list(after(parts, *gate))
        return sum((part.astype(F32) for part in parts), x[0].astype(F32))


class Sum:
    def __init__(self, x, dp, line):
        self.x, self.dp, self.line = x, dp, line
        self.rest = x.shape[1:]

    def cores(self):
        x = self.x.reshape((self.dp.count, self.line.count // 2, 2) + self.rest)
        mine = self.line.me % 2
        keep = lax.dynamic_index_in_dim(x, mine, 2, keepdims=False)
        send = lax.dynamic_index_in_dim(x, 1 - mine, 2, keepdims=False)
        self.x = keep + self.line.swap(send, 0)
        return self

    def all_pairs(self, line, me, count, shift, gate):
        mine = lax.dynamic_index_in_dim(self.x, me, 0, keepdims=False).astype(F32)
        parts = []
        for k in range(1, count):
            part = lax.dynamic_index_in_dim(self.x, me ^ k, 0, keepdims=False)
            parts.append(line.across(part, k << shift))
        if gate:
            parts = after(parts, *gate)
        return sum((part.astype(F32) for part in parts), mine)

    def groups(self, gate=()):
        self.x = self.all_pairs(self.dp, self.dp.me, self.dp.count, 0, gate).astype(self.x.dtype)
        return self

    def along(self, gate=()):
        return self.all_pairs(self.line, self.line.me // 2, self.line.count // 2, 1, gate)


def turned(x, me):
    count = x.shape[0]

    def kernel(me_ref, x_ref, out_ref):
        for k in range(count):
            out_ref[me_ref[0] ^ k] = x_ref[k]

    whole = pl.BlockSpec(x.shape, lambda i, me: (0,) * x.ndim, pipeline_mode=pl.Buffered(1))
    return pl.pallas_call(
        kernel,
        grid_spec=pltpu.PrefetchScalarGridSpec(
            num_scalar_prefetch=1, grid=(1,), in_specs=[whole], out_specs=whole
        ),
        out_shape=jax.ShapeDtypeStruct(x.shape, x.dtype),
        compiler_params=params(32, 1),
        name="turn",
    )(me.astype(jnp.int32)[None], x)


def tiles(x, gap, back=None):
    if back is None:
        rows, cols = x.shape
        count = rows // 8 * (cols // 128)
        high = gap // 8
        wide = -(-count // high)
        x = x.reshape(rows // 8, 8, cols // 128, 128).transpose(0, 2, 1, 3).reshape(count, 8, 128)
        x = jnp.pad(x, ((0, high * wide - count), (0, 0), (0, 0)))
        return x.reshape(high, wide, 8, 128).transpose(0, 2, 1, 3).reshape(gap, wide * 128)
    rows, cols = back
    count = rows // 8 * (cols // 128)
    high, wide = gap // 8, x.shape[-1] // 128
    x = x.reshape(-1, high, 8, wide, 128).transpose(0, 1, 3, 2, 4).reshape(-1, high * wide, 8, 128)
    x = x[:, :count].reshape(-1, rows // 8, cols // 128, 8, 128).transpose(0, 1, 3, 2, 4)
    return x.reshape(-1, cols)


def params(megabytes, dims):
    return pltpu.CompilerParams(
        vmem_limit_bytes=megabytes << 20, dimension_semantics=("arbitrary",) * dims
    )


def chained(kernel, at, count):
    def inner(*refs):
        kernel(*refs[:at], *refs[at + count :])

    return inner


def kept(count):
    return [pl.BlockSpec(memory_space=pl.ANY)] * count


def after(values, *others):
    def kernel(*refs):
        pass

    where = pl.BlockSpec(memory_space=pl.ANY)
    return pl.pallas_call(
        kernel,
        in_specs=[where] * (len(values) + len(others)),
        out_specs=[where] * len(values),
        out_shape=[jax.ShapeDtypeStruct(v.shape, v.dtype) for v in values],
        input_output_aliases={i: i for i in range(len(values))},
        name="after",
    )(*values, *others)


def cost(flops, moved, exps=0):
    return pl.CostEstimate(flops=flops, bytes_accessed=moved, transcendentals=exps)


def attend_kernel(step, len_ref, q_ref, k_ref, v_ref, o_ref, lse_ref):
    depth = k_ref.shape[-1]
    q = q_ref[0] * (depth**-0.5)
    s = dot_t(k_ref[0], q.astype(BF))
    ids = lax.broadcasted_iota(jnp.int32, s.shape, 0)
    s = jnp.where(ids < len_ref[step], s, MASKED)
    top = jnp.max(s, axis=0, keepdims=True)
    e = jnp.exp(s - top)
    total = jnp.sum(e, axis=0, keepdims=True)
    p = (e * (1.0 / total)).astype(BF)
    o_ref[0] = dot_w(p, v_ref[0]).astype(BF)
    lse_ref[0, 0] = top + jnp.log(total)


def attend(step, qkv, lens, heads, before=(), gate=()):
    micro, rows, all_width = qkv.shape
    depth = all_width // (heads + 2)
    spec = lambda f: pl.BlockSpec((1, rows, depth), f)

    def kernel(*refs):
        attend_kernel(step, *refs)

    return pl.pallas_call(
        chained(kernel, 4, len(before) + len(gate)),
        grid_spec=pltpu.PrefetchScalarGridSpec(
            num_scalar_prefetch=1,
            grid=(heads,),
            in_specs=[
                spec(lambda h, s: (step, 0, h)),
                spec(lambda h, s: (step, 0, heads)),
                spec(lambda h, s: (step, 0, heads + 1)),
            ]
            + kept(len(before) + len(gate)),
            out_specs=[
                spec(lambda h, s: (step, 0, h)),
                pl.BlockSpec((1, 1, 1, rows), lambda h, s: (step, h, 0, 0)),
            ],
        ),
        out_shape=[
            jax.ShapeDtypeStruct((micro, rows, heads * depth), BF),
            jax.ShapeDtypeStruct((micro, heads, 1, rows), F32),
        ],
        input_output_aliases={4 + i: i for i in range(len(before))},
        compiler_params=params(48, 1),
        cost_estimate=cost(4 * heads * rows * rows * depth, 2 * rows * all_width * 2),
        name="attend",
    )(lens, qkv, qkv, qkv, *before, *gate)


def attend_back_kernel(step, len_ref, q_ref, k_ref, v_ref, do_ref, lse_ref, dq_ref, dk_ref, dv_ref):
    depth = k_ref.shape[-1]
    scale = depth**-0.5

    @pl.when(pl.program_id(0) == 0)
    def _():
        dk_ref[...] = jnp.zeros_like(dk_ref)
        dv_ref[...] = jnp.zeros_like(dv_ref)

    q = (q_ref[0] * scale).astype(BF)
    do = do_ref[0]
    s = dot_t(k_ref[0], q)
    ids = lax.broadcasted_iota(jnp.int32, s.shape, 0)
    p = jnp.where(ids < len_ref[step], jnp.exp(s - lse_ref[0, 0]), 0.0)
    dv_ref[0] += dot(p.astype(BF), do)
    dp = dot_t(v_ref[0], do)
    centre = jnp.sum(p * dp, axis=0, keepdims=True)
    ds = (p * (dp - centre)).astype(BF)
    dk_ref[0] += dot(ds, q)
    dq_ref[0] = (dot_w(ds, k_ref[0]) * scale).astype(BF)


def attend_back(step, qkv, dout, lse, lens, heads, before=(), gate=()):
    micro, rows, all_width = qkv.shape
    depth = all_width // (heads + 2)
    spec = lambda f: pl.BlockSpec((1, rows, depth), f)

    def kernel(*refs):
        attend_back_kernel(step, *refs)

    return pl.pallas_call(
        chained(kernel, 6, len(before) + len(gate)),
        grid_spec=pltpu.PrefetchScalarGridSpec(
            num_scalar_prefetch=1,
            grid=(heads,),
            in_specs=[
                spec(lambda h, s: (step, 0, h)),
                spec(lambda h, s: (step, 0, heads)),
                spec(lambda h, s: (step, 0, heads + 1)),
                spec(lambda h, s: (step, 0, h)),
                pl.BlockSpec((1, 1, 1, rows), lambda h, s: (step, h, 0, 0)),
            ]
            + kept(len(before) + len(gate)),
            out_specs=[
                spec(lambda h, s: (step, 0, h)),
                spec(lambda h, s: (step, 0, 0)),
                spec(lambda h, s: (step, 0, 0)),
            ],
        ),
        out_shape=[
            jax.ShapeDtypeStruct((micro, rows, heads * depth), BF),
            jax.ShapeDtypeStruct((micro, rows, depth), F32),
            jax.ShapeDtypeStruct((micro, rows, depth), F32),
        ],
        input_output_aliases={6 + i: i for i in range(len(before))},
        compiler_params=params(48, 1),
        cost_estimate=cost(10 * heads * rows * rows * depth, 5 * rows * all_width * 2),
        name="attend_back",
    )(lens, qkv, qkv, qkv, dout, lse, *before, *gate)


def feed_kernel(
    o_ref, x_ref, cot_ref, wm_ref, gain_ref, wg_ref, wu_ref, wd_ref, spread_ref,
    out_ref, dx_ref, dmixed_ref, dattn_ref, hw_ref, mid_ref, dgate_ref, dup_ref, dgain_ref,
    h_ref, acc_ref, dh_ref,
):
    at = pl.program_id(0)
    last = pl.num_programs(0) - 1

    @pl.when(at == 0)
    def _():
        x1 = x_ref[...].astype(F32) + dot(o_ref[...], wm_ref[...])
        h = (normed(x1)[0] * gain_ref[...]).astype(BF)
        h_ref[...] = h
        hw_ref[...] = dot(h, spread_ref[...]).astype(BF)
        acc_ref[...] = x1
        dx_ref[...] = x1
        dh_ref[...] = jnp.zeros_like(dh_ref)

    h = h_ref[...]
    dy = cot_ref[...]
    gate = dot(h, wg_ref[...])
    up = dot(h, wu_ref[...])
    dmid = dot_t(dy, wd_ref[...])
    act, slope = gelu_parts(gate)
    mid = (act * up).astype(BF)
    dgate = (dmid * up * slope).astype(BF)
    dup = (dmid * act).astype(BF)
    mid_ref[...] = mid
    dgate_ref[...] = dgate
    dup_ref[...] = dup
    acc_ref[...] += dot(mid, wd_ref[...])
    dh_ref[...] += dot_t(dgate, wg_ref[...]) + dot_t(dup, wu_ref[...])

    @pl.when(at == last)
    def _():
        out_ref[...] = acc_ref[...].astype(BF)
        normal, factor = normed(dx_ref[...])
        dh = dh_ref[...]
        dgain_ref[...] = jnp.sum(dh * normal, axis=0, keepdims=True)
        dx = cot_ref[...].astype(F32) + norm_back(dh, normal, factor, gain_ref[...])
        dx_ref[...] = dx
        dmixed = dx.astype(BF)
        dmixed_ref[...] = dmixed
        dattn_ref[...] = dot_t(dmixed, wm_ref[...]).astype(BF)


def feed(step, micro, o, x, cot, wm, gain, wgu, wd, spread, before=(), gate=()):
    total, width = x.shape
    rows = total // micro
    hq, ff = o.shape[1], wd.shape[0]
    unit = 512
    chunks = ff // unit
    once = dict(pipeline_mode=pl.Buffered(1))
    row = lambda w: pl.BlockSpec((rows, w), lambda i: (step, 0), **once)
    col = lambda f: pl.BlockSpec((rows, unit), f)
    whole = lambda a: pl.BlockSpec(a.shape, lambda i: (0, 0), **once)
    out = lambda w, t: jax.ShapeDtypeStruct((total, w), t)
    wide = spread.shape[1]
    kernel = chained(feed_kernel, 9, len(before) + len(gate))
    return pl.pallas_call(
        kernel,
        grid=(chunks,),
        in_specs=[row(hq), row(width), row(width), whole(wm), whole(gain)]
        + [
            pl.BlockSpec((width, unit), lambda i: (0, i)),
            pl.BlockSpec((width, unit), lambda i: (0, chunks + i)),
            pl.BlockSpec((unit, width), lambda i: (i, 0)),
            whole(spread),
        ]
        + kept(len(before) + len(gate)),
        out_specs=[row(width), row(width), row(width), row(hq), row(wide)]
        + [col(lambda i: (step, i))] * 3
        + [pl.BlockSpec((1, width), lambda i: (0, 0))],
        out_shape=[
            out(width, BF), out(width, F32), out(width, BF), out(hq, BF), out(wide, BF),
            out(ff, BF), out(ff, BF), out(ff, BF), jax.ShapeDtypeStruct((1, width), F32),
        ],
        scratch_shapes=[
            pltpu.VMEM((rows, width), BF),
            pltpu.VMEM((rows, width), F32),
            pltpu.VMEM((rows, width), F32),
        ],
        input_output_aliases={9 + i: i for i in range(len(before))},
        compiler_params=params(60, 1),
        cost_estimate=cost(rows * (12 * width * ff + 4 * width * hq), rows * ff * 8 + wgu.size * 3),
        name="feed",
    )(o, x, cot, wm, gain, wgu, wgu, wd, spread, *before, *gate)


def weight_grad_kernel(x_ref, *refs):
    *g_refs, out_ref, turned_ref = refs
    at = pl.program_id(0)

    @pl.when(at == 0)
    def _():
        turned_ref[...] = x_ref[...].T

    each = pl.num_programs(0) // len(g_refs)
    for i, g_ref in enumerate(g_refs):

        @pl.when(at // each == i)
        def _():
            out_ref[...] = dot(turned_ref[...], g_ref[...]).astype(BF)


def weight_grad(x, grads, unit, columns=None, gate=()):
    rows, width = x.shape
    each = grads[0].shape[1] // unit
    count = each * len(grads)
    columns = columns or count * unit

    def place(i):
        return pl.BlockSpec(
            (rows, unit), lambda at: (0, jnp.clip(at - i * each, 0, each - 1))
        )

    return pl.pallas_call(
        chained(weight_grad_kernel, 1 + len(grads), len(gate)),
        grid=(count,),
        in_specs=[
            pl.BlockSpec((rows, width), lambda at: (0, 0), pipeline_mode=pl.Buffered(1))
        ]
        + [place(i) for i in range(len(grads))]
        + kept(len(gate)),
        out_specs=pl.BlockSpec((width, unit), lambda at: (0, at)),
        out_shape=jax.ShapeDtypeStruct((width, columns), BF),
        scratch_shapes=[pltpu.VMEM((width, rows), BF)],
        compiler_params=params(48, 1),
        cost_estimate=cost(2 * rows * width * count * unit, 2 * rows * (width + count * unit)),
        name="weight_grad",
    )(x, *grads, *gate)


def stack_heads(x, heads):
    depth = x.shape[-1] // heads
    return jnp.concatenate([x[:, h * depth : (h + 1) * depth] for h in range(heads)], axis=0)


def own_scores(heads, scale, length, seg_len, qkv_ref, k_ref):
    depth = k_ref.shape[-1]
    qkv = qkv_ref[0, 0].astype(F32)
    q = (stack_heads(qkv[:, : heads * depth], heads) * scale).astype(BF)
    near_k = qkv[:, heads * depth : (heads + 1) * depth].astype(BF)
    near_v = qkv[:, (heads + 1) * depth :].astype(BF)
    far = dot_t(k_ref[0], q)
    near = dot_t(near_k, q)
    far_ok = lax.broadcasted_iota(jnp.int32, far.shape, 0) < length
    near_ok = lax.broadcasted_iota(jnp.int32, near.shape, 0) < seg_len
    return q, near_k, near_v, jnp.where(far_ok, far, MASKED), jnp.where(near_ok, near, MASKED)


def own_kernel(heads, seg_len, own_ref, len_ref, qkv_ref, k_ref, v_ref, o_ref, lse_ref):
    m, c = pl.program_id(0), pl.program_id(1)
    mine = own_ref[m * pl.num_programs(1) + c] == 1
    depth = k_ref.shape[-1]
    rows = qkv_ref.shape[2]

    @pl.when(mine)
    def _():
        q, near_k, near_v, far, near = own_scores(
            heads, depth**-0.5, len_ref[m], seg_len, qkv_ref, k_ref
        )
        top = jnp.maximum(
            jnp.max(far, axis=0, keepdims=True), jnp.max(near, axis=0, keepdims=True)
        )
        far, near = jnp.exp(far - top), jnp.exp(near - top)
        total = jnp.sum(far, axis=0, keepdims=True) + jnp.sum(near, axis=0, keepdims=True)
        part = 1.0 / total
        o = dot_w((far * part).astype(BF), v_ref[0]) + dot_w((near * part).astype(BF), near_v)
        for h in range(heads):
            o_ref[0, 0, :, h * depth : (h + 1) * depth] = o[h * rows : (h + 1) * rows].astype(BF)
        lse_ref[0, 0] = top + jnp.log(total)

    @pl.when(jnp.logical_not(mine))
    def _():
        o_ref[...] = jnp.zeros_like(o_ref)
        lse_ref[...] = jnp.zeros_like(lse_ref)


def own_attend(seg_qkv, qkv, own, lens, heads, seg_len):
    n, micro, rows, all_width = seg_qkv.shape
    depth = all_width // (heads + 2)
    prefix = qkv.shape[1]
    seg = lambda w: pl.BlockSpec((1, 1, rows, w), lambda m, c, a, b: (c, m, 0, 0))
    stat = pl.BlockSpec((1, 1, 1, heads * rows), lambda m, c, a, b: (c, m, 0, 0))

    def kernel(*refs):
        own_kernel(heads, seg_len, *refs)

    return pl.pallas_call(
        kernel,
        grid_spec=pltpu.PrefetchScalarGridSpec(
            num_scalar_prefetch=2,
            grid=(micro, n),
            in_specs=[
                seg(all_width),
                pl.BlockSpec((1, prefix, depth), lambda m, c, a, b: (m, 0, heads)),
                pl.BlockSpec((1, prefix, depth), lambda m, c, a, b: (m, 0, heads + 1)),
            ],
            out_specs=[seg(heads * depth), stat],
        ),
        out_shape=[
            jax.ShapeDtypeStruct((n, micro, rows, heads * depth), BF),
            jax.ShapeDtypeStruct((n, micro, 1, heads * rows), F32),
        ],
        compiler_params=params(32, 2),
        cost_estimate=cost(4 * 2 * micro * heads * rows * prefix * depth, 4 * seg_qkv.size),
        name="own_attend",
    )(own, lens, seg_qkv, qkv, qkv)


def own_back_kernel(
    heads, seg_len, own_ref, len_ref, qkv_ref, k_ref, v_ref, do_ref, lse_ref, dqkv_ref, dk_ref, dv_ref
):
    m, c = pl.program_id(0), pl.program_id(1)
    mine = own_ref[m * pl.num_programs(1) + c] == 1
    depth = k_ref.shape[-1]
    rows = qkv_ref.shape[2]
    scale = depth**-0.5

    @pl.when(c == 0)
    def _():
        dk_ref[...] = jnp.zeros_like(dk_ref)
        dv_ref[...] = jnp.zeros_like(dv_ref)

    @pl.when(mine)
    def _():
        q, near_k, near_v, far, near = own_scores(heads, scale, len_ref[m], seg_len, qkv_ref, k_ref)
        far, near = jnp.exp(far - lse_ref[0, 0]), jnp.exp(near - lse_ref[0, 0])
        do = stack_heads(do_ref[0, 0].astype(F32), heads).astype(BF)
        dv_ref[0] += dot(far.astype(BF), do)
        dfar, dnear = dot_t(v_ref[0], do), dot_t(near_v, do)
        centre = jnp.sum(far * dfar, axis=0, keepdims=True)
        centre = centre + jnp.sum(near * dnear, axis=0, keepdims=True)
        sfar = (far * (dfar - centre)).astype(BF)
        snear = (near * (dnear - centre)).astype(BF)
        dk_ref[0] += dot(sfar, q)
        dq = (dot_w(sfar, k_ref[0]) + dot_w(snear, near_k)) * scale
        for h in range(heads):
            dqkv_ref[0, 0, :, h * depth : (h + 1) * depth] = dq[h * rows : (h + 1) * rows].astype(BF)
        dqkv_ref[0, 0, :, heads * depth : (heads + 1) * depth] = dot(snear, q).astype(BF)
        dqkv_ref[0, 0, :, (heads + 1) * depth :] = dot(near.astype(BF), do).astype(BF)

    @pl.when(jnp.logical_not(mine))
    def _():
        dqkv_ref[...] = jnp.zeros_like(dqkv_ref)


def own_back(seg_qkv, qkv, dout, lse, own, lens, heads, seg_len):
    n, micro, rows, all_width = seg_qkv.shape
    depth = all_width // (heads + 2)
    prefix = qkv.shape[1]
    seg = lambda w: pl.BlockSpec((1, 1, rows, w), lambda m, c, a, b: (c, m, 0, 0))
    item = lambda i: pl.BlockSpec((1, prefix, depth), lambda m, c, a, b: (m, 0, i))

    def kernel(*refs):
        own_back_kernel(heads, seg_len, *refs)

    return pl.pallas_call(
        kernel,
        grid_spec=pltpu.PrefetchScalarGridSpec(
            num_scalar_prefetch=2,
            grid=(micro, n),
            in_specs=[
                seg(all_width),
                item(heads),
                item(heads + 1),
                seg(heads * depth),
                pl.BlockSpec((1, 1, 1, heads * rows), lambda m, c, a, b: (c, m, 0, 0)),
            ],
            out_specs=[seg(all_width), item(0), item(0)],
        ),
        out_shape=[
            jax.ShapeDtypeStruct((n, micro, rows, all_width), BF),
            jax.ShapeDtypeStruct((micro, prefix, depth), F32),
            jax.ShapeDtypeStruct((micro, prefix, depth), F32),
        ],
        compiler_params=params(32, 2),
        cost_estimate=cost(10 * 2 * micro * heads * rows * prefix * depth, 8 * seg_qkv.size),
        name="own_back",
    )(own, lens, seg_qkv, qkv, qkv, dout, lse)


def per_device(
    prefix_rows,
    action_rows,
    segment_item,
    segment_time,
    item_weight,
    prefix_len,
    vlm_prenorm,
    vlm_query,
    vlm_key,
    vlm_value,
    vlm_mixer,
    vlm_midnorm,
    vlm_gate,
    vlm_expand,
    vlm_down,
    act_prenorm,
    act_query,
    act_key,
    act_value,
    act_mixer,
    act_midnorm,
    act_gate,
    act_expand,
    act_down,
    time_scales,
    cot_prefix,
    cot_action,
):
    micro, items, prefix, width = prefix_rows.shape
    seg_len, wide = action_rows.shape[2:]
    groups, n = lax.axis_size("dp"), lax.axis_size("noise")
    depth, hq = vlm_key.shape[1], vlm_query.shape[1]
    heads = hq // depth
    joint = hq + 2 * depth
    ff, ffa = vlm_gate.shape[1], act_gate.shape[1]
    levels = time_scales.shape[1]
    rows_p, rows_a = vlm_query.shape[0], act_query.shape[0]
    here = lax.axis_index("noise")
    every, line = Line(ALL), Line("noise")
    total = every.count
    dp = Line("dp")
    slot = -(-(seg_len + 1) // 8) * 8
    block = micro * slot

    lanes = lambda x, w: jnp.pad(x, ((0, 0), (0, w - x.shape[1])))
    gap = -(-rows_p // 8) * 8
    taller = lambda x: jnp.pad(x, ((0, gap - rows_p), (0, 0)))
    rows_m = vlm_mixer.shape[0]
    unit = act_down.shape[0]
    part = groups * unit

    item, time = segment_item[:, 0], segment_time[:, 0]
    spare = jnp.zeros((micro, slot - seg_len, wide), BF)
    tags = spare.at[:, 0, 0].set(item.astype(BF)).at[:, 0, 1].set(time.astype(BF))
    action_in = jnp.concatenate([action_rows[:, 0], tags], axis=1)
    hot = item[:, None] == jnp.arange(prefix_len.shape[1])[None, :]
    weight = (jnp.sum(jnp.where(hot, item_weight, 0), axis=1) + 1).astype(F32) / 8.0
    grad_action = cot_action[:, 0].astype(F32) * weight[:, None, None]
    grad_action = jnp.pad(grad_action, ((0, 0), (0, slot - seg_len), (0, 0)))

    pre_pack = jnp.concatenate(
        [
            vlm_query,
            vlm_key,
            vlm_value,
            lanes(jnp.stack([vlm_prenorm, vlm_midnorm], axis=1), 128),
        ],
        axis=1,
    )
    act_small = [act_prenorm[:, None], act_midnorm[:, None], time_scales.reshape(rows_a, -1)]
    act_pack = [act_query, act_key, act_value, lanes(jnp.concatenate(act_small, axis=1), 128)]
    act_pack = jnp.concatenate(act_pack, axis=1)
    first = [act_pack, taller(pre_pack), lanes(tiles(act_mixer, gap), act_pack.shape[1])]
    first = lax.all_gather(jnp.concatenate(first, axis=0), ALL, axis=0)
    act_a = first[:, :rows_a].reshape(total * rows_a, -1)
    pre_a = first[:, rows_a : rows_a + gap].reshape(total * gap, -1)
    suf_mixer = first[:, rows_a + gap :]

    fold = jnp.concatenate([vlm_mixer, vlm_down], axis=0)
    second = [taller(vlm_gate), taller(vlm_expand), tiles(fold, gap)]
    second = lax.all_gather(jnp.concatenate(second, axis=1), ALL, axis=0)

    cols = jnp.stack([act_gate, act_expand]).reshape(2, rows_a, groups, n, unit)
    cols = cols.transpose(3, 0, 1, 2, 4).reshape(n, 2, rows_a, part)
    cols = lax.all_to_all(cols, "noise", 0, 0, tiled=True)
    cols = cols.transpose(0, 2, 1, 3).reshape(n * rows_a, 2 * part)
    hidden_w = jnp.concatenate([cols, act_down.reshape(-1, 2 * part)], axis=0)
    hidden_w = jnp.stack([hidden_w] + [dp.across(hidden_w, k) for k in range(1, groups)])
    hidden_w = turned(hidden_w, dp.me)
    gu_w = hidden_w[:, : n * rows_a].reshape(-1, 2 * part)
    down_w = hidden_w[:, n * rows_a :].reshape(part, wide)
    dy_all = line.around(grad_action.astype(BF).reshape(block, wide)).reshape(-1, wide)

    seg_all = line.around(action_in)

    places = jnp.arange(total * gap)
    spread = (places // gap * rows_p + places % gap)[None, :] == jnp.arange(width)[:, None]
    spread = (spread & (places % gap < rows_p)[None, :]).astype(BF)
    pre_a = dot(spread, pre_a).astype(BF)
    pre_qkv = pre_a[:, :joint]
    pre_gain = pre_a[:, joint].astype(F32)
    pre_midgain = pre_a[:, joint + 1].astype(F32)
    suf_qkv = act_a[:, :joint]
    small = act_a[:, joint:].astype(F32)
    suf_gain, suf_midgain = small[:, 0], small[:, 1]
    table = small[:, 2 : 2 + time_scales.size // rows_a].reshape(2 * wide, levels)

    times = seg_all[:, :, seg_len, 1].astype(jnp.int32)
    own = (seg_all[:, :, seg_len, 0].astype(jnp.int32) == here).astype(jnp.int32)
    own = own.T.reshape(-1)
    is_row = (jnp.arange(slot) < seg_len)[:, None]
    hots = (times[..., None] == jnp.arange(levels)).astype(F32)
    mods = jnp.einsum("nmt,jt->nmj", hots, table, precision=HIGH)
    mod1_all = mods[:, :, None, :wide]
    mod2 = mods[0, :, None, wide:]
    an1, as1 = normed(jnp.where(is_row, seg_all, 0).astype(F32))
    ah1 = flatten((an1 * suf_gain * mod1_all).astype(BF))
    seg_qkv = dot(ah1, suf_qkv).astype(BF).reshape(n, micro, slot, joint)

    x = prefix_rows[:, 0]
    n1, s1 = normed(x.astype(F32))
    h1 = flatten((n1 * pre_gain).astype(BF))
    qkv = dot(h1, pre_qkv).astype(BF).reshape(micro, prefix, joint)
    lens = lax.dynamic_slice_in_dim(prefix_len, here, 1, axis=1)[:, 0]

    oa, lse_a = own_attend(seg_qkv, qkv, own, lens, heads, seg_len)

    outs = attend(0, qkv, lens, heads, (), (oa,))
    oa = line.home(oa.reshape(n, block, hq))
    outs = attend(1, qkv, lens, heads, outs, (oa,))
    o, lse = outs
    oa = line.home_end(oa, (o,)).astype(BF)
    suf_mixer = suf_mixer[..., : tiles(act_mixer, gap).shape[1]]
    suf_mixer = tiles(suf_mixer, gap, act_mixer.shape)
    a1 = jnp.where(is_row, action_in, 0).astype(F32) + dot(oa, suf_mixer).reshape(micro, slot, wide)
    an2, as2 = normed(a1)
    ah2 = (an2 * suf_midgain * mod2).astype(BF).reshape(block, wide)

    h_all = line.around(ah2).reshape(n * block, wide)
    gu = dot(h_all, gu_w)
    gate_a, up_a = gu[:, :part], gu[:, part:]
    act_g, slope_g = gelu_parts(gate_a)
    mid_a = (act_g * up_a).astype(BF)
    dmid_a = dot_t(dy_all, down_w)
    dgu = jnp.concatenate(
        [(dmid_a * up_a * slope_g).astype(BF), (dmid_a * act_g).astype(BF)], axis=1
    )
    grad_late = line.home(dot_t(dgu, gu_w).astype(BF).reshape(n, block, wide))
    out_a = line.home(dot(mid_a, down_w).astype(BF).reshape(n, block, wide))
    dff = jnp.concatenate(
        [
            dot_w(h_all, dgu).astype(BF).reshape(groups, n * rows_a, 2 * part),
            dot_w(mid_a, dy_all).astype(BF).reshape(groups, -1, 2 * part),
        ],
        axis=1,
    )
    dff = dff.reshape(-1, 2 * part)
    dff = lax.psum_scatter(dff, "dp", scatter_dimension=0, tiled=True)

    pre_gu = dot(spread, second[..., : 2 * ff].reshape(total * gap, -1)).astype(BF)
    fold = tiles(second[..., 2 * ff :], gap, fold.shape).reshape(total, -1, width)
    pre_mixer = fold[:, :rows_m].reshape(hq, width)
    pre_down = fold[:, rows_m:].reshape(ff, width)
    cot = cot_prefix.reshape(micro * prefix, width)

    def feed_half(step, outs, gate):
        return feed(
            step, micro, o.reshape(-1, hq), x.reshape(-1, width), cot,
            pre_mixer, pre_midgain[None], pre_gu, pre_down, spread, outs, gate,
        )

    outs = feed_half(0, (), (grad_late,))
    pre_dmid = outs[-1]
    grad_late = line.home_end(grad_late, (outs[0],)).reshape(micro, slot, wide)
    late_back = grad_late * an2
    suf_dmid = jnp.sum(late_back * mod2, axis=(0, 1))
    dmod2 = jnp.sum(late_back * suf_midgain, axis=1)
    da1 = grad_action + norm_back(grad_late, an2, as2, suf_midgain * mod2)
    dmixed_a = da1.astype(BF).reshape(block, wide)
    dattn_a = dot_t(dmixed_a, suf_mixer).astype(BF)
    outs = feed_half(1, outs[:-1], (dattn_a,))
    pre_dmid = pre_dmid + outs[-1]
    prefix_out, dx1, dmixed, dattn, h2, mid, dgate, dup = outs[:-1]
    dattn_all = line.around(dattn_a, (dx1,)).reshape(n, micro, slot, hq)

    dmd_w = jnp.concatenate(
        [
            weight_grad(o.reshape(-1, hq), [dmixed], width).reshape(total, rows_m, width),
            weight_grad(mid, [cot], width, gate=(dx1,)).reshape(total, -1, width),
        ],
        axis=1,
    )
    grads = [dmd_w, dot_w(oa, dmixed_a).astype(BF).reshape(total, rows_a, -1)]
    grads = [jax.vmap(lambda g: tiles(g, gap))(g) for g in grads]
    cut = grads[0].shape[-1]
    grads = jnp.concatenate(grads, axis=-1)
    grads_sum = lax.psum_scatter(grads, ALL, scatter_dimension=0)
    dmd_w = tiles(grads_sum[:, :cut], gap, dmd_w.shape[1:])
    dam_w = tiles(grads_sum[:, cut:], gap, (rows_a, wide))

    dseg, far_dk, far_dv = own_back(seg_qkv, qkv, dattn_all, lse_a, own, lens, heads, seg_len)
    dseg = dseg.reshape(n * block, joint)
    act_sum = Sum(dot_w(ah1, dseg).astype(BF).reshape(total, rows_a, -1), dp, line).cores()

    big_w = weight_grad(h2, [dgate, dup], 512, gate=(act_sum.x, grads))
    big_sum = Sum(big_w.reshape(total, gap, -1), dp, line).cores()
    dattn = dattn.reshape(micro, prefix, hq)
    outs = attend_back(0, qkv, dattn, lse, lens, heads, (), (big_w,))
    act_sum.groups((outs[0],))
    outs = attend_back(1, qkv, dattn, lse, lens, heads, outs, (big_sum.x, act_sum.x))
    dq, dk, dv = outs
    big_sum.groups((dq,))
    dkv = jnp.concatenate([(dk + far_dk).astype(BF), (dv + far_dv).astype(BF)], axis=-1)
    dqkv = jnp.concatenate([dq, dkv], axis=-1).reshape(-1, joint)
    h1_wide = dot(h1, spread).astype(BF)
    pre_sum = weight_grad(h1_wide, [dqkv], 512).reshape(total, gap, -1)
    pre_sum = Sum(pre_sum, dp, line).cores()

    dah1 = dot_t(dseg, suf_qkv).reshape(n, micro, slot, wide)
    first_back = dah1 * an1
    suf_dgain = jnp.sum(first_back * mod1_all, axis=(0, 1, 2))
    dmod1 = jnp.sum(first_back * suf_gain, axis=2)
    back = norm_back(dah1, an1, as1, suf_gain * mod1_all).astype(BF).reshape(n, block, wide)
    back = line.home_end(line.home(back)).reshape(micro, slot, wide)
    out_a = line.home_end(out_a).reshape(micro, slot, wide)
    action_out = (a1 + out_a)[:, :seg_len].astype(BF)
    action_grad = (da1 + back)[:, :seg_len]
    dtable = jnp.concatenate(
        [
            jnp.einsum("nmj,nmt->jt", dmod1, hots, precision=HIGH),
            jnp.einsum("mj,mt->jt", dmod2, hots[0], precision=HIGH),
        ],
        axis=0,
    )
    dh1 = dot_t(dqkv, pre_qkv).reshape(micro, prefix, width)
    pre_dgain = jnp.sum(dh1 * n1, axis=(0, 1))
    prefix_grad = dx1.reshape(micro, prefix, width) + norm_back(dh1, n1, s1, pre_gain)

    ddown_a = dff[n * rows_a :].reshape(unit, wide)
    dgu_a = dff[: n * rows_a].reshape(n, rows_a, 2 * part)
    dgu_a = lax.all_to_all(dgu_a, "noise", 0, 0, tiled=True)
    dgu_a = dgu_a.reshape(n, rows_a, 2, groups, unit).transpose(2, 1, 3, 0, 4)
    dgu_a = dgu_a.reshape(2, rows_a, ffa)
    smalls = jnp.concatenate(
        [
            dtable.reshape(total, -1),
            pre_dgain.reshape(total, rows_p),
            pre_dmid.reshape(total, rows_p),
            suf_dgain.reshape(total, rows_a),
            suf_dmid.reshape(total, rows_a),
        ],
        axis=1,
    )
    smalls = lanes(smalls, -(-smalls.shape[1] // 128) * 128).reshape(total, -1, 128)
    small_sum = Sum(smalls, dp, line)
    smalls = small_sum.cores().groups().along().reshape(-1)
    act_g = act_sum.along()
    big_g = big_sum.along()[:rows_p]
    pre_g = pre_sum.groups().along()[:rows_p]
    at = [dtable.size // total]
    for size in (rows_p, rows_p, rows_a, rows_a):
        at.append(at[-1] + size)
    return (
        prefix_out.reshape(prefix_rows.shape),
        action_out[:, None],
        prefix_grad[:, None],
        action_grad[:, None],
        smalls[at[0] : at[1]],
        pre_g[:, :hq],
        pre_g[:, hq : hq + depth],
        pre_g[:, hq + depth :],
        dmd_w[:rows_m].astype(F32),
        smalls[at[1] : at[2]],
        big_g[:, :ff],
        big_g[:, ff:],
        dmd_w[rows_m:].astype(F32),
        smalls[at[2] : at[3]],
        act_g[:, :hq],
        act_g[:, hq : hq + depth],
        act_g[:, hq + depth :],
        dam_w.astype(F32),
        smalls[at[3] : at[4]],
        dgu_a[0].astype(F32),
        dgu_a[1].astype(F32),
        ddown_a.astype(F32),
        smalls[: at[0]].reshape(-1, levels),
    )


def solution(mesh):
    return jax.shard_map(
        per_device,
        mesh=mesh,
        in_specs=(
            P(None, ("dp", "noise"), None, None),
            P(None, ("dp", "noise"), None, None),
            P(None, ("dp", "noise")),
            P(None, ("dp", "noise")),
            P(None, "dp"),
            P(None, "dp"),
            P(("dp", "noise")),
            P(("dp", "noise"), None),
            P(("dp", "noise"), None),
            P(("dp", "noise"), None),
            P(("dp", "noise"), None),
            P(("dp", "noise")),
            P(("dp", "noise"), None),
            P(("dp", "noise"), None),
            P(("dp", "noise"), None),
            P(("dp", "noise")),
            P(("dp", "noise"), None),
            P(("dp", "noise"), None),
            P(("dp", "noise"), None),
            P(("dp", "noise"), None),
            P(("dp", "noise")),
            P(("dp", "noise"), None),
            P(("dp", "noise"), None),
            P(("dp", "noise"), None),
            P(("dp", "noise"), None),
            P(None, ("dp", "noise"), None, None),
            P(None, ("dp", "noise"), None, None),
        ),
        out_specs=(
            P(None, ("dp", "noise"), None, None),
            P(None, ("dp", "noise"), None, None),
            P(None, ("dp", "noise"), None, None),
            P(None, ("dp", "noise"), None, None),
            P(("dp", "noise")),
            P(("dp", "noise"), None),
            P(("dp", "noise"), None),
            P(("dp", "noise"), None),
            P(("dp", "noise"), None),
            P(("dp", "noise")),
            P(("dp", "noise"), None),
            P(("dp", "noise"), None),
            P(("dp", "noise"), None),
            P(("dp", "noise")),
            P(("dp", "noise"), None),
            P(("dp", "noise"), None),
            P(("dp", "noise"), None),
            P(("dp", "noise"), None),
            P(("dp", "noise")),
            P(("dp", "noise"), None),
            P(("dp", "noise"), None),
            P(("dp", "noise"), None),
            P(("dp", "noise"), None),
        ),
        check_vma=False,
    )
```

time: 1040 us -> 667 us (0.64)
  waiting for transfers between devices: 385 us -> 156 us
  matrix products: 271 us -> 50.5 us
  Pallas kernels: 0 us -> 156 us
  local copies, waits for them, and re-layouts: 173 us -> 90.4 us
  starting transfers between devices: 39.7 us -> 116 us
  other arithmetic: 120 us -> 73.8 us
  blocking collectives: 25.4 us -> 0 us
    dot_general x53 -> x20, matrix products: 271 us -> 50.5 us  [the longest x8 25.6 us: dot(): lax.dot_general(a, b, (((1,), (0,)), ((), ())), preferred_element_type=F32)]
    all_gather x9 -> x2, waiting for transfers between devices: 239 us -> 52.4 us  [the longest x1 52.4 us: per_device(): first = lax.all_gather(jnp.concatenate(first, axis=0), ALL, axis=0)]
    pallas_call x0 -> x18, Pallas kernels: none -> 156 us  [the longest x2 62.4 us: feed(): pl.pallas_call(kernel, grid=(chunks,), in_specs=[row(hq), row(width), row...]
    ppermute x35 -> x63, starting transfers between devices: 33.2 us -> 102 us  [across(): lax.ppermute(x, self.axes, [(i, i ^ mask) for i in range(self.count)])]
    dynamic_slice x17 -> x1, local copies, waits for them, and re-layouts: 26.6 us -> 0.19 us  [per_device(): lens = lax.dynamic_slice_in_dim(prefix_len, here, 1, axis=1)[:, 0]]
    all_to_all x1 -> x0, blocking collectives: 25.4 us -> none  [per_device(): lax.all_to_all(cols.transpose(3, 0, 1, 2, 4).reshape(n, 2, rows_a, groups...]
    another operation x13 -> x5, local copies, waits for them, and re-layouts: 25.3 us -> 0.93 us
    unnamed x381 -> x241, local copies, waits for them, and re-layouts: 42.3 us -> 23.9 us
  transfers between devices with their start and end apart: 49 -> 69, of which waited for: 22 -> 22; matrix products, arithmetic and copies ran while one was open for 49% -> 28% of each run, Pallas kernels for 0% -> 24%
where the time goes in v2:
time: 667 us; the launch traced here: 658 us
  waiting for transfers between devices  156 us (23%)
  Pallas kernels  156 us (23%)
  starting transfers between devices  116 us (17%)
  local copies, waits for them, and re-layouts  90.4 us (14%)
  other arithmetic  73.8 us (11%)
  matrix products  50.5 us (8%)
  between operations  15.9 us (2%)
    ppermute x63, waiting for transfers between devices, across(): lax.ppermute(x, self.axes, [(i, i ^ mask) for i in range(self.count)])  104 us
    ppermute x63, starting transfers between devices, across(): lax.ppermute(x, self.axes, [(i, i ^ mask) for i in range(self.count)])  102 us
    pallas_call x2, Pallas kernels, feed(): pl.pallas_call(kernel, grid=(chunks,), in_specs=[row(hq), row(width), row...  62.4 us
    all_gather x1, waiting for transfers between devices, per_device(): first = lax.all_gather(jnp.concatenate(first, axis=0), ALL, axis=0)  52.4 us
    pallas_call x4, Pallas kernels, weight_grad(): pl.pallas_call(chained(weight_grad_kernel, 1 + len(grads), len(gate)), gr...  39.3 us
    pallas_call x2, Pallas kernels, attend_back(): pl.pallas_call(chained(kernel, 6, len(before) + len(gate)), grid_spec=plt...  28.5 us
    dot_general x8, matrix products, dot(): lax.dot_general(a, b, (((1,), (0,)), ((), ())), preferred_element_type=F32)  25.6 us
    unnamed x241, local copies, waits for them, and re-layouts  23.9 us
  transfers between devices with their start and end apart: 69, of which 22 were waited for; matrix products, arithmetic and copies ran while one was open for 28% of the time, Pallas kernels for 24%

profile of v2, /device:TPU:0, one launch (start us, length us, event | category | flops | bytes accessed | tf_op | source)
XLA Modules:
  0.0 658.4 jit_solution(11398699608624401446)
XLA Ops:
  20.3 3.1 collective-permute-start
  23.4 2.6 collective-permute-start.1
  27.4 5.1 all-to-all-start
  33.3 4.0 collective-permute-done
  37.3 13.1 %collective-permute-done.1 = bf16[2,56,1024]{2,1,0:T(8,128)(2,1)} collective-permute-done((bf16[2,56,1024]{2,1,0:T(8,128)(2,1)S(1)}, bf16[2,56,1024]{2,1,0:T(8,128)(2,1)}, u32[]{:S(2)}, u32[]{:S(2)}) %collective-permute-start.1) | collective-permute-done | bytes 229408 | tf_op jit(solution)/shard_map/ppermute | solution.py:63
  58.4 52.4 %all-gather.5.cloned.1.call-done = bf16[2560,1664]{1,0:T(8,128)(2,1)} async-done(((bf16[80,1664]{1,0:T(8,128)(2,1)}), bf16[2560,1664]{1,0:T(8,128)(2,1)}) %all-gather.5.cloned.1.call-update) | async-done | bytes 8519696 | tf_op jit(solution)/shard_map/all_gather | solution.py:657
  113.0 4.6 slice.355
  125.0 3.4 convolution_convert_fusion.2
  128.5 4.6 convolution_convert_fusion
  138.1 3.4 collective-permute-start.5
  141.6 4.0 collective-permute-start.6
  145.6 17.3 %collective-permute-done.5 = bf16[112,1024]{1,0:T(8,128)(2,1)S(1)} collective-permute-done((bf16[112,1024]{1,0:T(8,128)(2,1)S(1)}, bf16[112,1024]{1,0:T(8,128)(2,1)S(1)}, u32[]{:S(2)}, u32[]{:S(2)}) %collective-permute-start.5) | collective-permute-done | bytes 229408 | tf_op jit(solution)/shard_map/ppermute | solution.py:63
  163.0 9.8 %collective-permute-done.7 = bf16[112,1024]{1,0:T(8,128)(2,1)} collective-permute-done((bf16[112,1024]{1,0:T(8,128)(2,1)S(1)}, bf16[112,1024]{1,0:T(8,128)(2,1)}, u32[]{:S(2)}, u32[]{:S(2)}) %collective-permute-start.7) | collective-permute-done | bytes 229408 | tf_op jit(solution)/shard_map/ppermute | solution.py:63
  172.7 2.4 fusion.119
  183.2 10.9 %attend.2 = (bf16[2,816,1024]{2,1,0:T(8,128)(2,1)S(1)}, f32[2,4,1,816]{3,2,1,0:T(1,128)S(1)}) custom-call(s32[2]{0:T(128)S(1)} %fusion.114.refs_1_.refs_0_, bf16[2,816,1536]{2,1,0:T(8,128)(2,1)} %bitcast.485, bf16[2,816,1536]{2,1,0:T(8,128)(2,1)} %bitcast.486, bf16[2,816,1536]{2,1,0:T(8,128)(2,1)} %bitcast.487, bf16[8,2,56,1024]{3,2,1,0:T(8,128)(2,1)S(1)} %copy-done.8), custom_call_target="tpu_custom_call" | custom-call | flops 2727346176 | bytes 5013504 | tf_op jit(solution)/shard_map/attend/pallas_call | solution.py:212
  195.5 4.9 collective-permute-start.12
  203.1 10.9 %attend.3 = (bf16[2,816,1024]{2,1,0:T(8,128)(2,1)S(1)}, f32[2,4,1,816]{3,2,1,0:T(1,128)S(1)}) custom-call(s32[2]{0:T(128)S(1)} %fusion.114.refs_1_.refs_0_, bf16[2,816,1536]{2,1,0:T(8,128)(2,1)} %bitcast.488, bf16[2,816,1536]{2,1,0:T(8,128)(2,1)} %bitcast.489, bf16[2,816,1536]{2,1,0:T(8,128)(2,1)} %bitcast.490, ...), custom_call_target="tpu_custom_call", output_to_operand_aliasing={{0}: (4, {}), {1}: (5, {})} | custom-call | flops 2727346176 | bytes 5013504 | tf_op jit(solution)/shard_map/attend/pallas_call | solution.py:212
  217.5 6.9 %collective-permute-start.11 = (bf16[384,1024]{1,0:T(8,128)(2,1)}, bf16[384,1024]{1,0:T(8,128)(2,1)}, u32[]{:S(2)}, u32[]{:S(2)}) collective-permute-start(bf16[384,1024]{1,0:T(8,128)(2,1)} %constant_dynamic-update-slice_fusion), channel_id=1, source_target_pairs={{0,24},{8,16},{16,8},{24,0},{1,25},{9,17},{17,9},{25,1},{2,26},{10... | collective-permute-start | bytes 2359304 | tf_op jit(solution)/shard_map/ppermute | solution.py:63
  230.5 10.4 %collective-permute-start.15 = (bf16[112,1024]{1,0:T(8,128)(2,1)S(1)}, bf16[112,1024]{1,0:T(8,128)(2,1)S(1)}, u32[]{:S(2)}, u32[]{:S(2)}) collective-permute-start(bf16[112,1024]{1,0:T(8,128)(2,1)S(1)} %bitcast.594), channel_id=1, source_target_pairs={{0,2},{1,3},{2,0},{3,1},{4,6},{5,7},{6,4},{7,5},{8,10},{9,11},{10,... | collective-permute-start | bytes 688136 | tf_op jit(solution)/shard_map/ppermute | solution.py:63
  243.2 5.0 collective-permute-done.15
  253.0 7.6 %collective-permute-done.16 = bf16[112,1024]{1,0:T(8,128)(2,1)S(1)} collective-permute-done((bf16[112,1024]{1,0:T(8,128)(2,1)S(1)}, bf16[112,1024]{1,0:T(8,128)(2,1)S(1)}, u32[]{:S(2)}, u32[]{:S(2)}) %collective-permute-start.16) | collective-permute-done | bytes 229408 | tf_op jit(solution)/shard_map/ppermute | solution.py:63
  260.9 2.5 pad_maximum_fusion.3.x_ref
  265.5 3.8 convolution_convert_fusion.3.refs_0_
  269.5 2.4 fusion.129
  280.4 2.6 convolution_convert_fusion.5
  288.9 3.7 collective-permute-start.20
  298.4 2.4 collective-permute-start.25
  300.8 3.4 slice.371
  304.2 2.4 slice.368
  309.9 6.0 convolution_convert_fusion.1.refs_5_.refs_6_
  315.9 31.0 %feed.2 = (bf16[1632,640]{1,0:T(8,128)(2,1)}, f32[1632,640]{1,0:T(8,128)}, bf16[1632,640]{1,0:T(8,128)(2,1)}, bf16[1632,1024]{1,0:T(8,128)(2,1)}, bf16[1632,768]...) custom-call(bf16[1632,1024]{1,0:T(8,128)(2,1)} %bitcast.501, ...), custom_call_target="tpu_custom_call" | custom-call | flops 14973665280 | bytes 21233664 | tf_op jit(solution)/shard_map/feed/pallas_call | solution.py:359
  353.2 3.1 collective-permute-start.28
  356.3 31.5 %feed.3 = (bf16[1632,640]{1,0:T(8,128)(2,1)}, f32[1632,640]{1,0:T(8,128)}, bf16[1632,640]{1,0:T(8,128)(2,1)}, bf16[1632,1024]{1,0:T(8,128)(2,1)}, bf16[1632,768]...) custom-call(bf16[1632,1024]{1,0:T(8,128)(2,1)} %bitcast.502, ...), custom_call_target="tpu_custom_call", output_to_operand_aliasing={{0}: (9, {}), {1}: (10, {}), {2}: (11, {}), {3}: (12, {}), ... | custom-call | flops 14973665280 | bytes 21233664 | tf_op jit(solution)/shard_map/feed/pallas_call | solution.py:359
  392.7 5.3 collective-permute-done.29.refs_2_
  398.7 2.4 fusion.117
  404.1 5.1 weight_grad.4
  409.2 8.9 %weight_grad.5 = bf16[2048,640]{1,0:T(8,128)(2,1)S(1)} custom-call(bf16[1632,2048]{1,0:T(8,128)(2,1)} %get-tuple-element.126.refs_0_, bf16[1632,640]{1,0:T(8,128)(2,1)S(1)} %bitcast.514, f32[1632,640]{1,0:T(8,128)} %get-tuple-element.114.refs_3_.refs_2_), custom_call_target="tpu_custom_call" | custom-call | flops 4278190080 | bytes 8773632 | tf_op jit(solution)/shard_map/weight_grad/pallas_call | solution.py:416
  425.4 4.2 bitcast_convert_fusion
  433.4 4.5 multiply_reduce_fusion
  441.0 3.0 pad_maximum_fusion.refs_4_
  447.4 4.7 collective-permute-start.37
  452.1 2.4 collective-permute-start.38
  454.8 17.9 %weight_grad.6.refs_6_ = bf16[768,4096]{1,0:T(8,128)(2,1)} custom-call(bf16[1632,768]{1,0:T(8,128)(2,1)S(1)} %copy-done.12, bf16[1632,2048]{1,0:T(8,128)(2,1)} %get-tuple-element.118.refs_1_, bf16[1632,2048]{1,0:T(8,128)(2,1)} %get-tuple-element.119.refs_2_, bf16[4,4,32,1536]{3,2,1,0:T(8,128)(2,1)S(1)} %bitcast_add_fusion.1.refs_3_, ...), custom_call_target="tpu_custom_call" | custom-call | flops 10267656192 | bytes 15876096 | tf_op jit(solution)/shard_map/weight_grad/pallas_call | solution.py:416
  472.7 4.0 dynamic-slice_bitcast_fusion
  480.1 2.8 collective-permute-start.33
  484.5 14.3 %attend_back.2 = (bf16[2,816,1024]{2,1,0:T(8,128)(2,1)}, f32[2,816,256]{2,1,0:T(8,128)S(1)}, f32[2,816,256]{2,1,0:T(8,128)S(1)}) custom-call(s32[2]{0:T(128)S(1)} %fusion.114.refs_1_.refs_0_, bf16[2,816,1536]{2,1,0:T(8,128)(2,1)} %bitcast.491, bf16[2,816,1536]{2,1,0:T(8,128)(2,1)} %bitcast.492, bf16[2,816,1536]{2,1,0:T(8,128)(2,1)} %bitcast.493, ...), custom_call_target="tpu_custom_call" | custom-call | flops 6818365440 | bytes 12533760 | tf_op jit(solution)/shard_map/attend_back/pallas_call | solution.py:269
  498.8 3.9 collective-permute-done.34.refs_1_
  506.7 4.0 collective-permute-start.61
  513.1 8.7 %collective-permute-done.61 = bf16[32,1536]{1,0:T(8,128)(2,1)S(1)} collective-permute-done((bf16[32,1536]{1,0:T(8,128)(2,1)S(1)}, bf16[32,1536]{1,0:T(8,128)(2,1)S(1)}, u32[]{:S(2)}, u32[]{:S(2)}) %collective-permute-start.61) | collective-permute-done | bytes 98336 | tf_op jit(solution)/shard_map/ppermute | solution.py:63
  525.0 8.7 %all-to-all-start.1 = ((bf16[8,32,1024]{2,1,0:T(8,128)(2,1)}), bf16[8,32,1024]{2,1,0:T(8,128)(2,1)}, u32[]{:S(2)}, u32[]{:S(2)}) async-start(bf16[8,32,1024]{2,1,0:T(8,128)(2,1)} %bitcast.564), calls=%async_computation.2 | async-start | bytes 1048576 | tf_op jit(solution)/shard_map/all_to_all | solution.py:824
  535.5 3.5 bitcast_add_fusion.refs_9_
  544.4 14.2 %attend_back.3 = (bf16[2,816,1024]{2,1,0:T(8,128)(2,1)}, f32[2,816,256]{2,1,0:T(8,128)S(1)}, f32[2,816,256]{2,1,0:T(8,128)S(1)}) custom-call(s32[2]{0:T(128)S(1)} %fusion.114.refs_1_.refs_0_, bf16[2,816,1536]{2,1,0:T(8,128)(2,1)} %bitcast.494, bf16[2,816,1536]{2,1,0:T(8,128)(2,1)} %bitcast.495, ...), custom_call_target="tpu_custom_call", output_to_operand_aliasing={{0}: (6, {}), {1}: (7, {}), {2}: (8, {})} | custom-call | flops 6818365440 | bytes 12533760 | tf_op jit(solution)/shard_map/attend_back/pallas_call | solution.py:269
  562.5 5.9 fusion.8
  568.9 5.6 fusion.7
  575.3 2.6 pad_maximum_fusion.1
  581.5 7.4 %weight_grad.7 = bf16[768,1536]{1,0:T(8,128)(2,1)S(1)} custom-call(bf16[1632,768]{1,0:T(8,128)(2,1)S(1)} %copy-done.21, bf16[1632,1536]{1,0:T(8,128)(2,1)} %bitcast.548), custom_call_target="tpu_custom_call" | custom-call | flops 3850371072 | bytes 7520256 | tf_op jit(solution)/shard_map/weight_grad/pallas_call | solution.py:416
  589.0 2.4 collective-permute-start.44
  596.0 2.9 collective-permute-done.46
  609.6 5.0 collective-permute-done.56.refs_2_
  615.5 2.3 fusion.31
  618.7 2.9 collective-permute-start.58
  627.4 7.4 %collective-permute-done.58 = bf16[24,4096]{1,0:T(8,128)(2,1)S(1)} collective-permute-done((bf16[24,4096]{1,0:T(8,128)(2,1)S(1)}, bf16[24,4096]{1,0:T(8,128)(2,1)S(1)}, u32[]{:S(2)}, u32[]{:S(2)}) %collective-permute-start.58) | collective-permute-done | bytes 196640 | tf_op jit(solution)/shard_map/ppermute | solution.py:63
  637.8 2.6 collective-permute-start.52
  643.1 3.4 collective-permute-done.53
  (532 shorter events, 188.8 us)
Async XLA Ops:
  7.2 103.6 %all-gather.5.cloned.1.call-start = ((), (), s32[]{:S(2)}) async-start(), calls=%async_computation.5 | async-start | bytes 8785920 | tf_op jit(solution)/shard_map/all_gather | solution.py:657
  13.9 286.9 %all-gather.7.cloned.1.call-start = ((), (), s32[]{:S(2)}) async-start(), calls=%async_computation.6 | async-start | bytes 10543104 | tf_op jit(solution)/shard_map/all_gather | solution.py:664
  20.3 16.9 %collective-permute-start = (bf16[2,56,1024]{2,1,0:T(8,128)(2,1)S(1)}, bf16[2,56,1024]{2,1,0:T(8,128)(2,1)}, u32[]{:S(2)}, u32[]{:S(2)}) collective-permute-start(bf16[2,56,1024]{2,1,0:T(8,128)(2,1)S(1)} %pad_maximum_fusion.16), channel_id=1, source_target_pairs={{0,2},{1,3},{2,0},{3,1},{4,6},{5,7},{6,4},{7,5},{8,10},{9,11},{10,... | collective-permute-start | bytes 688136 | tf_op jit(solution)/shard_map/ppermute | solution.py:63
  23.4 26.9 %collective-permute-start.1 = (bf16[2,56,1024]{2,1,0:T(8,128)(2,1)S(1)}, bf16[2,56,1024]{2,1,0:T(8,128)(2,1)}, u32[]{:S(2)}, u32[]{:S(2)}) collective-permute-start(bf16[2,56,1024]{2,1,0:T(8,128)(2,1)S(1)} %pad_maximum_fusion.16), channel_id=1, source_target_pairs={{0,4},{1,5},{2,6},{3,7},{4,0},{5,1},{6,2},{7,3},{8,12},{9,13},{10,... | collective-permute-start | bytes 688136 | tf_op jit(solution)/shard_map/ppermute | solution.py:63
  26.0 24.3 %collective-permute-start.2 = (bf16[2,56,1024]{2,1,0:T(8,128)(2,1)S(1)}, bf16[2,56,1024]{2,1,0:T(8,128)(2,1)}, u32[]{:S(2)}, u32[]{:S(2)}) collective-permute-start(bf16[2,56,1024]{2,1,0:T(8,128)(2,1)S(1)} %pad_maximum_fusion.16), channel_id=1, source_target_pairs={{0,6},{1,7},{2,4},{3,5},{4,2},{5,3},{6,0},{7,1},{8,14},{9,15},{10,... | collective-permute-start | bytes 688136 | tf_op jit(solution)/shard_map/ppermute | solution.py:63
  27.4 147.7 %all-to-all-start = ((bf16[8,2,32,512]{3,1,2,0:T(2,128)(2,1)}), bf16[8,2,32,512]{3,1,2,0:T(2,128)(2,1)}, u32[]{:S(2)}, u32[]{:S(2)}) async-start(bf16[8,2,32,512]{3,1,2,0:T(2,128)(2,1)} %reshape.564), calls=%async_computation | async-start | bytes 1048576 | tf_op jit(solution)/shard_map/all_to_all | solution.py:668
  32.5 490.6 %reduce-scatter.5.cloned.1.call-start = ((), (), s32[]{:S(2)}) async-start(), calls=%async_computation.4 | async-start | bytes 3932160 | tf_op jit(solution)/shard_map/reduce_scatter | solution.py:741
  137.5 56.6 %collective-permute-start.4 = (bf16[4,112,1024]{2,1,0:T(8,128)(2,1)}, bf16[4,112,1024]{2,1,0:T(8,128)(2,1)}, u32[]{:S(2)}, u32[]{:S(2)}) collective-permute-start(bf16[4,112,1024]{2,1,0:T(8,128)(2,1)} %slice_bitcast_fusion.6), channel_id=1, source_target_pairs={{0,1},{1,0},{2,3},{3,2},{4,5},{5,4},{6,7},{7,6},{8,9},{9,8},{10,11... | collective-permute-start | bytes 2752520 | tf_op jit(solution)/shard_map/ppermute | solution.py:63
  138.1 24.8 %collective-permute-start.5 = (bf16[112,1024]{1,0:T(8,128)(2,1)S(1)}, bf16[112,1024]{1,0:T(8,128)(2,1)S(1)}, u32[]{:S(2)}, u32[]{:S(2)}) collective-permute-start(bf16[112,1024]{1,0:T(8,128)(2,1)S(1)} %bitcast.588), channel_id=1, source_target_pairs={{0,2},{1,3},{2,0},{3,1},{4,6},{5,7},{6,4},{7,5},{8,10},{9,11},{10,... | collective-permute-start | bytes 688136 | tf_op jit(solution)/shard_map/ppermute | solution.py:63
  141.6 21.4 %collective-permute-start.6 = (bf16[112,1024]{1,0:T(8,128)(2,1)S(1)}, bf16[112,1024]{1,0:T(8,128)(2,1)S(1)}, u32[]{:S(2)}, u32[]{:S(2)}) collective-permute-start(bf16[112,1024]{1,0:T(8,128)(2,1)S(1)} %bitcast.589), channel_id=1, source_target_pairs={{0,4},{1,5},{2,6},{3,7},{4,0},{5,1},{6,2},{7,3},{8,12},{9,13},{10,... | collective-permute-start | bytes 688136 | tf_op jit(solution)/shard_map/ppermute | solution.py:63
  145.6 27.1 %collective-permute-start.7 = (bf16[112,1024]{1,0:T(8,128)(2,1)S(1)}, bf16[112,1024]{1,0:T(8,128)(2,1)}, u32[]{:S(2)}, u32[]{:S(2)}) collective-permute-start(bf16[112,1024]{1,0:T(8,128)(2,1)S(1)} %bitcast.590), channel_id=1, source_target_pairs={{0,6},{1,7},{2,4},{3,5},{4,2},{5,3},{6,0},{7,1},{8,14},{9,15},{10,... | collective-permute-start | bytes 688136 | tf_op jit(solution)/shard_map/ppermute | solution.py:63
  175.1 67.2 %collective-permute-start.8 = (bf16[4,112,1024]{2,1,0:T(8,128)(2,1)}, bf16[4,112,1024]{2,1,0:T(8,128)(2,1)}, u32[]{:S(2)}, u32[]{:S(2)}) collective-permute-start(bf16[4,112,1024]{2,1,0:T(8,128)(2,1)} %get-tuple-element.303), channel_id=1, source_target_pairs={{0,1},{1,0},{2,3},{3,2},{4,5},{5,4},{6,7},{7,6},{8,9},{9,8},{10,11... | collective-permute-start | bytes 2752520 | tf_op jit(solution)/shard_map/ppermute | solution.py:63
  177.8 83.0 %collective-permute-start.9 = (bf16[384,1024]{1,0:T(8,128)(2,1)}, bf16[384,1024]{1,0:T(8,128)(2,1)}, u32[]{:S(2)}, u32[]{:S(2)}) collective-permute-start(bf16[384,1024]{1,0:T(8,128)(2,1)} %constant_dynamic-update-slice_fusion), channel_id=1, source_target_pairs={{0,8},{8,0},{16,24},{24,16},{1,9},{9,1},{17,25},{25,17},{2,10},{10... | collective-permute-start | bytes 2359304 | tf_op jit(solution)/shard_map/ppermute | solution.py:63
  195.5 20.8 %collective-permute-start.12 = (bf16[112,1024]{1,0:T(8,128)(2,1)S(1)}, bf16[112,1024]{1,0:T(8,128)(2,1)S(1)}, u32[]{:S(2)}, u32[]{:S(2)}) collective-permute-start(bf16[112,1024]{1,0:T(8,128)(2,1)S(1)} %get-tuple-element.301), channel_id=1, source_target_pairs={{0,2},{1,3},{2,0},{3,1},{4,6},{5,7},{6,4},{7,5},{8,10},{9,11},{10,... | collective-permute-start | bytes 688136 | tf_op jit(solution)/shard_map/ppermute | solution.py:63
  200.3 17.1 %collective-permute-start.13 = (bf16[112,1024]{1,0:T(8,128)(2,1)S(1)}, bf16[112,1024]{1,0:T(8,128)(2,1)S(1)}, u32[]{:S(2)}, u32[]{:S(2)}) collective-permute-start(bf16[112,1024]{1,0:T(8,128)(2,1)S(1)} %get-tuple-element.300), channel_id=1, source_target_pairs={{0,4},{1,5},{2,6},{3,7},{4,0},{5,1},{6,2},{7,3},{8,12},{9,13},{10,... | collective-permute-start | bytes 688136 | tf_op jit(solution)/shard_map/ppermute | solution.py:63
  201.7 23.9 %collective-permute-start.14 = (bf16[112,1024]{1,0:T(8,128)(2,1)S(1)}, bf16[112,1024]{1,0:T(8,128)(2,1)S(1)}, u32[]{:S(2)}, u32[]{:S(2)}) collective-permute-start(bf16[112,1024]{1,0:T(8,128)(2,1)S(1)} %get-tuple-element.299), channel_id=1, source_target_pairs={{0,6},{1,7},{2,4},{3,5},{4,2},{5,3},{6,0},{7,1},{8,14},{9,15},{10,... | collective-permute-start | bytes 688136 | tf_op jit(solution)/shard_map/ppermute | solution.py:63
  216.3 44.6 %collective-permute-start.10 = (bf16[384,1024]{1,0:T(8,128)(2,1)}, bf16[384,1024]{1,0:T(8,128)(2,1)}, u32[]{:S(2)}, u32[]{:S(2)}) collective-permute-start(bf16[384,1024]{1,0:T(8,128)(2,1)} %constant_dynamic-update-slice_fusion), channel_id=1, source_target_pairs={{0,16},{8,24},{16,0},{24,8},{1,17},{9,25},{17,1},{25,9},{2,18},{10... | collective-permute-start | bytes 2359304 | tf_op jit(solution)/shard_map/ppermute | solution.py:63
  217.5 43.4 %collective-permute-start.11 = (bf16[384,1024]{1,0:T(8,128)(2,1)}, bf16[384,1024]{1,0:T(8,128)(2,1)}, u32[]{:S(2)}, u32[]{:S(2)}) collective-permute-start(bf16[384,1024]{1,0:T(8,128)(2,1)} %constant_dynamic-update-slice_fusion), channel_id=1, source_target_pairs={{0,24},{8,16},{16,8},{24,0},{1,25},{9,17},{17,9},{25,1},{2,26},{10... | collective-permute-start | bytes 2359304 | tf_op jit(solution)/shard_map/ppermute | solution.py:63
  230.5 17.6 %collective-permute-start.15 = (bf16[112,1024]{1,0:T(8,128)(2,1)S(1)}, bf16[112,1024]{1,0:T(8,128)(2,1)S(1)}, u32[]{:S(2)}, u32[]{:S(2)}) collective-permute-start(bf16[112,1024]{1,0:T(8,128)(2,1)S(1)} %bitcast.594), channel_id=1, source_target_pairs={{0,2},{1,3},{2,0},{3,1},{4,6},{5,7},{6,4},{7,5},{8,10},{9,11},{10,... | collective-permute-start | bytes 688136 | tf_op jit(solution)/shard_map/ppermute | solution.py:63
  242.3 18.4 %collective-permute-start.16 = (bf16[112,1024]{1,0:T(8,128)(2,1)S(1)}, bf16[112,1024]{1,0:T(8,128)(2,1)S(1)}, u32[]{:S(2)}, u32[]{:S(2)}) collective-permute-start(bf16[112,1024]{1,0:T(8,128)(2,1)S(1)} %bitcast.595), channel_id=1, source_target_pairs={{0,4},{1,5},{2,6},{3,7},{4,0},{5,1},{6,2},{7,3},{8,12},{9,13},{10,... | collective-permute-start | bytes 688136 | tf_op jit(solution)/shard_map/ppermute | solution.py:63
  248.2 12.5 %collective-permute-start.17 = (bf16[112,1024]{1,0:T(8,128)(2,1)S(1)}, bf16[112,1024]{1,0:T(8,128)(2,1)S(1)}, u32[]{:S(2)}, u32[]{:S(2)}) collective-permute-start(bf16[112,1024]{1,0:T(8,128)(2,1)S(1)} %bitcast.596), channel_id=1, source_target_pairs={{0,6},{1,7},{2,4},{3,5},{4,2},{5,3},{6,0},{7,1},{8,14},{9,15},{10,... | collective-permute-start | bytes 688136 | tf_op jit(solution)/shard_map/ppermute | solution.py:63
  260.8 8.5 %collective-permute-start.18 = (bf16[4,112,1024]{2,1,0:T(8,128)(2,1)S(1)}, bf16[4,112,1024]{2,1,0:T(8,128)(2,1)S(1)}, u32[]{:S(2)}, u32[]{:S(2)}) collective-permute-start(bf16[4,112,1024]{2,1,0:T(8,128)(2,1)S(1)} %get-tuple-element.298), channel_id=1, source_target_pairs={{0,1},{1,0},{2,3},{3,2},{4,5},{5,4},{6,7},{7,6},{8,9},{9,8},{10,11... | collective-permute-start | bytes 2752520 | tf_op jit(solution)/shard_map/ppermute | solution.py:63
  277.2 9.1 %collective-permute-start.19 = (bf16[4,112,1024]{2,1,0:T(8,128)(2,1)}, bf16[4,112,1024]{2,1,0:T(8,128)(2,1)}, u32[]{:S(2)}, u32[]{:S(2)}) collective-permute-start(bf16[4,112,1024]{2,1,0:T(8,128)(2,1)} %slice_bitcast_fusion.4), channel_id=1, source_target_pairs={{0,1},{1,0},{2,3},{3,2},{4,5},{5,4},{6,7},{7,6},{8,9},{9,8},{10,11... | collective-permute-start | bytes 2752520 | tf_op jit(solution)/shard_map/ppermute | solution.py:63
  279.9 15.6 %collective-permute-start.23 = (bf16[4,112,1024]{2,1,0:T(8,128)(2,1)}, bf16[4,112,1024]{2,1,0:T(8,128)(2,1)}, u32[]{:S(2)}, u32[]{:S(2)}) collective-permute-start(bf16[4,112,1024]{2,1,0:T(8,128)(2,1)} %slice_bitcast_fusion.2), channel_id=1, source_target_pairs={{0,1},{1,0},{2,3},{3,2},{4,5},{5,4},{6,7},{7,6},{8,9},{9,8},{10,11... | collective-permute-start | bytes 2752520 | tf_op jit(solution)/shard_map/ppermute | solution.py:63
  286.3 361.6 %reduce-scatter.7.cloned.1.call-start = ((), (), s32[]{:S(2)}) async-start(), calls=%async_computation.7 | async-start | bytes 6285312
  288.9 58.0 %collective-permute-start.20 = (bf16[112,1024]{1,0:T(8,128)(2,1)}, bf16[112,1024]{1,0:T(8,128)(2,1)S(1)}, u32[]{:S(2)}, u32[]{:S(2)}) collective-permute-start(bf16[112,1024]{1,0:T(8,128)(2,1)} %get-tuple-element.296), channel_id=1, source_target_pairs={{0,2},{1,3},{2,0},{3,1},{4,6},{5,7},{6,4},{7,5},{8,10},{9,11},{10,... | collective-permute-start | bytes 688136 | tf_op jit(solution)/shard_map/ppermute | solution.py:63
  292.6 55.7 %collective-permute-start.21 = (bf16[112,1024]{1,0:T(8,128)(2,1)}, bf16[112,1024]{1,0:T(8,128)(2,1)S(1)}, u32[]{:S(2)}, u32[]{:S(2)}) collective-permute-start(bf16[112,1024]{1,0:T(8,128)(2,1)} %get-tuple-element.295), channel_id=1, source_target_pairs={{0,4},{1,5},{2,6},{3,7},{4,0},{5,1},{6,2},{7,3},{8,12},{9,13},{10,... | collective-permute-start | bytes 688136 | tf_op jit(solution)/shard_map/ppermute | solution.py:63
  294.1 54.2 %collective-permute-start.22 = (bf16[112,1024]{1,0:T(8,128)(2,1)}, bf16[112,1024]{1,0:T(8,128)(2,1)}, u32[]{:S(2)}, u32[]{:S(2)}) collective-permute-start(bf16[112,1024]{1,0:T(8,128)(2,1)} %get-tuple-element.294), channel_id=1, source_target_pairs={{0,6},{1,7},{2,4},{3,5},{4,2},{5,3},{6,0},{7,1},{8,14},{9,15},{10,... | collective-permute-start | bytes 688136 | tf_op jit(solution)/shard_map/ppermute | solution.py:63
  297.7 92.4 %collective-permute-start.24 = (bf16[112,1024]{1,0:T(8,128)(2,1)}, bf16[112,1024]{1,0:T(8,128)(2,1)S(1)}, u32[]{:S(2)}, u32[]{:S(2)}) collective-permute-start(bf16[112,1024]{1,0:T(8,128)(2,1)} %get-tuple-element.291), channel_id=1, source_target_pairs={{0,2},{1,3},{2,0},{3,1},{4,6},{5,7},{6,4},{7,5},{8,10},{9,11},{10,... | collective-permute-start | bytes 688136 | tf_op jit(solution)/shard_map/ppermute | solution.py:63
  298.4 93.0 %collective-permute-start.25 = (bf16[112,1024]{1,0:T(8,128)(2,1)}, bf16[112,1024]{1,0:T(8,128)(2,1)}, u32[]{:S(2)}, u32[]{:S(2)}) collective-permute-start(bf16[112,1024]{1,0:T(8,128)(2,1)} %get-tuple-element.293), channel_id=1, source_target_pairs={{0,4},{1,5},{2,6},{3,7},{4,0},{5,1},{6,2},{7,3},{8,12},{9,13},{10,... | collective-permute-start | bytes 688136 | tf_op jit(solution)/shard_map/ppermute | solution.py:63
  346.9 44.6 %collective-permute-start.26 = (bf16[112,1024]{1,0:T(8,128)(2,1)}, bf16[112,1024]{1,0:T(8,128)(2,1)}, u32[]{:S(2)}, u32[]{:S(2)}) collective-permute-start(bf16[112,1024]{1,0:T(8,128)(2,1)} %get-tuple-element.292), channel_id=1, source_target_pairs={{0,6},{1,7},{2,4},{3,5},{4,2},{5,3},{6,0},{7,1},{8,14},{9,15},{10,... | collective-permute-start | bytes 688136 | tf_op jit(solution)/shard_map/ppermute | solution.py:63
  353.2 39.5 %collective-permute-start.27 = (bf16[112,1024]{1,0:T(8,128)(2,1)S(1)}, bf16[112,1024]{1,0:T(8,128)(2,1)S(1)}, u32[]{:S(2)}, u32[]{:S(2)}) collective-permute-start(bf16[112,1024]{1,0:T(8,128)(2,1)S(1)} %convolution_convert_fusion.10.refs_17_), channel_id=1, source_target_pairs={{0,2},{1,3},{2,0},{3,1},{4,6},{5,7},{6,4},{7,5},{8,10},{9,11},{10,... | collective-permute-start | bytes 688136 | tf_op jit(solution)/shard_map/ppermute | solution.py:63
  353.2 39.4 %collective-permute-start.28 = (bf16[112,1024]{1,0:T(8,128)(2,1)S(1)}, bf16[112,1024]{1,0:T(8,128)(2,1)S(1)}, u32[]{:S(2)}, u32[]{:S(2)}) collective-permute-start(bf16[112,1024]{1,0:T(8,128)(2,1)S(1)} %convolution_convert_fusion.10.refs_17_), channel_id=1, source_target_pairs={{0,4},{1,5},{2,6},{3,7},{4,0},{5,1},{6,2},{7,3},{8,12},{9,13},{10,... | collective-permute-start | bytes 688136 | tf_op jit(solution)/shard_map/ppermute | solution.py:63
  390.1 7.9 %collective-permute-start.29 = (bf16[112,1024]{1,0:T(8,128)(2,1)S(1)}, bf16[112,1024]{1,0:T(8,128)(2,1)S(1)}, u32[]{:S(2)}, u32[]{:S(2)}) collective-permute-start(bf16[112,1024]{1,0:T(8,128)(2,1)S(1)} %copy-done.51), channel_id=1, source_target_pairs={{0,6},{1,7},{2,4},{3,5},{4,2},{5,3},{6,0},{7,1},{8,14},{9,15},{10,... | collective-permute-start | bytes 688136 | tf_op jit(solution)/shard_map/ppermute | solution.py:63
  401.1 19.3 %collective-permute-start.30 = (bf16[4,112,1024]{2,1,0:T(8,128)(2,1)}, bf16[4,112,1024]{2,1,0:T(8,128)(2,1)}, u32[]{:S(2)}, u32[]{:S(2)}) collective-permute-start(bf16[4,112,1024]{2,1,0:T(8,128)(2,1)} %get-tuple-element.290), channel_id=1, source_target_pairs={{0,1},{1,0},{2,3},{3,2},{4,5},{5,4},{6,7},{7,6},{8,9},{9,8},{10,11... | collective-permute-start | bytes 2752520 | tf_op jit(solution)/shard_map/ppermute | solution.py:63
  431.8 22.8 %collective-permute-start.31 = (bf16[4,4,32,1536]{3,2,1,0:T(8,128)(2,1)}, bf16[4,4,32,1536]{3,2,1,0:T(8,128)(2,1)S(1)}, u32[]{:S(2)}, u32[]{:S(2)}) collective-permute-start(bf16[4,4,32,1536]{3,2,1,0:T(8,128)(2,1)} %dynamic-slice_bitcast_fusion.1), channel_id=1, source_target_pairs={{0,1},{1,0},{2,3},{3,2},{4,5},{5,4},{6,7},{7,6},{8,9},{9,8},{10,11... | collective-permute-start | bytes 4718600 | tf_op jit(solution)/shard_map/ppermute | solution.py:63
  447.4 30.4 %collective-permute-start.37 = (bf16[112,1024]{1,0:T(8,128)(2,1)}, bf16[112,1024]{1,0:T(8,128)(2,1)}, u32[]{:S(2)}, u32[]{:S(2)}) collective-permute-start(bf16[112,1024]{1,0:T(8,128)(2,1)} %get-tuple-element.286), channel_id=1, source_target_pairs={{0,2},{1,3},{2,0},{3,1},{4,6},{5,7},{6,4},{7,5},{8,10},{9,11},{10,... | collective-permute-start | bytes 688136 | tf_op jit(solution)/shard_map/ppermute | solution.py:63
  452.1 25.7 %collective-permute-start.38 = (bf16[112,1024]{1,0:T(8,128)(2,1)}, bf16[112,1024]{1,0:T(8,128)(2,1)}, u32[]{:S(2)}, u32[]{:S(2)}) collective-permute-start(bf16[112,1024]{1,0:T(8,128)(2,1)} %get-tuple-element.288), channel_id=1, source_target_pairs={{0,4},{1,5},{2,6},{3,7},{4,0},{5,1},{6,2},{7,3},{8,12},{9,13},{10,... | collective-permute-start | bytes 688136 | tf_op jit(solution)/shard_map/ppermute | solution.py:63
  454.5 23.3 %collective-permute-start.39 = (bf16[112,1024]{1,0:T(8,128)(2,1)}, bf16[112,1024]{1,0:T(8,128)(2,1)}, u32[]{:S(2)}, u32[]{:S(2)}) collective-permute-start(bf16[112,1024]{1,0:T(8,128)(2,1)} %get-tuple-element.287), channel_id=1, source_target_pairs={{0,6},{1,7},{2,4},{3,5},{4,2},{5,3},{6,0},{7,1},{8,14},{9,15},{10,... | collective-permute-start | bytes 688136 | tf_op jit(solution)/shard_map/ppermute | solution.py:63
  476.7 58.8 %collective-permute-start.32 = (bf16[4,4,24,4096]{3,2,1,0:T(8,128)(2,1)}, bf16[4,4,24,4096]{3,2,1,0:T(8,128)(2,1)}, u32[]{:S(2)}, u32[]{:S(2)}) collective-permute-start(bf16[4,4,24,4096]{3,2,1,0:T(8,128)(2,1)} %dynamic-slice_bitcast_fusion), channel_id=1, source_target_pairs={{0,1},{1,0},{2,3},{3,2},{4,5},{5,4},{6,7},{7,6},{8,9},{9,8},{10,11... | collective-permute-start | bytes 9437192 | tf_op jit(solution)/shard_map/ppermute | solution.py:63
  480.1 18.7 %collective-permute-start.33 = (bf16[4,32,1536]{2,1,0:T(8,128)(2,1)S(1)}, bf16[4,32,1536]{2,1,0:T(8,128)(2,1)}, u32[]{:S(2)}, u32[]{:S(2)}) collective-permute-start(bf16[4,32,1536]{2,1,0:T(8,128)(2,1)S(1)} %get-tuple-element.282), channel_id=1, source_target_pairs={{0,8},{8,0},{16,24},{24,16},{1,9},{9,1},{17,25},{25,17},{2,10},{10... | collective-permute-start | bytes 1179656 | tf_op jit(solution)/shard_map/ppermute | solution.py:63
  483.0 19.7 %collective-permute-start.34 = (bf16[4,32,1536]{2,1,0:T(8,128)(2,1)S(1)}, bf16[4,32,1536]{2,1,0:T(8,128)(2,1)}, u32[]{:S(2)}, u32[]{:S(2)}) collective-permute-start(bf16[4,32,1536]{2,1,0:T(8,128)(2,1)S(1)} %get-tuple-element.281), channel_id=1, source_target_pairs={{0,16},{8,24},{16,0},{24,8},{1,17},{9,25},{17,1},{25,9},{2,18},{10... | collective-permute-start | bytes 1179656 | tf_op jit(solution)/shard_map/ppermute | solution.py:63
  484.0 20.2 %collective-permute-start.35 = (bf16[4,32,1536]{2,1,0:T(8,128)(2,1)S(1)}, bf16[4,32,1536]{2,1,0:T(8,128)(2,1)}, u32[]{:S(2)}, u32[]{:S(2)}) collective-permute-start(bf16[4,32,1536]{2,1,0:T(8,128)(2,1)S(1)} %get-tuple-element.280), channel_id=1, source_target_pairs={{0,24},{8,16},{16,8},{24,0},{1,25},{9,17},{17,9},{25,1},{2,26},{10... | collective-permute-start | bytes 1179656 | tf_op jit(solution)/shard_map/ppermute | solution.py:63
  505.9 7.2 %collective-permute-start.60 = (bf16[32,1536]{1,0:T(8,128)(2,1)S(1)}, bf16[32,1536]{1,0:T(8,128)(2,1)S(1)}, u32[]{:S(2)}, u32[]{:S(2)}) collective-permute-start(bf16[32,1536]{1,0:T(8,128)(2,1)S(1)} %get-tuple-element.311), channel_id=1, source_target_pairs={{0,2},{1,3},{2,0},{3,1},{4,6},{5,7},{6,4},{7,5},{8,10},{9,11},{10,... | collective-permute-start | bytes 294920 | tf_op jit(solution)/shard_map/ppermute | solution.py:63
  506.7 15.1 %collective-permute-start.61 = (bf16[32,1536]{1,0:T(8,128)(2,1)S(1)}, bf16[32,1536]{1,0:T(8,128)(2,1)S(1)}, u32[]{:S(2)}, u32[]{:S(2)}) collective-permute-start(bf16[32,1536]{1,0:T(8,128)(2,1)S(1)} %get-tuple-element.313), channel_id=1, source_target_pairs={{0,4},{1,5},{2,6},{3,7},{4,0},{5,1},{6,2},{7,3},{8,12},{9,13},{10,... | collective-permute-start | bytes 294920 | tf_op jit(solution)/shard_map/ppermute | solution.py:63
  510.7 11.1 %collective-permute-start.62 = (bf16[32,1536]{1,0:T(8,128)(2,1)S(1)}, bf16[32,1536]{1,0:T(8,128)(2,1)S(1)}, u32[]{:S(2)}, u32[]{:S(2)}) collective-permute-start(bf16[32,1536]{1,0:T(8,128)(2,1)S(1)} %get-tuple-element.312), channel_id=1, source_target_pairs={{0,6},{1,7},{2,4},{3,5},{4,2},{5,3},{6,0},{7,1},{8,14},{9,15},{10,... | collective-permute-start | bytes 294920 | tf_op jit(solution)/shard_map/ppermute | solution.py:63
  525.0 75.8 %all-to-all-start.1 = ((bf16[8,32,1024]{2,1,0:T(8,128)(2,1)}), bf16[8,32,1024]{2,1,0:T(8,128)(2,1)}, u32[]{:S(2)}, u32[]{:S(2)}) async-start(bf16[8,32,1024]{2,1,0:T(8,128)(2,1)} %bitcast.564), calls=%async_computation.2 | async-start | bytes 1048576 | tf_op jit(solution)/shard_map/all_to_all | solution.py:824
  540.5 69.1 %collective-permute-start.54 = (bf16[4,24,4096]{2,1,0:T(8,128)(2,1)}, bf16[4,24,4096]{2,1,0:T(8,128)(2,1)}, u32[]{:S(2)}, u32[]{:S(2)}) collective-permute-start(bf16[4,24,4096]{2,1,0:T(8,128)(2,1)} %get-tuple-element.277), channel_id=1, source_target_pairs={{0,8},{8,0},{16,24},{24,16},{1,9},{9,1},{17,25},{25,17},{2,10},{10... | collective-permute-start | bytes 2359304 | tf_op jit(solution)/shard_map/ppermute | solution.py:63
  542.1 67.5 %collective-permute-start.55 = (bf16[4,24,4096]{2,1,0:T(8,128)(2,1)}, bf16[4,24,4096]{2,1,0:T(8,128)(2,1)}, u32[]{:S(2)}, u32[]{:S(2)}) collective-permute-start(bf16[4,24,4096]{2,1,0:T(8,128)(2,1)} %get-tuple-element.276), channel_id=1, source_target_pairs={{0,16},{8,24},{16,0},{24,8},{1,17},{9,25},{17,1},{25,9},{2,18},{10... | collective-permute-start | bytes 2359304 | tf_op jit(solution)/shard_map/ppermute | solution.py:63
  568.7 9.2 %collective-permute-start.40 = (f32[4,4,9,128]{3,2,1,0:T(8,128)S(1)}, f32[4,4,9,128]{3,2,1,0:T(8,128)S(1)}, u32[]{:S(2)}, u32[]{:S(2)}) collective-permute-start(f32[4,4,9,128]{3,2,1,0:T(8,128)S(1)} %dynamic-slice_bitcast_fusion.15), channel_id=1, source_target_pairs={{0,1},{1,0},{2,3},{3,2},{4,5},{5,4},{6,7},{7,6},{8,9},{9,8},{10,11... | collective-permute-start | bytes 221192 | tf_op jit(solution)/shard_map/ppermute | solution.py:63
  577.9 11.0 %collective-permute-start.41 = (f32[4,9,128]{2,1,0:T(8,128)S(1)}, f32[4,9,128]{2,1,0:T(8,128)S(1)}, u32[]{:S(2)}, u32[]{:S(2)}) collective-permute-start(f32[4,9,128]{2,1,0:T(8,128)S(1)} %get-tuple-element.323), channel_id=1, source_target_pairs={{0,8},{8,0},{16,24},{24,16},{1,9},{9,1},{17,25},{25,17},{2,10},{10... | collective-permute-start | bytes 55304 | tf_op jit(solution)/shard_map/ppermute | solution.py:63
  578.2 10.7 %collective-permute-start.42 = (f32[4,9,128]{2,1,0:T(8,128)S(1)}, f32[4,9,128]{2,1,0:T(8,128)S(1)}, u32[]{:S(2)}, u32[]{:S(2)}) collective-permute-start(f32[4,9,128]{2,1,0:T(8,128)S(1)} %get-tuple-element.325), channel_id=1, source_target_pairs={{0,16},{8,24},{16,0},{24,8},{1,17},{9,25},{17,1},{25,9},{2,18},{10... | collective-permute-start | bytes 55304 | tf_op jit(solution)/shard_map/ppermute | solution.py:63
  579.4 9.6 %collective-permute-start.43 = (f32[4,9,128]{2,1,0:T(8,128)S(1)}, f32[4,9,128]{2,1,0:T(8,128)S(1)}, u32[]{:S(2)}, u32[]{:S(2)}) collective-permute-start(f32[4,9,128]{2,1,0:T(8,128)S(1)} %get-tuple-element.324), channel_id=1, source_target_pairs={{0,24},{8,16},{16,8},{24,0},{1,25},{9,17},{17,9},{25,1},{2,26},{10... | collective-permute-start | bytes 55304 | tf_op jit(solution)/shard_map/ppermute | solution.py:63
  589.0 6.0 collective-permute-start.44
  595.0 19.6 %collective-permute-start.56 = (bf16[4,24,4096]{2,1,0:T(8,128)(2,1)}, bf16[4,24,4096]{2,1,0:T(8,128)(2,1)S(1)}, u32[]{:S(2)}, u32[]{:S(2)}) collective-permute-start(bf16[4,24,4096]{2,1,0:T(8,128)(2,1)} %get-tuple-element.275), channel_id=1, source_target_pairs={{0,24},{8,16},{16,8},{24,0},{1,25},{9,17},{17,9},{25,1},{2,26},{10... | collective-permute-start | bytes 2359304 | tf_op jit(solution)/shard_map/ppermute | solution.py:63
  596.0 26.3 %collective-permute-start.47 = (bf16[4,4,24,1536]{3,2,1,0:T(8,128)(2,1)}, bf16[4,4,24,1536]{3,2,1,0:T(8,128)(2,1)}, u32[]{:S(2)}, u32[]{:S(2)}) collective-permute-start(bf16[4,4,24,1536]{3,2,1,0:T(8,128)(2,1)} %dynamic-slice_bitcast_fusion.2), channel_id=1, source_target_pairs={{0,1},{1,0},{2,3},{3,2},{4,5},{5,4},{6,7},{7,6},{8,9},{9,8},{10,11... | collective-permute-start | bytes 3538952 | tf_op jit(solution)/shard_map/ppermute | solution.py:63
  617.8 8.3 %collective-permute-start.57 = (bf16[24,4096]{1,0:T(8,128)(2,1)S(1)}, bf16[24,4096]{1,0:T(8,128)(2,1)S(1)}, u32[]{:S(2)}, u32[]{:S(2)}) collective-permute-start(bf16[24,4096]{1,0:T(8,128)(2,1)S(1)} %get-tuple-element.306), channel_id=1, source_target_pairs={{0,2},{1,3},{2,0},{3,1},{4,6},{5,7},{6,4},{7,5},{8,10},{9,11},{10,... | collective-permute-start | bytes 589832 | tf_op jit(solution)/shard_map/ppermute | solution.py:63
  618.7 16.1 %collective-permute-start.58 = (bf16[24,4096]{1,0:T(8,128)(2,1)S(1)}, bf16[24,4096]{1,0:T(8,128)(2,1)S(1)}, u32[]{:S(2)}, u32[]{:S(2)}) collective-permute-start(bf16[24,4096]{1,0:T(8,128)(2,1)S(1)} %get-tuple-element.308), channel_id=1, source_target_pairs={{0,4},{1,5},{2,6},{3,7},{4,0},{5,1},{6,2},{7,3},{8,12},{9,13},{10,... | collective-permute-start | bytes 589832 | tf_op jit(solution)/shard_map/ppermute | solution.py:63
  621.5 13.2 %collective-permute-start.59 = (bf16[24,4096]{1,0:T(8,128)(2,1)S(1)}, bf16[24,4096]{1,0:T(8,128)(2,1)S(1)}, u32[]{:S(2)}, u32[]{:S(2)}) collective-permute-start(bf16[24,4096]{1,0:T(8,128)(2,1)S(1)} %get-tuple-element.307), channel_id=1, source_target_pairs={{0,6},{1,7},{2,4},{3,5},{4,2},{5,3},{6,0},{7,1},{8,14},{9,15},{10,... | collective-permute-start | bytes 589832 | tf_op jit(solution)/shard_map/ppermute | solution.py:63
  623.8 11.0 %collective-permute-start.48 = (bf16[4,24,1536]{2,1,0:T(8,128)(2,1)S(1)}, bf16[4,24,1536]{2,1,0:T(8,128)(2,1)S(1)}, u32[]{:S(2)}, u32[]{:S(2)}) collective-permute-start(bf16[4,24,1536]{2,1,0:T(8,128)(2,1)S(1)} %get-tuple-element.283), channel_id=1, source_target_pairs={{0,8},{8,0},{16,24},{24,16},{1,9},{9,1},{17,25},{25,17},{2,10},{10... | collective-permute-start | bytes 884744 | tf_op jit(solution)/shard_map/ppermute | solution.py:63
  624.2 12.7 %collective-permute-start.49 = (bf16[4,24,1536]{2,1,0:T(8,128)(2,1)S(1)}, bf16[4,24,1536]{2,1,0:T(8,128)(2,1)S(1)}, u32[]{:S(2)}, u32[]{:S(2)}) collective-permute-start(bf16[4,24,1536]{2,1,0:T(8,128)(2,1)S(1)} %get-tuple-element.285), channel_id=1, source_target_pairs={{0,16},{8,24},{16,0},{24,8},{1,17},{9,25},{17,1},{25,9},{2,18},{10... | collective-permute-start | bytes 884744 | tf_op jit(solution)/shard_map/ppermute | solution.py:63
  626.2 10.8 %collective-permute-start.50 = (bf16[4,24,1536]{2,1,0:T(8,128)(2,1)S(1)}, bf16[4,24,1536]{2,1,0:T(8,128)(2,1)S(1)}, u32[]{:S(2)}, u32[]{:S(2)}) collective-permute-start(bf16[4,24,1536]{2,1,0:T(8,128)(2,1)S(1)} %get-tuple-element.284), channel_id=1, source_target_pairs={{0,24},{8,16},{16,8},{24,0},{1,25},{9,17},{17,9},{25,1},{2,26},{10... | collective-permute-start | bytes 884744 | tf_op jit(solution)/shard_map/ppermute | solution.py:63
  637.1 6.0 collective-permute-start.51
  640.4 6.2 collective-permute-start.53
  (119 other events, 1260.1 us)
Sparse Core Ops, SparseCore 0:
  14.1 96.6 all-gather.4
  114.4 123.0 all-gather.6
  286.4 45.6 reduce-scatter.4
  444.2 131.6 reduce-scatter.6

commit v3 on v2

--- a/solution.py
+++ b/solution.py
@@ -84,35 +84,88 @@
         return sum((part.astype(F32) for part in parts), x[0].astype(F32))
 
 
+def joint(jobs, *gate):
+    return list(after([line.across(x, mask) for line, x, mask in jobs], *gate))
+
+
+def fetch(x, rows, dp, line, beside):
+    far, count = line.count // 2, dp.count
+    *got, more = joint([(line, x, k << 1) for k in range(1, far)] + [(line, rows, 2)])
+    near = jnp.stack([x] + got)
+    rows = jnp.stack([rows, more])
+    jobs = [(dp, near, k) for k in range(1, count)]
+    for bit in range(2, far.bit_length()):
+        more = line.across(rows, 1 << bit)
+        if bit + 1 < far.bit_length():
+            rows = jnp.concatenate([rows, more])
+    done = beside(near)
+    got = [line.across(x, mask) for line, x, mask in jobs]
+    *got, more, done = after(got + [more, done])
+    same = jnp.stack([near] + got)
+    rows = jnp.concatenate([rows, more])
+    other, more = joint([(line, same, 1), (line, rows, 1)])
+    rows = jnp.stack([rows, more], axis=1).reshape((line.count,) + rows.shape[1:])
+
+    def kernel(me_ref, same_ref, other_ref, out_ref):
+        for kd in range(count):
+            for kz in range(far):
+                at = (me_ref[0] ^ kd) * line.count + (me_ref[1] ^ (2 * kz))
+                out_ref[at] = same_ref[kd, kz]
+                out_ref[at ^ 1] = other_ref[kd, kz]
+
+    def whole(a):
+        return pl.BlockSpec(a, lambda i, me: (0,) * len(a), pipeline_mode=pl.Buffered(1))
+
+    shape = (count * line.count,) + x.shape
+    me = jnp.stack([dp.me, line.me]).astype(jnp.int32)
+    return pl.pallas_call(
+        kernel,
+        grid_spec=pltpu.PrefetchScalarGridSpec(
+            num_scalar_prefetch=1,
+            grid=(1,),
+            in_specs=[whole(same.shape)] * 2,
+            out_specs=whole(shape),
+        ),
+        out_shape=jax.ShapeDtypeStruct(shape, x.dtype),
+        compiler_params=params(48, 1),
+        name="settle",
+    )(me, same, other), rows, done
+
+
 class Sum:
     def __init__(self, x, dp, line):
         self.x, self.dp, self.line = x, dp, line
         self.rest = x.shape[1:]
+        self.bits = list(range(1, line.count.bit_length() - 1))
+
+    def half(self, lead, bit, tail):
+        x = self.x.reshape(lead + (2,) + tail + self.rest)
+        mine = (self.line.me >> bit) & 1
+        self.x = lax.dynamic_index_in_dim(x, mine, len(lead), keepdims=False)
+        send = lax.dynamic_index_in_dim(x, 1 - mine, len(lead), keepdims=False)
+        return [(self.line, send, 1 << bit)]
 
     def cores(self):
-        x = self.x.reshape((self.dp.count, self.line.count // 2, 2) + self.rest)
-        mine = self.line.me % 2
-        keep = lax.dynamic_index_in_dim(x, mine, 2, keepdims=False)
-        send = lax.dynamic_index_in_dim(x, 1 - mine, 2, keepdims=False)
-        self.x = keep + self.line.swap(send, 0)
-        return self
-
-    def all_pairs(self, line, me, count, shift, gate):
-        mine = lax.dynamic_index_in_dim(self.x, me, 0, keepdims=False).astype(F32)
-        parts = []
-        for k in range(1, count):
-            part = lax.dynamic_index_in_dim(self.x, me ^ k, 0, keepdims=False)
-            parts.append(line.across(part, k << shift))
-        if gate:
-            parts = after(parts, *gate)
-        return sum((part.astype(F32) for part in parts), mine)
-
-    def groups(self, gate=()):
-        self.x = self.all_pairs(self.dp, self.dp.me, self.dp.count, 0, gate).astype(self.x.dtype)
-        return self
-
-    def along(self, gate=()):
-        return self.all_pairs(self.line, self.line.me // 2, self.line.count // 2, 1, gate)
+        return self.half((self.dp.count, self.line.count // 2), 0, ())
+
+    def groups(self):
+        take = lambda k: lax.dynamic_index_in_dim(self.x, self.dp.me ^ k, 0, keepdims=False)
+        jobs = [(self.dp, take(k), k) for k in range(1, self.dp.count)]
+        self.x = take(0)
+        return jobs
+
+    def along(self):
+        far = self.x.shape[0] if self.x.ndim > len(self.rest) else 1
+        return self.half((far // 2,), self.bits.pop(0), ())
+
+    def take(self, got):
+        kind = self.x.dtype
+        self.x = sum((x.astype(F32) for x in got), self.x.astype(F32)).astype(kind)
+
+    def result(self):
+        while self.bits:
+            self.take([line.across(x, mask) for line, x, mask in self.along()])
+        return self.x.reshape(self.rest).astype(F32)
 
 
 def turned(x, me):
@@ -184,7 +237,7 @@
 
 
 def cost(flops, moved, exps=0):
-    return pl.CostEstimate(flops=flops, bytes_accessed=moved, transcendentals=exps)
+    return pl.CostEstimate(flops=flops // 1000, bytes_accessed=moved // 1000, transcendentals=exps)
 
 
 def attend_kernel(step, len_ref, q_ref, k_ref, v_ref, o_ref, lse_ref):
@@ -298,8 +351,8 @@
 
 
 def feed_kernel(
-    o_ref, x_ref, cot_ref, wm_ref, gain_ref, wg_ref, wu_ref, wd_ref, spread_ref,
-    out_ref, dx_ref, dmixed_ref, dattn_ref, hw_ref, mid_ref, dgate_ref, dup_ref, dgain_ref,
+    o_ref, x_ref, cot_ref, wm_ref, gain_ref, wg_ref, wu_ref, wd_ref,
+    out_ref, dx_ref, dmixed_ref, dattn_ref, hs_ref, mid_ref, dgate_ref, dup_ref,
     h_ref, acc_ref, dh_ref,
 ):
     at = pl.program_id(0)
@@ -310,7 +363,7 @@
         x1 = x_ref[...].astype(F32) + dot(o_ref[...], wm_ref[...])
         h = (normed(x1)[0] * gain_ref[...]).astype(BF)
         h_ref[...] = h
-        hw_ref[...] = dot(h, spread_ref[...]).astype(BF)
+        hs_ref[...] = h
         acc_ref[...] = x1
         dx_ref[...] = x1
         dh_ref[...] = jnp.zeros_like(dh_ref)
@@ -335,7 +388,6 @@
         out_ref[...] = acc_ref[...].astype(BF)
         normal, factor = normed(dx_ref[...])
         dh = dh_ref[...]
-        dgain_ref[...] = jnp.sum(dh * normal, axis=0, keepdims=True)
         dx = cot_ref[...].astype(F32) + norm_back(dh, normal, factor, gain_ref[...])
         dx_ref[...] = dx
         dmixed = dx.astype(BF)
@@ -343,7 +395,7 @@
         dattn_ref[...] = dot_t(dmixed, wm_ref[...]).astype(BF)
 
 
-def feed(step, micro, o, x, cot, wm, gain, wgu, wd, spread, before=(), gate=()):
+def feed(step, micro, o, x, cot, wm, gain, wgu, wd, before=(), gate=()):
     total, width = x.shape
     rows = total // micro
     hq, ff = o.shape[1], wd.shape[0]
@@ -354,8 +406,7 @@
     col = lambda f: pl.BlockSpec((rows, unit), f)
     whole = lambda a: pl.BlockSpec(a.shape, lambda i: (0, 0), **once)
     out = lambda w, t: jax.ShapeDtypeStruct((total, w), t)
-    wide = spread.shape[1]
-    kernel = chained(feed_kernel, 9, len(before) + len(gate))
+    kernel = chained(feed_kernel, 8, len(before) + len(gate))
     return pl.pallas_call(
         kernel,
         grid=(chunks,),
@@ -364,35 +415,43 @@
             pl.BlockSpec((width, unit), lambda i: (0, i)),
             pl.BlockSpec((width, unit), lambda i: (0, chunks + i)),
             pl.BlockSpec((unit, width), lambda i: (i, 0)),
-            whole(spread),
         ]
         + kept(len(before) + len(gate)),
-        out_specs=[row(width), row(width), row(width), row(hq), row(wide)]
-        + [col(lambda i: (step, i))] * 3
-        + [pl.BlockSpec((1, width), lambda i: (0, 0))],
+        out_specs=[row(width), row(width), row(width), row(hq), row(width)]
+        + [col(lambda i: (step, i))] * 3,
         out_shape=[
-            out(width, BF), out(width, F32), out(width, BF), out(hq, BF), out(wide, BF),
-            out(ff, BF), out(ff, BF), out(ff, BF), jax.ShapeDtypeStruct((1, width), F32),
+            out(width, BF), out(width, F32), out(width, BF), out(hq, BF), out(width, BF),
+            out(ff, BF), out(ff, BF), out(ff, BF),
         ],
         scratch_shapes=[
             pltpu.VMEM((rows, width), BF),
             pltpu.VMEM((rows, width), F32),
             pltpu.VMEM((rows, width), F32),
         ],
-        input_output_aliases={9 + i: i for i in range(len(before))},
+        input_output_aliases={8 + i: i for i in range(len(before))},
         compiler_params=params(60, 1),
         cost_estimate=cost(rows * (12 * width * ff + 4 * width * hq), rows * ff * 8 + wgu.size * 3),
         name="feed",
-    )(o, x, cot, wm, gain, wgu, wgu, wd, spread, *before, *gate)
-
-
-def weight_grad_kernel(x_ref, *refs):
+    )(o, x, cot, wm, gain, wgu, wgu, wd, *before, *gate)
+
+
+def weight_grad_kernel(spread, x_ref, *refs):
+    if spread:
+        spread_ref, *refs = refs
     *g_refs, out_ref, turned_ref = refs
     at = pl.program_id(0)
 
     @pl.when(at == 0)
     def _():
-        turned_ref[...] = x_ref[...].T
+        if spread:
+            turned_ref[...] = lax.dot_general(
+                spread_ref[...],
+                x_ref[...],
+                (((0,), (1,)), ((), ())),
+                preferred_element_type=F32,
+            ).astype(BF)
+        else:
+            turned_ref[...] = x_ref[...].T
 
     each = pl.num_programs(0) // len(g_refs)
     for i, g_ref in enumerate(g_refs):
@@ -402,11 +461,17 @@
             out_ref[...] = dot(turned_ref[...], g_ref[...]).astype(BF)
 
 
-def weight_grad(x, grads, unit, columns=None, gate=()):
+def weight_grad(x, grads, unit, spread=None, gate=()):
     rows, width = x.shape
     each = grads[0].shape[1] // unit
     count = each * len(grads)
-    columns = columns or count * unit
+    columns = count * unit
+    whole = lambda a: pl.BlockSpec(a.shape, lambda at: (0, 0), pipeline_mode=pl.Buffered(1))
+    extra = [] if spread is None else [spread]
+    width = width if spread is None else spread.shape[1]
+
+    def kernel(*refs):
+        weight_grad_kernel(spread is not None, *refs)
 
     def place(i):
         return pl.BlockSpec(
@@ -414,11 +479,9 @@
         )
 
     return pl.pallas_call(
-        chained(weight_grad_kernel, 1 + len(grads), len(gate)),
+        chained(kernel, 1 + len(extra) + len(grads), len(gate)),
         grid=(count,),
-        in_specs=[
-            pl.BlockSpec((rows, width), lambda at: (0, 0), pipeline_mode=pl.Buffered(1))
-        ]
+        in_specs=[whole(a) for a in [x] + extra]
         + [place(i) for i in range(len(grads))]
         + kept(len(gate)),
         out_specs=pl.BlockSpec((width, unit), lambda at: (0, at)),
@@ -427,7 +490,7 @@
         compiler_params=params(48, 1),
         cost_estimate=cost(2 * rows * width * count * unit, 2 * rows * (width + count * unit)),
         name="weight_grad",
-    )(x, *grads, *gate)
+    )(x, *extra, *grads, *gate)
 
 
 def stack_heads(x, heads):
@@ -614,7 +677,7 @@
     groups, n = lax.axis_size("dp"), lax.axis_size("noise")
     depth, hq = vlm_key.shape[1], vlm_query.shape[1]
     heads = hq // depth
-    joint = hq + 2 * depth
+    width_qkv = hq + 2 * depth
     ff, ffa = vlm_gate.shape[1], act_gate.shape[1]
     levels = time_scales.shape[1]
     rows_p, rows_a = vlm_query.shape[0], act_query.shape[0]
@@ -653,38 +716,34 @@
     act_small = [act_prenorm[:, None], act_midnorm[:, None], time_scales.reshape(rows_a, -1)]
     act_pack = [act_query, act_key, act_value, lanes(jnp.concatenate(act_small, axis=1), 128)]
     act_pack = jnp.concatenate(act_pack, axis=1)
-    first = [act_pack, taller(pre_pack), lanes(tiles(act_mixer, gap), act_pack.shape[1])]
-    first = lax.all_gather(jnp.concatenate(first, axis=0), ALL, axis=0)
-    act_a = first[:, :rows_a].reshape(total * rows_a, -1)
-    pre_a = first[:, rows_a : rows_a + gap].reshape(total * gap, -1)
-    suf_mixer = first[:, rows_a + gap :]
-
     fold = jnp.concatenate([vlm_mixer, vlm_down], axis=0)
-    second = [taller(vlm_gate), taller(vlm_expand), tiles(fold, gap)]
+    second = [taller(vlm_gate), taller(vlm_expand), tiles(fold, gap), tiles(act_mixer, gap)]
+    cut = 2 * ff + second[2].shape[1]
     second = lax.all_gather(jnp.concatenate(second, axis=1), ALL, axis=0)
 
-    cols = jnp.stack([act_gate, act_expand]).reshape(2, rows_a, groups, n, unit)
-    cols = cols.transpose(3, 0, 1, 2, 4).reshape(n, 2, rows_a, part)
-    cols = lax.all_to_all(cols, "noise", 0, 0, tiled=True)
+    def beside(near):
+        cols = jnp.stack([act_gate, act_expand]).reshape(2, rows_a, groups, n, unit)
+        cols = cols.transpose(3, 0, 1, 2, 4).reshape(n, 2, rows_a, part)
+        (cols,) = after([cols], near)
+        return lax.all_to_all(cols, "noise", 0, 0, tiled=True)
+
+    first = jnp.concatenate([act_pack, taller(pre_pack)], axis=0)
+    first, seg_all, cols = fetch(first, action_in, dp, line, beside)
     cols = cols.transpose(0, 2, 1, 3).reshape(n * rows_a, 2 * part)
     hidden_w = jnp.concatenate([cols, act_down.reshape(-1, 2 * part)], axis=0)
-    hidden_w = jnp.stack([hidden_w] + [dp.across(hidden_w, k) for k in range(1, groups)])
-    hidden_w = turned(hidden_w, dp.me)
-    gu_w = hidden_w[:, : n * rows_a].reshape(-1, 2 * part)
-    down_w = hidden_w[:, n * rows_a :].reshape(part, wide)
-    dy_all = line.around(grad_action.astype(BF).reshape(block, wide)).reshape(-1, wide)
-
-    seg_all = line.around(action_in)
+    dy_own = grad_action.astype(BF).reshape(block, wide)
+    act_a = first[:, :rows_a].reshape(total * rows_a, -1)
+    pre_a = first[:, rows_a:].reshape(total * gap, -1)
 
     places = jnp.arange(total * gap)
     spread = (places // gap * rows_p + places % gap)[None, :] == jnp.arange(width)[:, None]
     spread = (spread & (places % gap < rows_p)[None, :]).astype(BF)
     pre_a = dot(spread, pre_a).astype(BF)
-    pre_qkv = pre_a[:, :joint]
-    pre_gain = pre_a[:, joint].astype(F32)
-    pre_midgain = pre_a[:, joint + 1].astype(F32)
-    suf_qkv = act_a[:, :joint]
-    small = act_a[:, joint:].astype(F32)
+    pre_qkv = pre_a[:, :width_qkv]
+    pre_gain = pre_a[:, width_qkv].astype(F32)
+    pre_midgain = pre_a[:, width_qkv + 1].astype(F32)
+    suf_qkv = act_a[:, :width_qkv]
+    small = act_a[:, width_qkv:].astype(F32)
     suf_gain, suf_midgain = small[:, 0], small[:, 1]
     table = small[:, 2 : 2 + time_scales.size // rows_a].reshape(2 * wide, levels)
 
@@ -698,23 +757,28 @@
     mod2 = mods[0, :, None, wide:]
     an1, as1 = normed(jnp.where(is_row, seg_all, 0).astype(F32))
     ah1 = flatten((an1 * suf_gain * mod1_all).astype(BF))
-    seg_qkv = dot(ah1, suf_qkv).astype(BF).reshape(n, micro, slot, joint)
+    seg_qkv = dot(ah1, suf_qkv).astype(BF).reshape(n, micro, slot, width_qkv)
 
     x = prefix_rows[:, 0]
     n1, s1 = normed(x.astype(F32))
     h1 = flatten((n1 * pre_gain).astype(BF))
-    qkv = dot(h1, pre_qkv).astype(BF).reshape(micro, prefix, joint)
+    qkv = dot(h1, pre_qkv).astype(BF).reshape(micro, prefix, width_qkv)
     lens = lax.dynamic_slice_in_dim(prefix_len, here, 1, axis=1)[:, 0]
 
     oa, lse_a = own_attend(seg_qkv, qkv, own, lens, heads, seg_len)
 
-    outs = attend(0, qkv, lens, heads, (), (oa,))
     oa = line.home(oa.reshape(n, block, hq))
+    hidden_w, dy_own = after([hidden_w, dy_own], oa)
+    hidden_w = jnp.stack([hidden_w] + [dp.across(hidden_w, k) for k in range(1, groups)])
+    hidden_w = turned(hidden_w, dp.me)
+    dy_all = line.around(dy_own).reshape(-1, wide)
+    gu_w = hidden_w[:, : n * rows_a].reshape(-1, 2 * part)
+    down_w = hidden_w[:, n * rows_a :].reshape(part, wide)
+    outs = attend(0, qkv, lens, heads, (), (seg_qkv,))
     outs = attend(1, qkv, lens, heads, outs, (oa,))
     o, lse = outs
     oa = line.home_end(oa, (o,)).astype(BF)
-    suf_mixer = suf_mixer[..., : tiles(act_mixer, gap).shape[1]]
-    suf_mixer = tiles(suf_mixer, gap, act_mixer.shape)
+    suf_mixer = tiles(second[..., cut:], gap, act_mixer.shape)
     a1 = jnp.where(is_row, action_in, 0).astype(F32) + dot(oa, suf_mixer).reshape(micro, slot, wide)
     an2, as2 = normed(a1)
     ah2 = (an2 * suf_midgain * mod2).astype(BF).reshape(block, wide)
@@ -729,7 +793,8 @@
         [(dmid_a * up_a * slope_g).astype(BF), (dmid_a * act_g).astype(BF)], axis=1
     )
     grad_late = line.home(dot_t(dgu, gu_w).astype(BF).reshape(n, block, wide))
-    out_a = line.home(dot(mid_a, down_w).astype(BF).reshape(n, block, wide))
+    out_a = turned(dot(mid_a, down_w).astype(BF).reshape(n, block, wide), here)
+    out_a = lax.psum_scatter(out_a, "noise", scatter_dimension=0)
     dff = jnp.concatenate(
         [
             dot_w(h_all, dgu).astype(BF).reshape(groups, n * rows_a, 2 * part),
@@ -741,7 +806,7 @@
     dff = lax.psum_scatter(dff, "dp", scatter_dimension=0, tiled=True)
 
     pre_gu = dot(spread, second[..., : 2 * ff].reshape(total * gap, -1)).astype(BF)
-    fold = tiles(second[..., 2 * ff :], gap, fold.shape).reshape(total, -1, width)
+    fold = tiles(second[..., 2 * ff : cut], gap, fold.shape).reshape(total, -1, width)
     pre_mixer = fold[:, :rows_m].reshape(hq, width)
     pre_down = fold[:, rows_m:].reshape(ff, width)
     cot = cot_prefix.reshape(micro * prefix, width)
@@ -749,27 +814,50 @@
     def feed_half(step, outs, gate):
         return feed(
             step, micro, o.reshape(-1, hq), x.reshape(-1, width), cot,
-            pre_mixer, pre_midgain[None], pre_gu, pre_down, spread, outs, gate,
+            pre_mixer, pre_midgain[None], pre_gu, pre_down, outs, gate,
         )
 
     outs = feed_half(0, (), (grad_late,))
-    pre_dmid = outs[-1]
     grad_late = line.home_end(grad_late, (outs[0],)).reshape(micro, slot, wide)
     late_back = grad_late * an2
-    suf_dmid = jnp.sum(late_back * mod2, axis=(0, 1))
     dmod2 = jnp.sum(late_back * suf_midgain, axis=1)
     da1 = grad_action + norm_back(grad_late, an2, as2, suf_midgain * mod2)
     dmixed_a = da1.astype(BF).reshape(block, wide)
     dattn_a = dot_t(dmixed_a, suf_mixer).astype(BF)
-    outs = feed_half(1, outs[:-1], (dattn_a,))
-    pre_dmid = pre_dmid + outs[-1]
-    prefix_out, dx1, dmixed, dattn, h2, mid, dgate, dup = outs[:-1]
+    outs = feed_half(1, outs, (dattn_a,))
+    prefix_out, dx1, dmixed, dattn, h2, mid, dgate, dup = outs
     dattn_all = line.around(dattn_a, (dx1,)).reshape(n, micro, slot, hq)
 
+    big_w = weight_grad(h2, [dgate, dup], 512, spread)
+    big_sum = Sum(big_w.reshape(total, gap, -1), dp, line)
+    big_way = joint(big_sum.cores())
+
+    (dattn_all,) = after([dattn_all], big_w)
+    dseg, far_dk, far_dv = own_back(seg_qkv, qkv, dattn_all, lse_a, own, lens, heads, seg_len)
+    dseg = dseg.reshape(n * block, width_qkv)
+    dah1 = dot_t(dseg, suf_qkv).reshape(n, micro, slot, wide)
+    dmod1 = jnp.sum(dah1 * an1 * suf_gain, axis=2)
+    back = norm_back(dah1, an1, as1, suf_gain * mod1_all).astype(BF).reshape(n, block, wide)
+    dtable = jnp.concatenate(
+        [
+            jnp.einsum("nmj,nmt->jt", dmod1, hots, precision=HIGH),
+            jnp.einsum("mj,mt->jt", dmod2, hots[0], precision=HIGH),
+        ],
+        axis=0,
+    )
+    table_cols = dtable.size // wide
+    dtable = lanes(dtable.reshape(wide, table_cols), 128).astype(BF)
+    act_w = jnp.concatenate([dot_w(ah1, dseg).astype(BF), dtable], axis=1)
+    act_sum = Sum(act_w.reshape(total, rows_a, -1), dp, line)
+    big_sum.take(big_way)
+
+    early = (big_sum.x, act_w)
     dmd_w = jnp.concatenate(
         [
-            weight_grad(o.reshape(-1, hq), [dmixed], width).reshape(total, rows_m, width),
-            weight_grad(mid, [cot], width, gate=(dx1,)).reshape(total, -1, width),
+            weight_grad(o.reshape(-1, hq), [dmixed], width, gate=early).reshape(
+                total, rows_m, width
+            ),
+            weight_grad(mid, [cot], width, gate=early).reshape(total, -1, width),
         ],
         axis=1,
     )
@@ -781,92 +869,90 @@
     dmd_w = tiles(grads_sum[:, :cut], gap, dmd_w.shape[1:])
     dam_w = tiles(grads_sum[:, cut:], gap, (rows_a, wide))
 
-    dseg, far_dk, far_dv = own_back(seg_qkv, qkv, dattn_all, lse_a, own, lens, heads, seg_len)
-    dseg = dseg.reshape(n * block, joint)
-    act_sum = Sum(dot_w(ah1, dseg).astype(BF).reshape(total, rows_a, -1), dp, line).cores()
-
-    big_w = weight_grad(h2, [dgate, dup], 512, gate=(act_sum.x, grads))
-    big_sum = Sum(big_w.reshape(total, gap, -1), dp, line).cores()
     dattn = dattn.reshape(micro, prefix, hq)
-    outs = attend_back(0, qkv, dattn, lse, lens, heads, (), (big_w,))
-    act_sum.groups((outs[0],))
+    outs = attend_back(0, qkv, dattn, lse, lens, heads, (), (grads,))
+    *big_way, act_way = joint(big_sum.groups() + act_sum.cores(), outs[0])
+    big_sum.take(big_way)
+    act_sum.take([act_way])
     outs = attend_back(1, qkv, dattn, lse, lens, heads, outs, (big_sum.x, act_sum.x))
     dq, dk, dv = outs
-    big_sum.groups((dq,))
+    big_way, *act_way = joint(big_sum.along() + act_sum.groups(), dq)
+    big_sum.take([big_way])
+    act_sum.take(act_way)
     dkv = jnp.concatenate([(dk + far_dk).astype(BF), (dv + far_dv).astype(BF)], axis=-1)
-    dqkv = jnp.concatenate([dq, dkv], axis=-1).reshape(-1, joint)
-    h1_wide = dot(h1, spread).astype(BF)
-    pre_sum = weight_grad(h1_wide, [dqkv], 512).reshape(total, gap, -1)
-    pre_sum = Sum(pre_sum, dp, line).cores()
-
-    dah1 = dot_t(dseg, suf_qkv).reshape(n, micro, slot, wide)
-    first_back = dah1 * an1
-    suf_dgain = jnp.sum(first_back * mod1_all, axis=(0, 1, 2))
-    dmod1 = jnp.sum(first_back * suf_gain, axis=2)
-    back = norm_back(dah1, an1, as1, suf_gain * mod1_all).astype(BF).reshape(n, block, wide)
-    back = line.home_end(line.home(back)).reshape(micro, slot, wide)
-    out_a = line.home_end(out_a).reshape(micro, slot, wide)
-    action_out = (a1 + out_a)[:, :seg_len].astype(BF)
-    action_grad = (da1 + back)[:, :seg_len]
-    dtable = jnp.concatenate(
-        [
-            jnp.einsum("nmj,nmt->jt", dmod1, hots, precision=HIGH),
-            jnp.einsum("mj,mt->jt", dmod2, hots[0], precision=HIGH),
-        ],
-        axis=0,
-    )
-    dh1 = dot_t(dqkv, pre_qkv).reshape(micro, prefix, width)
-    pre_dgain = jnp.sum(dh1 * n1, axis=(0, 1))
-    prefix_grad = dx1.reshape(micro, prefix, width) + norm_back(dh1, n1, s1, pre_gain)
-
+    dqkv = jnp.concatenate([dq, dkv], axis=-1).reshape(-1, width_qkv)
+    pre_w = weight_grad(h1, [dqkv], 512, spread, (big_sum.x, act_sum.x))
+    back = back.reshape((n // 2, 2) + back.shape[1:])
+    jobs = [big_sum.along() if big_sum.bits else [], act_sum.along(), [(line, back[:, 1], 1)]]
+    *ways, back_way = joint(sum(jobs, []), pre_w)
+    for way, each in zip(ways, [s for s, j in zip((big_sum, act_sum), jobs) if j]):
+        each.take([way])
+    back = back[:, 0] + back_way
+    pre_sum = Sum(pre_w.reshape(total, gap, -1), dp, line)
+    jobs = act_sum.along() if act_sum.bits else []
+    *ways, pre_way = joint(jobs + pre_sum.cores(), back)
+    for way in ways:
+        act_sum.take([way])
+    pre_sum.take([pre_way])
+    pre_sum.take(joint(pre_sum.groups()))
+    (dqkv, back) = after([dqkv, back], pre_w)
+
+    (dff,) = after([dff], pre_w)
     ddown_a = dff[n * rows_a :].reshape(unit, wide)
     dgu_a = dff[: n * rows_a].reshape(n, rows_a, 2 * part)
     dgu_a = lax.all_to_all(dgu_a, "noise", 0, 0, tiled=True)
     dgu_a = dgu_a.reshape(n, rows_a, 2, groups, unit).transpose(2, 1, 3, 0, 4)
-    dgu_a = dgu_a.reshape(2, rows_a, ffa)
-    smalls = jnp.concatenate(
-        [
-            dtable.reshape(total, -1),
-            pre_dgain.reshape(total, rows_p),
-            pre_dmid.reshape(total, rows_p),
-            suf_dgain.reshape(total, rows_a),
-            suf_dmid.reshape(total, rows_a),
-        ],
-        axis=1,
-    )
-    smalls = lanes(smalls, -(-smalls.shape[1] // 128) * 128).reshape(total, -1, 128)
-    small_sum = Sum(smalls, dp, line)
-    smalls = small_sum.cores().groups().along().reshape(-1)
-    act_g = act_sum.along()
-    big_g = big_sum.along()[:rows_p]
-    pre_g = pre_sum.groups().along()[:rows_p]
-    at = [dtable.size // total]
-    for size in (rows_p, rows_p, rows_a, rows_a):
-        at.append(at[-1] + size)
+    dgu_a = dgu_a.reshape(2, rows_a, ffa).astype(F32)
+    back = line.home_end(back).reshape(micro, slot, wide)
+    action_out = (a1 + out_a.reshape(micro, slot, wide))[:, :seg_len].astype(BF)
+    action_grad = (da1 + back)[:, :seg_len]
+    dh1 = dot_t(dqkv, pre_qkv).reshape(micro, prefix, width)
+    prefix_grad = dx1.reshape(micro, prefix, width) + norm_back(dh1, n1, s1, pre_gain)
+
+    big_g = big_sum.result()[:rows_p]
+    act_g = act_sum.result()
+    pre_g = pre_sum.result()[:rows_p]
+
+    def gain_grad(pairs, gain):
+        sums = sum(jnp.sum(w.astype(F32) * dw, axis=1) for w, dw in pairs)
+        return sums / gain.astype(F32)
+
+    pre_pairs = [
+        (vlm_query, pre_g[:, :hq]),
+        (vlm_key, pre_g[:, hq : hq + depth]),
+        (vlm_value, pre_g[:, hq + depth :]),
+    ]
+    mid_pairs = [(vlm_gate, big_g[:, :ff]), (vlm_expand, big_g[:, ff:])]
+    act_pairs = [
+        (act_query, act_g[:, :hq]),
+        (act_key, act_g[:, hq : hq + depth]),
+        (act_value, act_g[:, hq + depth : width_qkv]),
+    ]
+    late_pairs = [(act_gate, dgu_a[0]), (act_expand, dgu_a[1])]
     return (
         prefix_out.reshape(prefix_rows.shape),
         action_out[:, None],
         prefix_grad[:, None],
         action_grad[:, None],
-        smalls[at[0] : at[1]],
+        gain_grad(pre_pairs, vlm_prenorm),
         pre_g[:, :hq],
         pre_g[:, hq : hq + depth],
         pre_g[:, hq + depth :],
         dmd_w[:rows_m].astype(F32),
-        smalls[at[1] : at[2]],
+        gain_grad(mid_pairs, vlm_midnorm),
         big_g[:, :ff],
         big_g[:, ff:],
         dmd_w[rows_m:].astype(F32),
-        smalls[at[2] : at[3]],
+        gain_grad(act_pairs, act_prenorm),
         act_g[:, :hq],
         act_g[:, hq : hq + depth],
-        act_g[:, hq + depth :],
+        act_g[:, hq + depth : width_qkv],
         dam_w.astype(F32),
-        smalls[at[3] : at[4]],
-        dgu_a[0].astype(F32),
-        dgu_a[1].astype(F32),
+        gain_grad(late_pairs, act_midnorm),
+        dgu_a[0],
+        dgu_a[1],
         ddown_a.astype(F32),
-        smalls[: at[0]].reshape(-1, levels),
+        act_g[:, width_qkv : width_qkv + table_cols].reshape(-1, levels),
     )
 
 

time: 667 us -> 608 us (0.912)
  waiting for transfers between devices: 156 us -> 102 us
  starting transfers between devices: 116 us -> 88.6 us
  other arithmetic: 73.8 us -> 88.3 us
    all_gather x1 -> x0, waiting for transfers between devices: 52.4 us -> none  [per_device(): first = lax.all_gather(jnp.concatenate(first, axis=0), ALL, axis=0)]
    ppermute x63 -> x55, starting transfers between devices: 102 us -> 78.4 us  [across(): lax.ppermute(x, self.axes, [(i, i ^ mask) for i in range(self.count)])]
    unnamed x241 -> x317, local copies, waits for them, and re-layouts: 23.9 us -> 40 us
    convert_element_type x6 -> x15, other arithmetic: 7.19 us -> 18.4 us  [the longest x9 15.5 us: take(): self.x = sum((x.astype(F32) for x in got), self.x.astype(F32)).astype(kind)]
    another operation x1 -> x8, other arithmetic: 0.02 us -> 9.57 us  [the longest x2 4.75 us: fetch(): same = jnp.stack([near] + got)]
    pallas_call x4 -> x5, Pallas kernels: 39.3 us -> 47.8 us  [the longest x4 42.4 us: weight_grad(): pl.pallas_call(chained(kernel, 1 + len(extra) + len(grads), len(gate)), g...]
    slice x12 -> x7, local copies, waits for them, and re-layouts: 13.4 us -> 6.09 us  [the longest x1 2.37 us: per_device(): second[..., 2 * ff:cut]]
    dot_general x8 -> x7, matrix products: 25.6 us -> 20 us  [dot(): lax.dot_general(a, b, (((1,), (0,)), ((), ())), preferred_element_type=F32)]
  transfers between devices with their start and end apart: 69 -> 61, of which waited for: 22 -> 13; matrix products, arithmetic and copies ran while one was open for 28% -> 31% of each run, Pallas kernels for 24% -> 27%
where the time goes in v3:
time: 608 us; the launch traced here: 605 us
  Pallas kernels  161 us (26%)
  waiting for transfers between devices  102 us (17%)
  local copies, waits for them, and re-layouts  95.7 us (16%)
  starting transfers between devices  88.6 us (15%)
  other arithmetic  88.3 us (15%)
  matrix products  52.8 us (9%)
  between operations  16.3 us (3%)
    ppermute x55, waiting for transfers between devices, across(): lax.ppermute(x, self.axes, [(i, i ^ mask) for i in range(self.count)])  102 us
    ppermute x55, starting transfers between devices, across(): lax.ppermute(x, self.axes, [(i, i ^ mask) for i in range(self.count)])  78.4 us
    pallas_call x2, Pallas kernels, feed(): pl.pallas_call(kernel, grid=(chunks,), in_specs=[row(hq), row(width), row...  58.2 us
    pallas_call x4, Pallas kernels, weight_grad(): pl.pallas_call(chained(kernel, 1 + len(extra) + len(grads), len(gate)), g...  42.4 us
    unnamed x317, local copies, waits for them, and re-layouts  40 us
    pallas_call x2, Pallas kernels, attend_back(): pl.pallas_call(chained(kernel, 6, len(before) + len(gate)), grid_spec=plt...  28.4 us
    pallas_call x2, Pallas kernels, attend(): pl.pallas_call(chained(kernel, 4, len(before) + len(gate)), grid_spec=plt...  21.8 us
    dot_general x5, matrix products, dot_t(): lax.dot_general(a, b, (((1,), (1,)), ((), ())), preferred_element_type=F32)  20.6 us
  transfers between devices with their start and end apart: 61, of which 13 were waited for; matrix products, arithmetic and copies ran while one was open for 31% of the time, Pallas kernels for 27%

profile of v3, /device:TPU:0, one launch (start us, length us, event | category | flops | bytes accessed | tf_op | source)
XLA Modules:
  0.0 605.1 jit_solution(17395772584682156495)
XLA Ops:
  15.8 3.1 collective-permute-start
  18.9 2.6 collective-permute-start.1
  28.9 10.5 %collective-permute-done.1.refs_1_ = bf16[56,1664]{1,0:T(8,128)(2,1)S(1)} collective-permute-done((bf16[56,1664]{1,0:T(8,128)(2,1)S(1)}, bf16[56,1664]{1,0:T(8,128)(2,1)S(1)}, u32[]{:S(2)}, u32[]{:S(2)}) %collective-permute-start.1) | collective-permute-done | bytes 186400 | tf_op jit(solution)/shard_map/ppermute | solution.py:63
  39.5 5.1 collective-permute-done.3.refs_3_
  45.3 2.3 fusion.102
  47.6 5.4 all-to-all-start
  58.7 2.9 collective-permute-start.7
  61.6 42.1 %collective-permute-done.7.refs_3_ = bf16[2,2,56,1024]{3,2,1,0:T(8,128)(2,1)S(1)} collective-permute-done((bf16[2,2,56,1024]{3,2,1,0:T(8,128)(2,1)S(1)}, bf16[2,2,56,1024]{3,2,1,0:T(8,128)(2,1)S(1)}, u32[]{:S(2)}, u32[]{:S(2)}) %collective-permute-start.7) | collective-permute-done | bytes 458784 | tf_op jit(solution)/shard_map/ppermute | solution.py:63
  106.5 2.4 pad_maximum_fusion.5.same_ref
  112.0 2.2 fusion.2
  116.3 5.4 settle.1
  121.7 4.1 slice.325
  141.6 4.3 convolution_convert_fusion
  146.0 3.2 convolution_convert_fusion.2
  151.5 2.1 collective-permute-done.10
  154.5 2.5 collective-permute-start.18
  157.1 4.7 collective-permute-start.19
  165.5 10.9 %attend.2 = (bf16[2,816,1024]{2,1,0:T(8,128)(2,1)S(1)}, f32[2,4,1,816]{3,2,1,0:T(1,128)S(1)}) custom-call(s32[2]{0:T(128)S(1)} %fusion.98.refs_0_.refs_1_, bf16[2,816,1536]{2,1,0:T(8,128)(2,1)} %bitcast.442, bf16[2,816,1536]{2,1,0:T(8,128)(2,1)} %bitcast.443, bf16[2,816,1536]{2,1,0:T(8,128)(2,1)} %bitcast.444, bf16[8,2,56,1536]{3,2,1,0:T(8,128)(2,1)S(1)} %bitcast.460), custom_call_target="tpu_custom_call" | custom-call | flops 2727346 | bytes 5013 | tf_op jit(solution)/shard_map/attend/pallas_call | solution.py:265
  177.1 2.4 collective-permute-start.12
  180.6 10.9 %attend.3 = (bf16[2,816,1024]{2,1,0:T(8,128)(2,1)S(1)}, f32[2,4,1,816]{3,2,1,0:T(1,128)S(1)}) custom-call(s32[2]{0:T(128)S(1)} %fusion.98.refs_0_.refs_1_, bf16[2,816,1536]{2,1,0:T(8,128)(2,1)} %bitcast.445, bf16[2,816,1536]{2,1,0:T(8,128)(2,1)} %bitcast.446, bf16[2,816,1536]{2,1,0:T(8,128)(2,1)} %bitcast.447, ...), custom_call_target="tpu_custom_call", output_to_operand_aliasing={{0}: (4, {}), {1}: (5, {})} | custom-call | flops 2727346 | bytes 5013 | tf_op jit(solution)/shard_map/attend/pallas_call | solution.py:265
  199.7 2.9 collective-permute-start.22
  204.1 2.3 collective-permute-start.16
  209.7 12.0 %collective-permute-done.22 = bf16[112,1024]{1,0:T(8,128)(2,1)} collective-permute-done((bf16[112,1024]{1,0:T(8,128)(2,1)S(1)}, bf16[112,1024]{1,0:T(8,128)(2,1)}, u32[]{:S(2)}, u32[]{:S(2)}) %collective-permute-start.22) | collective-permute-done | bytes 229408 | tf_op jit(solution)/shard_map/ppermute | solution.py:63
  225.4 12.9 %collective-permute-done.16 = bf16[384,1024]{1,0:T(8,128)(2,1)S(1)} collective-permute-done((bf16[384,1024]{1,0:T(8,128)(2,1)}, bf16[384,1024]{1,0:T(8,128)(2,1)S(1)}, u32[]{:S(2)}, u32[]{:S(2)}) %collective-permute-start.16) | collective-permute-done | bytes 786464 | tf_op jit(solution)/shard_map/ppermute | solution.py:63
  241.9 2.5 fusion.110
  244.5 2.2 multiply_convert_fusion.6
  253.2 3.2 slice.338
  256.4 2.4 slice.335
  262.0 6.1 %convolution_convert_fusion.1.refs_5_.refs_6_ = bf16[640,4096]{1,0:T(8,128)(2,1)} fusion(bf16[768,4096]{1,0:T(8,128)(2,1)S(1)} %bitcast.511, s32[768]{0:T(1024)S(1)} %copy-done.131, pred[768]{0:T(1024)(128)(4,1)S(1)} %copy-done.142), kind=kOutput, calls=%fused_computation.3 | convolution fusion | flops 4030136320 | bytes 11538176 | tf_op jit(solution)/shard_map/dot_general | solution.py:41
  271.2 5.6 collective-permute-start.26
  276.8 2.4 collective-permute-start.28
  279.2 3.7 convolution_convert_fusion.4
  283.0 29.2 %feed.2 = (bf16[1632,640]{1,0:T(8,128)(2,1)}, f32[1632,640]{1,0:T(8,128)}, bf16[1632,640]{1,0:T(8,128)(2,1)}, bf16[1632,1024]{1,0:T(8,128)(2,1)}, bf16[1632,640]...) custom-call(bf16[1632,1024]{1,0:T(8,128)(2,1)} %bitcast.456, ...), custom_call_target="tpu_custom_call" | custom-call | flops 14973665 | bytes 21233 | tf_op jit(solution)/shard_map/feed/pallas_call | solution.py:410
  320.2 2.4 collective-permute-start.32
  323.9 2.2 pad_maximum_fusion.4
  326.2 29.0 %feed.3 = (bf16[1632,640]{1,0:T(8,128)(2,1)}, f32[1632,640]{1,0:T(8,128)}, bf16[1632,640]{1,0:T(8,128)(2,1)}, bf16[1632,1024]{1,0:T(8,128)(2,1)}, bf16[1632,640]...) custom-call(bf16[1632,1024]{1,0:T(8,128)(2,1)} %bitcast.457, ...), custom_call_target="tpu_custom_call", output_to_operand_aliasing={{0}: (8, {}), {1}: (9, {}), {2}: (10, {}), {3}: (11, {}), {... | custom-call | flops 14973665 | bytes 21233 | tf_op jit(solution)/shard_map/feed/pallas_call | solution.py:410
  357.0 18.9 %weight_grad.4.refs_1_ = bf16[768,4096]{1,0:T(8,128)(2,1)} custom-call(bf16[1632,640]{1,0:T(8,128)(2,1)S(1)} %copy-done.16, bf16[640,768]{1,0:T(8,128)(2,1)S(1)} %fusion.16.refs_1_, bf16[1632,2048]{1,0:T(8,128)(2,1)} %get-tuple-element.155.refs_2_, bf16[1632,2048]{1,0:T(8,128)(2,1)} %get-tuple-element.156.refs_3_), custom_call_target="tpu_custom_call" | custom-call | flops 10267656 | bytes 15876 | tf_op jit(solution)/shard_map/weight_grad/pallas_call | solution.py:481
  378.2 4.0 dynamic-slice_bitcast_fusion
  388.6 2.4 copy-done.3
  395.0 6.0 multiply_reduce_fusion.1
  401.8 5.9 bitcast_convert_fusion
  409.5 2.2 copy-done.54
  417.4 4.0 fusion.1.refs_2_
  424.8 3.5 collective-permute-start.35
  429.7 5.1 weight_grad.5
  434.8 8.8 %weight_grad.6 = bf16[2048,640]{1,0:T(8,128)(2,1)S(1)} custom-call(bf16[1632,2048]{1,0:T(8,128)(2,1)} %get-tuple-element.162.refs_0_, bf16[1632,640]{1,0:T(8,128)(2,1)S(1)} %bitcast.464, bf16[4,4,24,4096]{3,2,1,0:T(8,128)(2,1)} %copy-done.32, bf16[1024,1664]{1,0:T(8,128)(2,1)} %copy-done.27), custom_call_target="tpu_custom_call" | custom-call | flops 4278190 | bytes 8773 | tf_op jit(solution)/shard_map/weight_grad/pallas_call | solution.py:481
  445.3 3.2 pad_maximum_fusion.refs_6_
  448.5 14.0 %attend_back.2 = (bf16[2,816,1024]{2,1,0:T(8,128)(2,1)}, f32[2,816,256]{2,1,0:T(8,128)S(1)}, f32[2,816,256]{2,1,0:T(8,128)S(1)}) custom-call(s32[2]{0:T(128)S(1)} %fusion.98.refs_0_.refs_1_, bf16[2,816,1536]{2,1,0:T(8,128)(2,1)} %bitcast.448, bf16[2,816,1536]{2,1,0:T(8,128)(2,1)} %bitcast.449, bf16[2,816,1536]{2,1,0:T(8,128)(2,1)} %bitcast.450, ...), custom_call_target="tpu_custom_call" | custom-call | flops 6818365 | bytes 12533 | tf_op jit(solution)/shard_map/attend_back/pallas_call | solution.py:322
  466.6 2.6 fusion.9.refs_10_
  478.4 14.4 %attend_back.3 = (bf16[2,816,1024]{2,1,0:T(8,128)(2,1)}, f32[2,816,256]{2,1,0:T(8,128)S(1)}, f32[2,816,256]{2,1,0:T(8,128)S(1)}) custom-call(s32[2]{0:T(128)S(1)} %fusion.98.refs_0_.refs_1_, bf16[2,816,1536]{2,1,0:T(8,128)(2,1)} %bitcast.451, bf16[2,816,1536]{2,1,0:T(8,128)(2,1)} %bitcast.452, ...), custom_call_target="tpu_custom_call", output_to_operand_aliasing={{0}: (6, {}), {1}: (7, {}), {2}: (8, {})} | custom-call | flops 6818365 | bytes 12533 | tf_op jit(solution)/shard_map/attend_back/pallas_call | solution.py:322
  494.9 2.6 pad_maximum_fusion.1
  501.9 6.3 %collective-permute-start.42 = (bf16[1,24,4096]{2,1,0:T(8,128)(2,1)S(1)}, bf16[1,24,4096]{2,1,0:T(8,128)(2,1)S(1)}, u32[]{:S(2)}, u32[]{:S(2)}) collective-permute-start(bf16[1,24,4096]{2,1,0:T(8,128)(2,1)S(1)} %constant_dynamic-slice_fusion.2), channel_id=1, source_target_pairs={{0,4},{1,5},{2,6},{3,7},{4,0},{5,1},{6,2},{7,3},{8,12},{9,13},{10,... | collective-permute-start | bytes 589832 | tf_op jit(solution)/shard_map/ppermute | solution.py:63
  508.2 9.6 %weight_grad.7.refs_3_.refs_2_.refs_1_ = bf16[768,1536]{1,0:T(8,128)(2,1)} custom-call(bf16[1632,640]{1,0:T(8,128)(2,1)S(1)} %copy-done.15, bf16[640,768]{1,0:T(8,128)(2,1)S(1)} %copy-done.12, bf16[1632,1536]{1,0:T(8,128)(2,1)} %bitcast.484, bf16[2,24,4096]{2,1,0:T(8,128)(2,1)S(1)} %fusion.40.refs_3_, bf16[4,32,1664]{2,1,0:T(8,128)(2,1)S(1)} %fusion.39.refs_4_), custom_call_target="tpu_custom_call" | custom-call | flops 3850371 | bytes 7520 | tf_op jit(solution)/shard_map/weight_grad/pallas_call | solution.py:481
  517.8 2.4 dynamic-slice_bitcast_fusion.2
  520.2 4.6 collective-permute-done.42.refs_0_
  529.3 2.3 fusion.34.refs_1_.refs_2_
  535.8 4.6 all-to-all-start.1
  546.8 2.3 collective-permute-start.52
  550.0 2.8 collective-permute-start.45
  554.4 8.9 %multiply_reduce_fusion = (f32[1632]{0:T(1024)S(1)}, f32[1632,640]{1,0:T(8,128)}) fusion(bf16[1632,640]{1,0:T(8,128)(2,1)S(1)} %bitcast.483, f32[640]{0:T(1024)S(1)} %copy-done.124, f32[1632]{0:T(1024)S(1)} %copy-done.126, bf16[1632,1536]{1,0:T(8,128)(2,1)} %get-tuple-element.180, bf16[640,1664]{1,0:T(8,128)(2,1)S(1)} %copy-done.120), kind=kOutput, calls=%fused_computation.16 | convolution fusion | flops 3213863424 | bytes 13265280 | tf_op jit(solution)/shard_map/dot_general | solution.py:45
  564.2 5.4 fusion.6
  574.4 6.4 %collective-permute-done.47 = bf16[112,1024]{1,0:T(8,128)(2,1)S(1)} collective-permute-done((bf16[112,1024]{1,0:T(8,128)(2,1)S(1)}, bf16[112,1024]{1,0:T(8,128)(2,1)S(1)}, u32[]{:S(2)}, u32[]{:S(2)}) %collective-permute-start.47) | collective-permute-done | bytes 229408 | tf_op jit(solution)/shard_map/ppermute | solution.py:63
  582.4 2.7 collective-permute-start.54
  586.3 2.2 collective-permute-done.54
  (609 shorter events, 180.7 us)
Async XLA Ops:
  7.2 107.7 %copy-start = (s32[2,8]{1,0:T(2,128)S(1)}, s32[2,8]{1,0:T(2,128)}, u32[]{:S(2)}) copy-start(s32[2,8]{1,0:T(2,128)} %param.36) | copy-start | bytes 196
  7.2 188.9 %all-gather.3.cloned.1.call-start = ((), (), s32[]{:S(2)}) async-start(), calls=%async_computation.7 | async-start | bytes 12773376 | tf_op jit(solution)/shard_map/all_gather | solution.py:722
  15.8 13.1 %collective-permute-start = (bf16[56,1664]{1,0:T(8,128)(2,1)S(1)}, bf16[56,1664]{1,0:T(8,128)(2,1)S(1)}, u32[]{:S(2)}, u32[]{:S(2)}) collective-permute-start(bf16[56,1664]{1,0:T(8,128)(2,1)S(1)} %fusion.67), channel_id=1, source_target_pairs={{0,2},{1,3},{2,0},{3,1},{4,6},{5,7},{6,4},{7,5},{8,10},{9,11},{10,... | collective-permute-start | bytes 559112 | tf_op jit(solution)/shard_map/ppermute | solution.py:63
  18.9 20.5 %collective-permute-start.1 = (bf16[56,1664]{1,0:T(8,128)(2,1)S(1)}, bf16[56,1664]{1,0:T(8,128)(2,1)S(1)}, u32[]{:S(2)}, u32[]{:S(2)}) collective-permute-start(bf16[56,1664]{1,0:T(8,128)(2,1)S(1)} %fusion.67), channel_id=1, source_target_pairs={{0,4},{1,5},{2,6},{3,7},{4,0},{5,1},{6,2},{7,3},{8,12},{9,13},{10,... | collective-permute-start | bytes 559112 | tf_op jit(solution)/shard_map/ppermute | solution.py:63
  21.5 18.0 %collective-permute-start.2 = (bf16[56,1664]{1,0:T(8,128)(2,1)S(1)}, bf16[56,1664]{1,0:T(8,128)(2,1)S(1)}, u32[]{:S(2)}, u32[]{:S(2)}) collective-permute-start(bf16[56,1664]{1,0:T(8,128)(2,1)S(1)} %fusion.67), channel_id=1, source_target_pairs={{0,6},{1,7},{2,4},{3,5},{4,2},{5,3},{6,0},{7,1},{8,14},{9,15},{10,... | collective-permute-start | bytes 559112 | tf_op jit(solution)/shard_map/ppermute | solution.py:63
  26.2 18.3 %collective-permute-start.3 = (bf16[2,56,1024]{2,1,0:T(8,128)(2,1)S(1)}, bf16[2,56,1024]{2,1,0:T(8,128)(2,1)S(1)}, u32[]{:S(2)}, u32[]{:S(2)}) collective-permute-start(bf16[2,56,1024]{2,1,0:T(8,128)(2,1)S(1)} %pad_maximum_fusion.20), channel_id=1, source_target_pairs={{0,2},{1,3},{2,0},{3,1},{4,6},{5,7},{6,4},{7,5},{8,10},{9,11},{10,... | collective-permute-start | bytes 688136 | tf_op jit(solution)/shard_map/ppermute | solution.py:63
  47.6 56.9 %all-to-all-start = ((bf16[8,2,32,512]{3,2,1,0:T(8,128)(2,1)}), bf16[8,2,32,512]{3,2,1,0:T(8,128)(2,1)S(1)}, u32[]{:S(2)}, u32[]{:S(2)}) async-start(bf16[8,2,32,512]{3,2,1,0:T(8,128)(2,1)} %after.18), calls=%async_computation | async-start | bytes 1048576 | tf_op jit(solution)/shard_map/all_to_all | solution.py:728
  53.0 362.5 %reduce-scatter.6.cloned.1.call-start = ((), (), s32[]{:S(2)}) async-start(), calls=%async_computation.5 | async-start | bytes 2064384 | tf_op jit(solution)/shard_map/reduce_scatter | solution.py:797
  53.1 50.7 %collective-permute-start.4 = (bf16[4,56,1664]{2,1,0:T(8,128)(2,1)S(1)}, bf16[4,56,1664]{2,1,0:T(8,128)(2,1)S(1)}, u32[]{:S(2)}, u32[]{:S(2)}) collective-permute-start(bf16[4,56,1664]{2,1,0:T(8,128)(2,1)S(1)} %copy-done.59), channel_id=1, source_target_pairs={{0,8},{8,0},{16,24},{24,16},{1,9},{9,1},{17,25},{25,17},{2,10},{10... | collective-permute-start | bytes 2236424 | tf_op jit(solution)/shard_map/ppermute | solution.py:63
  54.7 49.1 %collective-permute-start.5 = (bf16[4,56,1664]{2,1,0:T(8,128)(2,1)S(1)}, bf16[4,56,1664]{2,1,0:T(8,128)(2,1)S(1)}, u32[]{:S(2)}, u32[]{:S(2)}) collective-permute-start(bf16[4,56,1664]{2,1,0:T(8,128)(2,1)S(1)} %copy-done.59), channel_id=1, source_target_pairs={{0,16},{8,24},{16,0},{24,8},{1,17},{9,25},{17,1},{25,9},{2,18},{10... | collective-permute-start | bytes 2236424 | tf_op jit(solution)/shard_map/ppermute | solution.py:63
  56.2 48.3 %collective-permute-start.6 = (bf16[4,56,1664]{2,1,0:T(8,128)(2,1)S(1)}, bf16[4,56,1664]{2,1,0:T(8,128)(2,1)S(1)}, u32[]{:S(2)}, u32[]{:S(2)}) collective-permute-start(bf16[4,56,1664]{2,1,0:T(8,128)(2,1)S(1)} %copy-done.59), channel_id=1, source_target_pairs={{0,24},{8,16},{16,8},{24,0},{1,25},{9,17},{17,9},{25,1},{2,26},{10... | collective-permute-start | bytes 2236424 | tf_op jit(solution)/shard_map/ppermute | solution.py:63
  58.7 45.0 %collective-permute-start.7 = (bf16[2,2,56,1024]{3,2,1,0:T(8,128)(2,1)S(1)}, bf16[2,2,56,1024]{3,2,1,0:T(8,128)(2,1)S(1)}, u32[]{:S(2)}, u32[]{:S(2)}) collective-permute-start(bf16[2,2,56,1024]{3,2,1,0:T(8,128)(2,1)S(1)} %pad_maximum_fusion.19), channel_id=1, source_target_pairs={{0,4},{1,5},{2,6},{3,7},{4,0},{5,1},{6,2},{7,3},{8,12},{9,13},{10,... | collective-permute-start | bytes 1376264 | tf_op jit(solution)/shard_map/ppermute | solution.py:63
  108.9 7.4 %collective-permute-start.8 = (bf16[4,4,56,1664]{3,2,1,0:T(8,128)(2,1)S(1)}, bf16[4,4,56,1664]{3,2,1,0:T(8,128)(2,1)}, u32[]{:S(2)}, u32[]{:S(2)}) collective-permute-start(bf16[4,4,56,1664]{3,2,1,0:T(8,128)(2,1)S(1)} %pad_maximum_fusion.5.same_ref), channel_id=1, source_target_pairs={{0,1},{1,0},{2,3},{3,2},{4,5},{5,4},{6,7},{7,6},{8,9},{9,8},{10,11... | collective-permute-start | bytes 8945672 | tf_op jit(solution)/shard_map/ppermute | solution.py:63
  110.3 6.0 collective-permute-start.9
  151.0 2.5 collective-permute-start.10
  154.5 38.7 %collective-permute-start.18 = (bf16[112,1024]{1,0:T(8,128)(2,1)}, bf16[112,1024]{1,0:T(8,128)(2,1)}, u32[]{:S(2)}, u32[]{:S(2)}) collective-permute-start(bf16[112,1024]{1,0:T(8,128)(2,1)} %get-tuple-element.358), channel_id=1, source_target_pairs={{0,2},{1,3},{2,0},{3,1},{4,6},{5,7},{6,4},{7,5},{8,10},{9,11},{10,... | collective-permute-start | bytes 688136 | tf_op jit(solution)/shard_map/ppermute | solution.py:63
  157.1 37.6 %collective-permute-start.19 = (bf16[112,1024]{1,0:T(8,128)(2,1)}, bf16[112,1024]{1,0:T(8,128)(2,1)}, u32[]{:S(2)}, u32[]{:S(2)}) collective-permute-start(bf16[112,1024]{1,0:T(8,128)(2,1)} %get-tuple-element.357), channel_id=1, source_target_pairs={{0,4},{1,5},{2,6},{3,7},{4,0},{5,1},{6,2},{7,3},{8,12},{9,13},{10,... | collective-permute-start | bytes 688136 | tf_op jit(solution)/shard_map/ppermute | solution.py:63
  161.7 32.9 %collective-permute-start.20 = (bf16[112,1024]{1,0:T(8,128)(2,1)}, bf16[112,1024]{1,0:T(8,128)(2,1)}, u32[]{:S(2)}, u32[]{:S(2)}) collective-permute-start(bf16[112,1024]{1,0:T(8,128)(2,1)} %get-tuple-element.356), channel_id=1, source_target_pairs={{0,6},{1,7},{2,4},{3,5},{4,2},{5,3},{6,0},{7,1},{8,14},{9,15},{10,... | collective-permute-start | bytes 688136 | tf_op jit(solution)/shard_map/ppermute | solution.py:63
  176.4 26.2 %collective-permute-start.11 = (bf16[112,1024]{1,0:T(8,128)(2,1)}, bf16[112,1024]{1,0:T(8,128)(2,1)}, u32[]{:S(2)}, u32[]{:S(2)}) collective-permute-start(bf16[112,1024]{1,0:T(8,128)(2,1)} %get-tuple-element.133), channel_id=1, source_target_pairs={{0,2},{1,3},{2,0},{3,1},{4,6},{5,7},{6,4},{7,5},{8,10},{9,11},{10,... | collective-permute-start | bytes 688136 | tf_op jit(solution)/shard_map/ppermute | solution.py:63
  177.1 27.0 %collective-permute-start.12 = (bf16[112,1024]{1,0:T(8,128)(2,1)}, bf16[112,1024]{1,0:T(8,128)(2,1)}, u32[]{:S(2)}, u32[]{:S(2)}) collective-permute-start(bf16[112,1024]{1,0:T(8,128)(2,1)} %get-tuple-element.133), channel_id=1, source_target_pairs={{0,4},{1,5},{2,6},{3,7},{4,0},{5,1},{6,2},{7,3},{8,12},{9,13},{10,... | collective-permute-start | bytes 688136 | tf_op jit(solution)/shard_map/ppermute | solution.py:63
  193.2 10.9 %collective-permute-start.13 = (bf16[112,1024]{1,0:T(8,128)(2,1)}, bf16[112,1024]{1,0:T(8,128)(2,1)S(1)}, u32[]{:S(2)}, u32[]{:S(2)}) collective-permute-start(bf16[112,1024]{1,0:T(8,128)(2,1)} %get-tuple-element.133), channel_id=1, source_target_pairs={{0,6},{1,7},{2,4},{3,5},{4,2},{5,3},{6,0},{7,1},{8,14},{9,15},{10,... | collective-permute-start | bytes 688136 | tf_op jit(solution)/shard_map/ppermute | solution.py:63
  199.6 8.6 %collective-permute-start.21 = (bf16[112,1024]{1,0:T(8,128)(2,1)S(1)}, bf16[112,1024]{1,0:T(8,128)(2,1)S(1)}, u32[]{:S(2)}, u32[]{:S(2)}) collective-permute-start(bf16[112,1024]{1,0:T(8,128)(2,1)S(1)} %bitcast.555), channel_id=1, source_target_pairs={{0,2},{1,3},{2,0},{3,1},{4,6},{5,7},{6,4},{7,5},{8,10},{9,11},{10,... | collective-permute-start | bytes 688136 | tf_op jit(solution)/shard_map/ppermute | solution.py:63
  199.7 21.9 %collective-permute-start.22 = (bf16[112,1024]{1,0:T(8,128)(2,1)S(1)}, bf16[112,1024]{1,0:T(8,128)(2,1)}, u32[]{:S(2)}, u32[]{:S(2)}) collective-permute-start(bf16[112,1024]{1,0:T(8,128)(2,1)S(1)} %bitcast.556), channel_id=1, source_target_pairs={{0,4},{1,5},{2,6},{3,7},{4,0},{5,1},{6,2},{7,3},{8,12},{9,13},{10,... | collective-permute-start | bytes 688136 | tf_op jit(solution)/shard_map/ppermute | solution.py:63
  202.6 19.0 %collective-permute-start.23 = (bf16[112,1024]{1,0:T(8,128)(2,1)S(1)}, bf16[112,1024]{1,0:T(8,128)(2,1)}, u32[]{:S(2)}, u32[]{:S(2)}) collective-permute-start(bf16[112,1024]{1,0:T(8,128)(2,1)S(1)} %bitcast.557), channel_id=1, source_target_pairs={{0,6},{1,7},{2,4},{3,5},{4,2},{5,3},{6,0},{7,1},{8,14},{9,15},{10,... | collective-permute-start | bytes 688136 | tf_op jit(solution)/shard_map/ppermute | solution.py:63
  204.1 21.3 %collective-permute-start.15 = (bf16[384,1024]{1,0:T(8,128)(2,1)}, bf16[384,1024]{1,0:T(8,128)(2,1)S(1)}, u32[]{:S(2)}, u32[]{:S(2)}) collective-permute-start(bf16[384,1024]{1,0:T(8,128)(2,1)} %get-tuple-element.134), channel_id=1, source_target_pairs={{0,8},{8,0},{16,24},{24,16},{1,9},{9,1},{17,25},{25,17},{2,10},{10... | collective-permute-start | bytes 2359304 | tf_op jit(solution)/shard_map/ppermute | solution.py:63
  204.1 34.2 %collective-permute-start.16 = (bf16[384,1024]{1,0:T(8,128)(2,1)}, bf16[384,1024]{1,0:T(8,128)(2,1)S(1)}, u32[]{:S(2)}, u32[]{:S(2)}) collective-permute-start(bf16[384,1024]{1,0:T(8,128)(2,1)} %get-tuple-element.134), channel_id=1, source_target_pairs={{0,16},{8,24},{16,0},{24,8},{1,17},{9,25},{17,1},{25,9},{2,18},{10... | collective-permute-start | bytes 2359304 | tf_op jit(solution)/shard_map/ppermute | solution.py:63
  208.2 31.9 %collective-permute-start.17 = (bf16[384,1024]{1,0:T(8,128)(2,1)}, bf16[384,1024]{1,0:T(8,128)(2,1)S(1)}, u32[]{:S(2)}, u32[]{:S(2)}) collective-permute-start(bf16[384,1024]{1,0:T(8,128)(2,1)} %get-tuple-element.134), channel_id=1, source_target_pairs={{0,24},{8,16},{16,8},{24,0},{1,25},{9,17},{17,9},{25,1},{2,26},{10... | collective-permute-start | bytes 2359304 | tf_op jit(solution)/shard_map/ppermute | solution.py:63
  221.6 19.7 %collective-permute-start.14 = (bf16[4,112,1024]{2,1,0:T(8,128)(2,1)S(1)}, bf16[4,112,1024]{2,1,0:T(8,128)(2,1)S(1)}, u32[]{:S(2)}, u32[]{:S(2)}) collective-permute-start(bf16[4,112,1024]{2,1,0:T(8,128)(2,1)S(1)} %get-tuple-element.360), channel_id=1, source_target_pairs={{0,1},{1,0},{2,3},{3,2},{4,5},{5,4},{6,7},{7,6},{8,9},{9,8},{10,11... | collective-permute-start | bytes 2752520 | tf_op jit(solution)/shard_map/ppermute | solution.py:63
  222.9 18.9 %collective-permute-start.24 = (bf16[4,112,1024]{2,1,0:T(8,128)(2,1)S(1)}, bf16[4,112,1024]{2,1,0:T(8,128)(2,1)S(1)}, u32[]{:S(2)}, u32[]{:S(2)}) collective-permute-start(bf16[4,112,1024]{2,1,0:T(8,128)(2,1)S(1)} %get-tuple-element.355), channel_id=1, source_target_pairs={{0,1},{1,0},{2,3},{3,2},{4,5},{5,4},{6,7},{7,6},{8,9},{9,8},{10,11... | collective-permute-start | bytes 2752520 | tf_op jit(solution)/shard_map/ppermute | solution.py:63
  223.9 131.4 %copy-start.11 = (bf16[640,768]{1,0:T(8,128)(2,1)}, bf16[640,768]{1,0:T(8,128)(2,1)S(1)}, u32[]{:S(2)}) copy-start(bf16[640,768]{1,0:T(8,128)(2,1)S(1)} %fusion.16.refs_1_) | copy-start | bytes 2949124
  249.9 18.2 %collective-permute-start.25 = (bf16[4,112,1024]{2,1,0:T(8,128)(2,1)}, bf16[4,112,1024]{2,1,0:T(8,128)(2,1)}, u32[]{:S(2)}, u32[]{:S(2)}) collective-permute-start(bf16[4,112,1024]{2,1,0:T(8,128)(2,1)} %slice_bitcast_fusion.2), channel_id=1, source_target_pairs={{0,1},{1,0},{2,3},{3,2},{4,5},{5,4},{6,7},{7,6},{8,9},{9,8},{10,11... | collective-permute-start | bytes 2752520 | tf_op jit(solution)/shard_map/ppermute | solution.py:63
  252.5 279.6 %reduce-scatter.8.cloned.1.call-start = ((), (), s32[]{:S(2)}) async-start(), calls=%async_computation.6 | async-start | bytes 3932160 | tf_op jit(solution)/shard_map/reduce_scatter | solution.py:806
  253.2 148.6 %copy-start.128 = (f32[8,2,56]{2,1,0:T(2,128)}, f32[8,2,56]{2,1,0:T(2,128)S(1)}, u32[]{:S(2)}) copy-start(f32[8,2,56]{2,1,0:T(2,128)S(1)} %copy.313) | copy-start | bytes 10756
  271.2 40.9 %collective-permute-start.26 = (bf16[112,1024]{1,0:T(8,128)(2,1)}, bf16[112,1024]{1,0:T(8,128)(2,1)S(1)}, u32[]{:S(2)}, u32[]{:S(2)}) collective-permute-start(bf16[112,1024]{1,0:T(8,128)(2,1)} %get-tuple-element.353), channel_id=1, source_target_pairs={{0,2},{1,3},{2,0},{3,1},{4,6},{5,7},{6,4},{7,5},{8,10},{9,11},{10,... | collective-permute-start | bytes 688136 | tf_op jit(solution)/shard_map/ppermute | solution.py:63
  276.8 35.3 %collective-permute-start.27 = (bf16[112,1024]{1,0:T(8,128)(2,1)S(1)}, bf16[112,1024]{1,0:T(8,128)(2,1)}, u32[]{:S(2)}, u32[]{:S(2)}) collective-permute-start(bf16[112,1024]{1,0:T(8,128)(2,1)S(1)} %get-tuple-element.352), channel_id=1, source_target_pairs={{0,4},{1,5},{2,6},{3,7},{4,0},{5,1},{6,2},{7,3},{8,12},{9,13},{10,... | collective-permute-start | bytes 688136 | tf_op jit(solution)/shard_map/ppermute | solution.py:63
  276.8 35.3 %collective-permute-start.28 = (bf16[112,1024]{1,0:T(8,128)(2,1)S(1)}, bf16[112,1024]{1,0:T(8,128)(2,1)}, u32[]{:S(2)}, u32[]{:S(2)}) collective-permute-start(bf16[112,1024]{1,0:T(8,128)(2,1)S(1)} %get-tuple-element.351), channel_id=1, source_target_pairs={{0,6},{1,7},{2,4},{3,5},{4,2},{5,3},{6,0},{7,1},{8,14},{9,15},{10,... | collective-permute-start | bytes 688136 | tf_op jit(solution)/shard_map/ppermute | solution.py:63
  318.3 57.6 %collective-permute-start.30 = (bf16[112,1024]{1,0:T(8,128)(2,1)}, bf16[112,1024]{1,0:T(8,128)(2,1)S(1)}, u32[]{:S(2)}, u32[]{:S(2)}) collective-permute-start(bf16[112,1024]{1,0:T(8,128)(2,1)} %convolution_convert_fusion.9.refs_16_), channel_id=1, source_target_pairs={{0,2},{1,3},{2,0},{3,1},{4,6},{5,7},{6,4},{7,5},{8,10},{9,11},{10,... | collective-permute-start | bytes 688136 | tf_op jit(solution)/shard_map/ppermute | solution.py:63
  319.4 56.5 %collective-permute-start.31 = (bf16[112,1024]{1,0:T(8,128)(2,1)}, bf16[112,1024]{1,0:T(8,128)(2,1)S(1)}, u32[]{:S(2)}, u32[]{:S(2)}) collective-permute-start(bf16[112,1024]{1,0:T(8,128)(2,1)} %convolution_convert_fusion.9.refs_16_), channel_id=1, source_target_pairs={{0,4},{1,5},{2,6},{3,7},{4,0},{5,1},{6,2},{7,3},{8,12},{9,13},{10,... | collective-permute-start | bytes 688136 | tf_op jit(solution)/shard_map/ppermute | solution.py:63
  320.2 55.7 %collective-permute-start.32 = (bf16[112,1024]{1,0:T(8,128)(2,1)}, bf16[112,1024]{1,0:T(8,128)(2,1)S(1)}, u32[]{:S(2)}, u32[]{:S(2)}) collective-permute-start(bf16[112,1024]{1,0:T(8,128)(2,1)} %convolution_convert_fusion.9.refs_16_), channel_id=1, source_target_pairs={{0,6},{1,7},{2,4},{3,5},{4,2},{5,3},{6,0},{7,1},{8,14},{9,15},{10,... | collective-permute-start | bytes 688136 | tf_op jit(solution)/shard_map/ppermute | solution.py:63
  326.1 268.4 %reduce-scatter.10.cloned.1.call-start = ((), (), s32[]{:S(2)}) async-start(), calls=%async_computation.8 | async-start | bytes 6285312
  378.1 7.0 %collective-permute-start.33 = (bf16[4,112,1024]{2,1,0:T(8,128)(2,1)S(1)}, bf16[4,112,1024]{2,1,0:T(8,128)(2,1)S(1)}, u32[]{:S(2)}, u32[]{:S(2)}) collective-permute-start(bf16[4,112,1024]{2,1,0:T(8,128)(2,1)S(1)} %get-tuple-element.350), channel_id=1, source_target_pairs={{0,1},{1,0},{2,3},{3,2},{4,5},{5,4},{6,7},{7,6},{8,9},{9,8},{10,11... | collective-permute-start | bytes 2752520 | tf_op jit(solution)/shard_map/ppermute | solution.py:63
  382.2 35.2 %collective-permute-start.29 = (bf16[4,4,24,4096]{3,2,1,0:T(8,128)(2,1)}, bf16[4,4,24,4096]{3,2,1,0:T(8,128)(2,1)}, u32[]{:S(2)}, u32[]{:S(2)}) collective-permute-start(bf16[4,4,24,4096]{3,2,1,0:T(8,128)(2,1)} %dynamic-slice_bitcast_fusion), channel_id=1, source_target_pairs={{0,1},{1,0},{2,3},{3,2},{4,5},{5,4},{6,7},{7,6},{8,9},{9,8},{10,11... | collective-permute-start | bytes 9437192 | tf_op jit(solution)/shard_map/ppermute | solution.py:63
  409.4 55.5 %collective-permute-start.37 = (bf16[4,4,32,1664]{3,2,1,0:T(8,128)(2,1)}, bf16[4,4,32,1664]{3,2,1,0:T(8,128)(2,1)S(1)}, u32[]{:S(2)}, u32[]{:S(2)}) collective-permute-start(bf16[4,4,32,1664]{3,2,1,0:T(8,128)(2,1)} %dynamic-slice_bitcast_fusion.1), channel_id=1, source_target_pairs={{0,1},{1,0},{2,3},{3,2},{4,5},{5,4},{6,7},{7,6},{8,9},{9,8},{10,11... | collective-permute-start | bytes 5111816 | tf_op jit(solution)/shard_map/ppermute | solution.py:63
  415.5 104.7 %collective-permute-start.44 = (bf16[4,112,1024]{2,1,0:T(8,128)(2,1)}, bf16[4,112,1024]{2,1,0:T(8,128)(2,1)}, u32[]{:S(2)}, u32[]{:S(2)}) collective-permute-start(bf16[4,112,1024]{2,1,0:T(8,128)(2,1)} %slice_bitcast_fusion), channel_id=1, source_target_pairs={{0,1},{1,0},{2,3},{3,2},{4,5},{5,4},{6,7},{7,6},{8,9},{9,8},{10,11... | collective-permute-start | bytes 2752520 | tf_op jit(solution)/shard_map/ppermute | solution.py:63
  423.0 41.9 %collective-permute-start.34 = (bf16[4,24,4096]{2,1,0:T(8,128)(2,1)}, bf16[4,24,4096]{2,1,0:T(8,128)(2,1)S(1)}, u32[]{:S(2)}, u32[]{:S(2)}) collective-permute-start(bf16[4,24,4096]{2,1,0:T(8,128)(2,1)} %get-tuple-element.335), channel_id=1, source_target_pairs={{0,8},{8,0},{16,24},{24,16},{1,9},{9,1},{17,25},{25,17},{2,10},{10... | collective-permute-start | bytes 2359304 | tf_op jit(solution)/shard_map/ppermute | solution.py:63
  424.8 40.1 %collective-permute-start.35 = (bf16[4,24,4096]{2,1,0:T(8,128)(2,1)}, bf16[4,24,4096]{2,1,0:T(8,128)(2,1)S(1)}, u32[]{:S(2)}, u32[]{:S(2)}) collective-permute-start(bf16[4,24,4096]{2,1,0:T(8,128)(2,1)} %get-tuple-element.334), channel_id=1, source_target_pairs={{0,16},{8,24},{16,0},{24,8},{1,17},{9,25},{17,1},{25,9},{2,18},{10... | collective-permute-start | bytes 2359304 | tf_op jit(solution)/shard_map/ppermute | solution.py:63
  428.2 36.7 %collective-permute-start.36 = (bf16[4,24,4096]{2,1,0:T(8,128)(2,1)}, bf16[4,24,4096]{2,1,0:T(8,128)(2,1)}, u32[]{:S(2)}, u32[]{:S(2)}) collective-permute-start(bf16[4,24,4096]{2,1,0:T(8,128)(2,1)} %get-tuple-element.333), channel_id=1, source_target_pairs={{0,24},{8,16},{16,8},{24,0},{1,25},{9,17},{17,9},{25,1},{2,26},{10... | collective-permute-start | bytes 2359304 | tf_op jit(solution)/shard_map/ppermute | solution.py:63
  470.1 27.4 %collective-permute-start.39 = (bf16[4,32,1664]{2,1,0:T(8,128)(2,1)}, bf16[4,32,1664]{2,1,0:T(8,128)(2,1)S(1)}, u32[]{:S(2)}, u32[]{:S(2)}) collective-permute-start(bf16[4,32,1664]{2,1,0:T(8,128)(2,1)} %get-tuple-element.340), channel_id=1, source_target_pairs={{0,8},{8,0},{16,24},{24,16},{1,9},{9,1},{17,25},{25,17},{2,10},{10... | collective-permute-start | bytes 1277960 | tf_op jit(solution)/shard_map/ppermute | solution.py:63
  470.7 26.8 %collective-permute-start.40 = (bf16[4,32,1664]{2,1,0:T(8,128)(2,1)S(1)}, bf16[4,32,1664]{2,1,0:T(8,128)(2,1)S(1)}, u32[]{:S(2)}, u32[]{:S(2)}) collective-permute-start(bf16[4,32,1664]{2,1,0:T(8,128)(2,1)S(1)} %get-tuple-element.339), channel_id=1, source_target_pairs={{0,16},{8,24},{16,0},{24,8},{1,17},{9,25},{17,1},{25,9},{2,18},{10... | collective-permute-start | bytes 1277960 | tf_op jit(solution)/shard_map/ppermute | solution.py:63
  472.2 26.1 %collective-permute-start.41 = (bf16[4,32,1664]{2,1,0:T(8,128)(2,1)S(1)}, bf16[4,32,1664]{2,1,0:T(8,128)(2,1)}, u32[]{:S(2)}, u32[]{:S(2)}) collective-permute-start(bf16[4,32,1664]{2,1,0:T(8,128)(2,1)S(1)} %get-tuple-element.338), channel_id=1, source_target_pairs={{0,24},{8,16},{16,8},{24,0},{1,25},{9,17},{17,9},{25,1},{2,26},{10... | collective-permute-start | bytes 1277960 | tf_op jit(solution)/shard_map/ppermute | solution.py:63
  476.4 21.2 %collective-permute-start.38 = (bf16[2,24,4096]{2,1,0:T(8,128)(2,1)}, bf16[2,24,4096]{2,1,0:T(8,128)(2,1)S(1)}, u32[]{:S(2)}, u32[]{:S(2)}) collective-permute-start(bf16[2,24,4096]{2,1,0:T(8,128)(2,1)} %dynamic-slice_bitcast_fusion.9), channel_id=1, source_target_pairs={{0,2},{1,3},{2,0},{3,1},{4,6},{5,7},{6,4},{7,5},{8,10},{9,11},{10,... | collective-permute-start | bytes 1179656 | tf_op jit(solution)/shard_map/ppermute | solution.py:63
  500.7 24.2 %collective-permute-start.43 = (bf16[2,32,1664]{2,1,0:T(8,128)(2,1)S(1)}, bf16[2,32,1664]{2,1,0:T(8,128)(2,1)S(1)}, u32[]{:S(2)}, u32[]{:S(2)}) collective-permute-start(bf16[2,32,1664]{2,1,0:T(8,128)(2,1)S(1)} %dynamic-slice_bitcast_fusion.13), channel_id=1, source_target_pairs={{0,2},{1,3},{2,0},{3,1},{4,6},{5,7},{6,4},{7,5},{8,10},{9,11},{10,... | collective-permute-start | bytes 638984 | tf_op jit(solution)/shard_map/ppermute | solution.py:63
  501.9 23.0 %collective-permute-start.42 = (bf16[1,24,4096]{2,1,0:T(8,128)(2,1)S(1)}, bf16[1,24,4096]{2,1,0:T(8,128)(2,1)S(1)}, u32[]{:S(2)}, u32[]{:S(2)}) collective-permute-start(bf16[1,24,4096]{2,1,0:T(8,128)(2,1)S(1)} %constant_dynamic-slice_fusion.2), channel_id=1, source_target_pairs={{0,4},{1,5},{2,6},{3,7},{4,0},{5,1},{6,2},{7,3},{8,12},{9,13},{10,... | collective-permute-start | bytes 589832 | tf_op jit(solution)/shard_map/ppermute | solution.py:63
  520.2 20.2 %collective-permute-start.49 = (bf16[4,4,24,1536]{3,2,1,0:T(8,128)(2,1)}, bf16[4,4,24,1536]{3,2,1,0:T(8,128)(2,1)}, u32[]{:S(2)}, u32[]{:S(2)}) collective-permute-start(bf16[4,4,24,1536]{3,2,1,0:T(8,128)(2,1)} %dynamic-slice_bitcast_fusion.2), channel_id=1, source_target_pairs={{0,1},{1,0},{2,3},{3,2},{4,5},{5,4},{6,7},{7,6},{8,9},{9,8},{10,11... | collective-permute-start | bytes 3538952 | tf_op jit(solution)/shard_map/ppermute | solution.py:63
  527.3 13.1 %collective-permute-start.48 = (bf16[1,32,1664]{2,1,0:T(8,128)(2,1)S(1)}, bf16[1,32,1664]{2,1,0:T(8,128)(2,1)S(1)}, u32[]{:S(2)}, u32[]{:S(2)}) collective-permute-start(bf16[1,32,1664]{2,1,0:T(8,128)(2,1)S(1)} %constant_dynamic-slice_fusion.1), channel_id=1, source_target_pairs={{0,4},{1,5},{2,6},{3,7},{4,0},{5,1},{6,2},{7,3},{8,12},{9,13},{10,... | collective-permute-start | bytes 319496 | tf_op jit(solution)/shard_map/ppermute | solution.py:63
  535.8 54.8 %all-to-all-start.1 = ((bf16[8,32,1024]{2,1,0:T(8,128)(2,1)}), bf16[8,32,1024]{2,1,0:T(8,128)(2,1)}, u32[]{:S(2)}, u32[]{:S(2)}) async-start(bf16[8,32,1024]{2,1,0:T(8,128)(2,1)} %bitcast.216), calls=%async_computation.3 | async-start | bytes 1048576 | tf_op jit(solution)/shard_map/all_to_all | solution.py:903
  545.6 25.3 %collective-permute-start.50 = (bf16[4,24,1536]{2,1,0:T(8,128)(2,1)}, bf16[4,24,1536]{2,1,0:T(8,128)(2,1)}, u32[]{:S(2)}, u32[]{:S(2)}) collective-permute-start(bf16[4,24,1536]{2,1,0:T(8,128)(2,1)} %get-tuple-element.343), channel_id=1, source_target_pairs={{0,8},{8,0},{16,24},{24,16},{1,9},{9,1},{17,25},{25,17},{2,10},{10... | collective-permute-start | bytes 884744 | tf_op jit(solution)/shard_map/ppermute | solution.py:63
  546.8 24.9 %collective-permute-start.51 = (bf16[4,24,1536]{2,1,0:T(8,128)(2,1)}, bf16[4,24,1536]{2,1,0:T(8,128)(2,1)}, u32[]{:S(2)}, u32[]{:S(2)}) collective-permute-start(bf16[4,24,1536]{2,1,0:T(8,128)(2,1)} %get-tuple-element.342), channel_id=1, source_target_pairs={{0,16},{8,24},{16,0},{24,8},{1,17},{9,25},{17,1},{25,9},{2,18},{10... | collective-permute-start | bytes 884744 | tf_op jit(solution)/shard_map/ppermute | solution.py:63
  546.8 24.9 %collective-permute-start.52 = (bf16[4,24,1536]{2,1,0:T(8,128)(2,1)}, bf16[4,24,1536]{2,1,0:T(8,128)(2,1)}, u32[]{:S(2)}, u32[]{:S(2)}) collective-permute-start(bf16[4,24,1536]{2,1,0:T(8,128)(2,1)} %get-tuple-element.341), channel_id=1, source_target_pairs={{0,24},{8,16},{16,8},{24,0},{1,25},{9,17},{17,9},{25,1},{2,26},{10... | collective-permute-start | bytes 884744 | tf_op jit(solution)/shard_map/ppermute | solution.py:63
  550.0 24.4 %collective-permute-start.45 = (bf16[112,1024]{1,0:T(8,128)(2,1)}, bf16[112,1024]{1,0:T(8,128)(2,1)}, u32[]{:S(2)}, u32[]{:S(2)}) collective-permute-start(bf16[112,1024]{1,0:T(8,128)(2,1)} %get-tuple-element.346), channel_id=1, source_target_pairs={{0,2},{1,3},{2,0},{3,1},{4,6},{5,7},{6,4},{7,5},{8,10},{9,11},{10,... | collective-permute-start | bytes 688136 | tf_op jit(solution)/shard_map/ppermute | solution.py:63
  552.8 21.6 %collective-permute-start.46 = (bf16[112,1024]{1,0:T(8,128)(2,1)}, bf16[112,1024]{1,0:T(8,128)(2,1)}, u32[]{:S(2)}, u32[]{:S(2)}) collective-permute-start(bf16[112,1024]{1,0:T(8,128)(2,1)} %get-tuple-element.348), channel_id=1, source_target_pairs={{0,4},{1,5},{2,6},{3,7},{4,0},{5,1},{6,2},{7,3},{8,12},{9,13},{10,... | collective-permute-start | bytes 688136 | tf_op jit(solution)/shard_map/ppermute | solution.py:63
  570.9 9.9 %collective-permute-start.47 = (bf16[112,1024]{1,0:T(8,128)(2,1)S(1)}, bf16[112,1024]{1,0:T(8,128)(2,1)S(1)}, u32[]{:S(2)}, u32[]{:S(2)}) collective-permute-start(bf16[112,1024]{1,0:T(8,128)(2,1)S(1)} %copy-done.110), channel_id=1, source_target_pairs={{0,6},{1,7},{2,4},{3,5},{4,2},{5,3},{6,0},{7,1},{8,14},{9,15},{10,... | collective-permute-start | bytes 688136 | tf_op jit(solution)/shard_map/ppermute | solution.py:63
  573.2 9.1 %collective-permute-start.53 = (bf16[2,24,1536]{2,1,0:T(8,128)(2,1)S(1)}, bf16[2,24,1536]{2,1,0:T(8,128)(2,1)S(1)}, u32[]{:S(2)}, u32[]{:S(2)}) collective-permute-start(bf16[2,24,1536]{2,1,0:T(8,128)(2,1)S(1)} %dynamic-slice_bitcast_fusion.14), channel_id=1, source_target_pairs={{0,2},{1,3},{2,0},{3,1},{4,6},{5,7},{6,4},{7,5},{8,10},{9,11},{10,... | collective-permute-start | bytes 442376 | tf_op jit(solution)/shard_map/ppermute | solution.py:63
  582.4 6.1 %collective-permute-start.54 = (bf16[1,24,1536]{2,1,0:T(8,128)(2,1)S(1)}, bf16[1,24,1536]{2,1,0:T(8,128)(2,1)S(1)}, u32[]{:S(2)}, u32[]{:S(2)}) collective-permute-start(bf16[1,24,1536]{2,1,0:T(8,128)(2,1)S(1)} %constant_dynamic-slice_fusion), channel_id=1, source_target_pairs={{0,4},{1,5},{2,6},{3,7},{4,0},{5,1},{6,2},{7,3},{8,12},{9,13},{10,... | collective-permute-start | bytes 221192 | tf_op jit(solution)/shard_map/ppermute | solution.py:63
  (151 other events, 914.9 us)
Sparse Core Ops, SparseCore 0:
  11.5 127.5 all-gather.2
  252.6 39.9 reduce-scatter.5
  326.2 41.1 reduce-scatter.7
  448.6 130.5 reduce-scatter.9

commit v4 on v3

--- a/solution.py
+++ b/solution.py
@@ -731,6 +731,7 @@
     first, seg_all, cols = fetch(first, action_in, dp, line, beside)
     cols = cols.transpose(0, 2, 1, 3).reshape(n * rows_a, 2 * part)
     hidden_w = jnp.concatenate([cols, act_down.reshape(-1, 2 * part)], axis=0)
+    hidden_w = lax.all_gather(hidden_w, "dp", axis=0)
     dy_own = grad_action.astype(BF).reshape(block, wide)
     act_a = first[:, :rows_a].reshape(total * rows_a, -1)
     pre_a = first[:, rows_a:].reshape(total * gap, -1)
@@ -768,9 +769,7 @@
     oa, lse_a = own_attend(seg_qkv, qkv, own, lens, heads, seg_len)
 
     oa = line.home(oa.reshape(n, block, hq))
-    hidden_w, dy_own = after([hidden_w, dy_own], oa)
-    hidden_w = jnp.stack([hidden_w] + [dp.across(hidden_w, k) for k in range(1, groups)])
-    hidden_w = turned(hidden_w, dp.me)
+    (dy_own,) = after([dy_own], oa)
     dy_all = line.around(dy_own).reshape(-1, wide)
     gu_w = hidden_w[:, : n * rows_a].reshape(-1, 2 * part)
     down_w = hidden_w[:, n * rows_a :].reshape(part, wide)
@@ -783,7 +782,11 @@
     an2, as2 = normed(a1)
     ah2 = (an2 * suf_midgain * mod2).astype(BF).reshape(block, wide)
 
-    h_all = line.around(ah2).reshape(n * block, wide)
+    pre_gu = dot(spread, second[..., : 2 * ff].reshape(total * gap, -1)).astype(BF)
+    fold = tiles(second[..., 2 * ff : cut], gap, fold.shape).reshape(total, -1, width)
+    pre_mixer = fold[:, :rows_m].reshape(hq, width)
+    pre_down = fold[:, rows_m:].reshape(ff, width)
+    h_all = line.around(ah2, (pre_gu, pre_mixer, pre_down)).reshape(n * block, wide)
     gu = dot(h_all, gu_w)
     gate_a, up_a = gu[:, :part], gu[:, part:]
     act_g, slope_g = gelu_parts(gate_a)
@@ -805,10 +808,6 @@
     dff = dff.reshape(-1, 2 * part)
     dff = lax.psum_scatter(dff, "dp", scatter_dimension=0, tiled=True)
 
-    pre_gu = dot(spread, second[..., : 2 * ff].reshape(total * gap, -1)).astype(BF)
-    fold = tiles(second[..., 2 * ff : cut], gap, fold.shape).reshape(total, -1, width)
-    pre_mixer = fold[:, :rows_m].reshape(hq, width)
-    pre_down = fold[:, rows_m:].reshape(ff, width)
     cot = cot_prefix.reshape(micro * prefix, width)
 
     def feed_half(step, outs, gate):

time: 608 us -> 603 us (level); the launches traced: 605 us -> 593 us
  waiting for transfers between devices: 102 us -> 82.8 us
  starting transfers between devices: 88.6 us -> 81.2 us
  local copies, waits for them, and re-layouts: 95.7 us -> 103 us
    ppermute x55 -> x52, waiting for transfers between devices: 102 us -> 82.7 us  [across(): lax.ppermute(x, self.axes, [(i, i ^ mask) for i in range(self.count)])]
    ppermute x55 -> x52, starting transfers between devices: 78.4 us -> 70.9 us  [across(): lax.ppermute(x, self.axes, [(i, i ^ mask) for i in range(self.count)])]
    unnamed x317 -> x321, local copies, waits for them, and re-layouts: 40 us -> 46.5 us
  transfers between devices with their start and end apart: 61 -> 59, of which waited for: 13 -> 13; matrix products, arithmetic and copies ran while one was open for 31% -> 32% of each run, Pallas kernels for 27% -> 27%
where the time goes in v4:
time: 603 us; the launch traced here: 593 us
  Pallas kernels  164 us (27%)
  local copies, waits for them, and re-layouts  103 us (17%)
  other arithmetic  88.9 us (15%)
  waiting for transfers between devices  82.8 us (14%)
  starting transfers between devices  81.2 us (13%)
  matrix products  56.7 us (9%)
  between operations  16.6 us (3%)
    ppermute x52, waiting for transfers between devices, across(): lax.ppermute(x, self.axes, [(i, i ^ mask) for i in range(self.count)])  82.7 us
    ppermute x52, starting transfers between devices, across(): lax.ppermute(x, self.axes, [(i, i ^ mask) for i in range(self.count)])  70.9 us
    pallas_call x2, Pallas kernels, feed(): pl.pallas_call(kernel, grid=(chunks,), in_specs=[row(hq), row(width), row...  58.2 us
    unnamed x321, local copies, waits for them, and re-layouts  46.5 us
    pallas_call x4, Pallas kernels, weight_grad(): pl.pallas_call(chained(kernel, 1 + len(extra) + len(grads), len(gate)), g...  42.4 us
    pallas_call x2, Pallas kernels, attend_back(): pl.pallas_call(chained(kernel, 6, len(before) + len(gate)), grid_spec=plt...  28.4 us
    dot_general x7, matrix products, dot(): lax.dot_general(a, b, (((1,), (0,)), ((), ())), preferred_element_type=F32)  22.5 us
    pallas_call x2, Pallas kernels, attend(): pl.pallas_call(chained(kernel, 4, len(before) + len(gate)), grid_spec=plt...  22.3 us
  transfers between devices with their start and end apart: 59, of which 13 were waited for; matrix products, arithmetic and copies ran while one was open for 32% of the time, Pallas kernels for 27%

profile of v4, /device:TPU:0, one launch (start us, length us, event | category | flops | bytes accessed | tf_op | source)
XLA Modules:
  0.0 593.1 jit_solution(11116602211653281674)
XLA Ops:
  15.9 3.1 collective-permute-start
  18.9 2.6 collective-permute-start.1
  28.6 10.8 %collective-permute-done.1.refs_1_ = bf16[56,1664]{1,0:T(8,128)(2,1)S(1)} collective-permute-done((bf16[56,1664]{1,0:T(8,128)(2,1)S(1)}, bf16[56,1664]{1,0:T(8,128)(2,1)S(1)}, u32[]{:S(2)}, u32[]{:S(2)}) %collective-permute-start.1) | collective-permute-done | bytes 186400 | tf_op jit(solution)/shard_map/ppermute | solution.py:63
  39.5 5.1 collective-permute-done.3.refs_3_
  45.3 2.3 fusion.102
  47.6 5.4 all-to-all-start
  58.7 2.9 collective-permute-start.7
  61.7 42.2 %collective-permute-done.7.refs_3_ = bf16[2,2,56,1024]{3,2,1,0:T(8,128)(2,1)S(1)} collective-permute-done((bf16[2,2,56,1024]{3,2,1,0:T(8,128)(2,1)S(1)}, bf16[2,2,56,1024]{3,2,1,0:T(8,128)(2,1)S(1)}, u32[]{:S(2)}, u32[]{:S(2)}) %collective-permute-start.7) | collective-permute-done | bytes 458784 | tf_op jit(solution)/shard_map/ppermute | solution.py:63
  109.3 2.7 fusion.101
  116.7 5.5 settle.1
  122.1 2.5 slice.325
  128.7 3.4 slice.322
  135.9 3.4 convolution_convert_fusion.2
  139.5 4.6 convolution_convert_fusion.3
  145.1 4.4 convolution_convert_fusion
  149.5 2.5 own_attend.1
  157.7 2.3 collective-permute-start.13
  163.4 3.7 collective-permute-done.11
  167.1 3.5 collective-permute-start.17
  172.3 10.9 %attend.2 = (bf16[2,816,1024]{2,1,0:T(8,128)(2,1)S(1)}, f32[2,4,1,816]{3,2,1,0:T(1,128)S(1)}) custom-call(s32[2]{0:T(128)S(1)} %fusion.98.refs_0_.refs_1_, bf16[2,816,1536]{2,1,0:T(8,128)(2,1)} %bitcast.437, bf16[2,816,1536]{2,1,0:T(8,128)(2,1)} %bitcast.438, bf16[2,816,1536]{2,1,0:T(8,128)(2,1)} %bitcast.439, bf16[8,2,56,1536]{3,2,1,0:T(8,128)(2,1)S(1)} %bitcast.455), custom_call_target="tpu_custom_call" | custom-call | flops 2727346 | bytes 5013 | tf_op jit(solution)/shard_map/attend/pallas_call | solution.py:265
  183.3 11.4 %attend.3 = (bf16[2,816,1024]{2,1,0:T(8,128)(2,1)S(1)}, f32[2,4,1,816]{3,2,1,0:T(1,128)S(1)}) custom-call(s32[2]{0:T(128)S(1)} %fusion.98.refs_0_.refs_1_, bf16[2,816,1536]{2,1,0:T(8,128)(2,1)} %bitcast.440, bf16[2,816,1536]{2,1,0:T(8,128)(2,1)} %bitcast.441, bf16[2,816,1536]{2,1,0:T(8,128)(2,1)} %bitcast.442, ...), custom_call_target="tpu_custom_call", output_to_operand_aliasing={{0}: (4, {}), {1}: (5, {})} | custom-call | flops 2727346 | bytes 5013 | tf_op jit(solution)/shard_map/attend/pallas_call | solution.py:265
  203.9 3.6 collective-permute-start.18
  207.5 2.4 collective-permute-start.20
  210.0 3.2 slice.338
  213.2 5.9 convolution_convert_fusion.1.refs_3_.refs_5_.refs_6_
  219.1 2.4 slice.335
  227.0 2.5 fusion.104
  238.7 2.5 fusion.110
  241.2 3.4 multiply_convert_fusion.6
  248.0 3.6 convolution_convert_fusion.7
  259.0 4.0 collective-permute-start.23
  263.0 2.4 collective-permute-start.25
  265.4 3.8 convolution_convert_fusion.4
  269.2 29.0 %feed.2 = (bf16[1632,640]{1,0:T(8,128)(2,1)}, f32[1632,640]{1,0:T(8,128)}, bf16[1632,640]{1,0:T(8,128)(2,1)}, bf16[1632,1024]{1,0:T(8,128)(2,1)}, bf16[1632,640]...) custom-call(bf16[1632,1024]{1,0:T(8,128)(2,1)} %bitcast.451, ...), custom_call_target="tpu_custom_call" | custom-call | flops 14973665 | bytes 21233 | tf_op jit(solution)/shard_map/feed/pallas_call | solution.py:410
  304.7 2.5 collective-permute-start.29
  310.5 29.2 %feed.3 = (bf16[1632,640]{1,0:T(8,128)(2,1)}, f32[1632,640]{1,0:T(8,128)}, bf16[1632,640]{1,0:T(8,128)(2,1)}, bf16[1632,1024]{1,0:T(8,128)(2,1)}, bf16[1632,640]...) custom-call(bf16[1632,1024]{1,0:T(8,128)(2,1)} %bitcast.452, ...), custom_call_target="tpu_custom_call", output_to_operand_aliasing={{0}: (8, {}), {1}: (9, {}), {2}: (10, {}), {3}: (11, {}), {... | custom-call | flops 14973665 | bytes 21233 | tf_op jit(solution)/shard_map/feed/pallas_call | solution.py:410
  341.4 18.9 %weight_grad.4.refs_1_ = bf16[768,4096]{1,0:T(8,128)(2,1)} custom-call(bf16[1632,640]{1,0:T(8,128)(2,1)S(1)} %copy-done.16, bf16[640,768]{1,0:T(8,128)(2,1)S(1)} %fusion.16.refs_1_, bf16[1632,2048]{1,0:T(8,128)(2,1)} %get-tuple-element.157.refs_2_, bf16[1632,2048]{1,0:T(8,128)(2,1)} %get-tuple-element.158.refs_3_), custom_call_target="tpu_custom_call" | custom-call | flops 10267656 | bytes 15876 | tf_op jit(solution)/shard_map/weight_grad/pallas_call | solution.py:481
  363.3 3.9 dynamic-slice_bitcast_fusion
  373.6 2.4 copy-done.3
  377.5 2.9 own_back.1
  380.5 5.3 multiply_reduce_fusion.1
  386.7 5.9 bitcast_convert_fusion
  401.1 4.0 fusion.1.refs_2_
  407.5 6.6 %collective-permute-start.31 = (bf16[4,24,4096]{2,1,0:T(8,128)(2,1)}, bf16[4,24,4096]{2,1,0:T(8,128)(2,1)S(1)}, u32[]{:S(2)}, u32[]{:S(2)}) collective-permute-start(bf16[4,24,4096]{2,1,0:T(8,128)(2,1)} %get-tuple-element.337), channel_id=1, source_target_pairs={{0,8},{8,0},{16,24},{24,16},{1,9},{9,1},{17,25},{25,17},{2,10},{10... | collective-permute-start | bytes 2359304 | tf_op jit(solution)/shard_map/ppermute | solution.py:63
  415.6 5.1 weight_grad.5
  420.7 8.8 %weight_grad.6 = bf16[2048,640]{1,0:T(8,128)(2,1)S(1)} custom-call(bf16[1632,2048]{1,0:T(8,128)(2,1)} %get-tuple-element.164.refs_0_, bf16[1632,640]{1,0:T(8,128)(2,1)S(1)} %bitcast.459, bf16[4,4,24,4096]{3,2,1,0:T(8,128)(2,1)} %copy-done.32, bf16[1024,1664]{1,0:T(8,128)(2,1)} %copy-done.27), custom_call_target="tpu_custom_call" | custom-call | flops 4278190 | bytes 8773 | tf_op jit(solution)/shard_map/weight_grad/pallas_call | solution.py:481
  431.1 3.2 pad_maximum_fusion.refs_6_
  434.4 14.0 %attend_back.2 = (bf16[2,816,1024]{2,1,0:T(8,128)(2,1)}, f32[2,816,256]{2,1,0:T(8,128)S(1)}, f32[2,816,256]{2,1,0:T(8,128)S(1)}) custom-call(s32[2]{0:T(128)S(1)} %fusion.98.refs_0_.refs_1_, bf16[2,816,1536]{2,1,0:T(8,128)(2,1)} %bitcast.443, bf16[2,816,1536]{2,1,0:T(8,128)(2,1)} %bitcast.444, bf16[2,816,1536]{2,1,0:T(8,128)(2,1)} %bitcast.445, ...), custom_call_target="tpu_custom_call" | custom-call | flops 6818365 | bytes 12533 | tf_op jit(solution)/shard_map/attend_back/pallas_call | solution.py:322
  452.2 2.5 fusion.9.refs_10_
  461.8 4.7 collective-permute-start.35
  466.5 14.4 %attend_back.3 = (bf16[2,816,1024]{2,1,0:T(8,128)(2,1)}, f32[2,816,256]{2,1,0:T(8,128)S(1)}, f32[2,816,256]{2,1,0:T(8,128)S(1)}) custom-call(s32[2]{0:T(128)S(1)} %fusion.98.refs_0_.refs_1_, bf16[2,816,1536]{2,1,0:T(8,128)(2,1)} %bitcast.446, bf16[2,816,1536]{2,1,0:T(8,128)(2,1)} %bitcast.447, ...), custom_call_target="tpu_custom_call", output_to_operand_aliasing={{0}: (6, {}), {1}: (7, {}), {2}: (8, {})} | custom-call | flops 6818365 | bytes 12533 | tf_op jit(solution)/shard_map/attend_back/pallas_call | solution.py:322
  483.7 2.6 pad_maximum_fusion.1
  490.7 9.6 %weight_grad.7.refs_3_.refs_2_.refs_1_ = bf16[768,1536]{1,0:T(8,128)(2,1)} custom-call(bf16[1632,640]{1,0:T(8,128)(2,1)S(1)} %copy-done.15, bf16[640,768]{1,0:T(8,128)(2,1)S(1)} %copy-done.12, bf16[1632,1536]{1,0:T(8,128)(2,1)} %bitcast.479, bf16[2,24,4096]{2,1,0:T(8,128)(2,1)S(1)} %fusion.40.refs_3_, bf16[4,32,1664]{2,1,0:T(8,128)(2,1)S(1)} %fusion.39.refs_4_), custom_call_target="tpu_custom_call" | custom-call | flops 3850371 | bytes 7520 | tf_op jit(solution)/shard_map/weight_grad/pallas_call | solution.py:481
  500.3 2.4 dynamic-slice_bitcast_fusion.2
  502.8 8.2 %collective-permute-done.39.refs_0_ = bf16[1,24,4096]{2,1,0:T(8,128)(2,1)S(1)} collective-permute-done((bf16[1,24,4096]{2,1,0:T(8,128)(2,1)S(1)}, bf16[1,24,4096]{2,1,0:T(8,128)(2,1)S(1)}, u32[]{:S(2)}, u32[]{:S(2)}) %collective-permute-start.39) | collective-permute-done | bytes 196640 | tf_op jit(solution)/shard_map/ppermute | solution.py:63
  515.4 2.3 fusion.34.refs_1_.refs_2_
  521.9 4.5 all-to-all-start.1
  532.5 2.6 collective-permute-start.47
  535.1 2.2 collective-permute-start.48
  540.3 2.4 collective-permute-start.43
  542.7 8.8 %multiply_reduce_fusion = (f32[1632]{0:T(1024)S(1)}, f32[1632,640]{1,0:T(8,128)}) fusion(bf16[1632,640]{1,0:T(8,128)(2,1)S(1)} %bitcast.478, f32[640]{0:T(1024)S(1)} %copy-done.133, f32[1632]{0:T(1024)S(1)} %copy-done.135, bf16[1632,1536]{1,0:T(8,128)(2,1)} %get-tuple-element.182, bf16[640,1664]{1,0:T(8,128)(2,1)S(1)} %copy-done.129), kind=kOutput, calls=%fused_computation.16 | convolution fusion | flops 3213863424 | bytes 13265280 | tf_op jit(solution)/shard_map/dot_general | solution.py:45
  552.5 5.4 fusion.6
  561.7 7.3 %collective-permute-done.44 = bf16[112,1024]{1,0:T(8,128)(2,1)S(1)} collective-permute-done((bf16[112,1024]{1,0:T(8,128)(2,1)S(1)}, bf16[112,1024]{1,0:T(8,128)(2,1)S(1)}, u32[]{:S(2)}, u32[]{:S(2)}) %collective-permute-start.44) | collective-permute-done | bytes 229408 | tf_op jit(solution)/shard_map/ppermute | solution.py:63
  570.5 2.5 collective-permute-start.51
  (609 shorter events, 177.2 us)
Async XLA Ops:
  7.2 105.9 %copy-start = (s32[2,8]{1,0:T(2,128)S(1)}, s32[2,8]{1,0:T(2,128)}, u32[]{:S(2)}) copy-start(s32[2,8]{1,0:T(2,128)} %param.36) | copy-start | bytes 196
  7.2 192.5 %all-gather.5.cloned.1.call-start = ((), (), s32[]{:S(2)}) async-start(), calls=%async_computation.7 | async-start | bytes 12773376 | tf_op jit(solution)/shard_map/all_gather | solution.py:722
  15.9 12.7 %collective-permute-start = (bf16[56,1664]{1,0:T(8,128)(2,1)S(1)}, bf16[56,1664]{1,0:T(8,128)(2,1)S(1)}, u32[]{:S(2)}, u32[]{:S(2)}) collective-permute-start(bf16[56,1664]{1,0:T(8,128)(2,1)S(1)} %fusion.67), channel_id=1, source_target_pairs={{0,2},{1,3},{2,0},{3,1},{4,6},{5,7},{6,4},{7,5},{8,10},{9,11},{10,... | collective-permute-start | bytes 559112 | tf_op jit(solution)/shard_map/ppermute | solution.py:63
  18.9 20.5 %collective-permute-start.1 = (bf16[56,1664]{1,0:T(8,128)(2,1)S(1)}, bf16[56,1664]{1,0:T(8,128)(2,1)S(1)}, u32[]{:S(2)}, u32[]{:S(2)}) collective-permute-start(bf16[56,1664]{1,0:T(8,128)(2,1)S(1)} %fusion.67), channel_id=1, source_target_pairs={{0,4},{1,5},{2,6},{3,7},{4,0},{5,1},{6,2},{7,3},{8,12},{9,13},{10,... | collective-permute-start | bytes 559112 | tf_op jit(solution)/shard_map/ppermute | solution.py:63
  21.5 18.0 %collective-permute-start.2 = (bf16[56,1664]{1,0:T(8,128)(2,1)S(1)}, bf16[56,1664]{1,0:T(8,128)(2,1)S(1)}, u32[]{:S(2)}, u32[]{:S(2)}) collective-permute-start(bf16[56,1664]{1,0:T(8,128)(2,1)S(1)} %fusion.67), channel_id=1, source_target_pairs={{0,6},{1,7},{2,4},{3,5},{4,2},{5,3},{6,0},{7,1},{8,14},{9,15},{10,... | collective-permute-start | bytes 559112 | tf_op jit(solution)/shard_map/ppermute | solution.py:63
  25.3 19.3 %collective-permute-start.3 = (bf16[2,56,1024]{2,1,0:T(8,128)(2,1)S(1)}, bf16[2,56,1024]{2,1,0:T(8,128)(2,1)S(1)}, u32[]{:S(2)}, u32[]{:S(2)}) collective-permute-start(bf16[2,56,1024]{2,1,0:T(8,128)(2,1)S(1)} %pad_maximum_fusion.19), channel_id=1, source_target_pairs={{0,2},{1,3},{2,0},{3,1},{4,6},{5,7},{6,4},{7,5},{8,10},{9,11},{10,... | collective-permute-start | bytes 688136 | tf_op jit(solution)/shard_map/ppermute | solution.py:63
  47.6 57.0 %all-to-all-start = ((bf16[8,2,32,512]{3,2,1,0:T(8,128)(2,1)}), bf16[8,2,32,512]{3,2,1,0:T(8,128)(2,1)S(1)}, u32[]{:S(2)}, u32[]{:S(2)}) async-start(bf16[8,2,32,512]{3,2,1,0:T(8,128)(2,1)} %after.19), calls=%async_computation | async-start | bytes 1048576 | tf_op jit(solution)/shard_map/all_to_all | solution.py:728
  53.1 176.5 %all-gather.7.cloned.1.call-start = ((), (), s32[]{:S(2)}) async-start(), calls=%async_computation.8 | async-start | bytes 3932160 | tf_op jit(solution)/shard_map/all_gather | solution.py:734
  53.1 50.7 %collective-permute-start.4 = (bf16[4,56,1664]{2,1,0:T(8,128)(2,1)S(1)}, bf16[4,56,1664]{2,1,0:T(8,128)(2,1)S(1)}, u32[]{:S(2)}, u32[]{:S(2)}) collective-permute-start(bf16[4,56,1664]{2,1,0:T(8,128)(2,1)S(1)} %copy-done.60), channel_id=1, source_target_pairs={{0,8},{8,0},{16,24},{24,16},{1,9},{9,1},{17,25},{25,17},{2,10},{10... | collective-permute-start | bytes 2236424 | tf_op jit(solution)/shard_map/ppermute | solution.py:63
  54.7 49.2 %collective-permute-start.5 = (bf16[4,56,1664]{2,1,0:T(8,128)(2,1)S(1)}, bf16[4,56,1664]{2,1,0:T(8,128)(2,1)S(1)}, u32[]{:S(2)}, u32[]{:S(2)}) collective-permute-start(bf16[4,56,1664]{2,1,0:T(8,128)(2,1)S(1)} %copy-done.60), channel_id=1, source_target_pairs={{0,16},{8,24},{16,0},{24,8},{1,17},{9,25},{17,1},{25,9},{2,18},{10... | collective-permute-start | bytes 2236424 | tf_op jit(solution)/shard_map/ppermute | solution.py:63
  56.2 48.4 %collective-permute-start.6 = (bf16[4,56,1664]{2,1,0:T(8,128)(2,1)S(1)}, bf16[4,56,1664]{2,1,0:T(8,128)(2,1)S(1)}, u32[]{:S(2)}, u32[]{:S(2)}) collective-permute-start(bf16[4,56,1664]{2,1,0:T(8,128)(2,1)S(1)} %copy-done.60), channel_id=1, source_target_pairs={{0,24},{8,16},{16,8},{24,0},{1,25},{9,17},{17,9},{25,1},{2,26},{10... | collective-permute-start | bytes 2236424 | tf_op jit(solution)/shard_map/ppermute | solution.py:63
  57.6 46.2 %copy-start.72 = (bf16[1,2,56,1024]{3,2,1,0:T(8,128)(2,1)}, bf16[1,2,56,1024]{3,2,1,0:T(8,128)(2,1)S(1)}, u32[]{:S(2)}) copy-start(bf16[1,2,56,1024]{3,2,1,0:T(8,128)(2,1)S(1)} %fusion.135) | copy-start | bytes 688132
  58.7 45.1 %collective-permute-start.7 = (bf16[2,2,56,1024]{3,2,1,0:T(8,128)(2,1)S(1)}, bf16[2,2,56,1024]{3,2,1,0:T(8,128)(2,1)S(1)}, u32[]{:S(2)}, u32[]{:S(2)}) collective-permute-start(bf16[2,2,56,1024]{3,2,1,0:T(8,128)(2,1)S(1)} %pad_maximum_fusion.18), channel_id=1, source_target_pairs={{0,4},{1,5},{2,6},{3,7},{4,0},{5,1},{6,2},{7,3},{8,12},{9,13},{10,... | collective-permute-start | bytes 1376264 | tf_op jit(solution)/shard_map/ppermute | solution.py:63
  108.6 8.1 %collective-permute-start.8 = (bf16[4,4,56,1664]{3,2,1,0:T(8,128)(2,1)S(1)}, bf16[4,4,56,1664]{3,2,1,0:T(8,128)(2,1)}, u32[]{:S(2)}, u32[]{:S(2)}) collective-permute-start(bf16[4,4,56,1664]{3,2,1,0:T(8,128)(2,1)S(1)} %pad_maximum_fusion.4.same_ref), channel_id=1, source_target_pairs={{0,1},{1,0},{2,3},{3,2},{4,5},{5,4},{6,7},{7,6},{8,9},{9,8},{10,11... | collective-permute-start | bytes 8945672 | tf_op jit(solution)/shard_map/ppermute | solution.py:63
  112.0 4.6 collective-permute-start.9
  113.1 31.3 %copy-start.134 = (f32[1632]{0:T(1024)}, f32[1632]{0:T(1024)S(1)}, u32[]{:S(2)}) copy-start(f32[1632]{0:T(1024)S(1)} %rsqrt.36) | copy-start | bytes 19588
  114.0 25.6 %copy-start.136 = (s32[768]{0:T(1024)}, s32[768]{0:T(1024)S(1)}, u32[]{:S(2)}) copy-start(s32[768]{0:T(1024)S(1)} %fusion.91) | copy-start | bytes 9220
  116.6 282.6 %reduce-scatter.6.cloned.1.call-start = ((), (), s32[]{:S(2)}) async-start(), calls=%async_computation.5 | async-start | bytes 2064384 | tf_op jit(solution)/shard_map/reduce_scatter | solution.py:800
  152.1 2.5 collective-permute-start.10
  155.7 11.4 %collective-permute-start.11 = (bf16[112,1024]{1,0:T(8,128)(2,1)}, bf16[112,1024]{1,0:T(8,128)(2,1)S(1)}, u32[]{:S(2)}, u32[]{:S(2)}) collective-permute-start(bf16[112,1024]{1,0:T(8,128)(2,1)} %after.22), channel_id=1, source_target_pairs={{0,2},{1,3},{2,0},{3,1},{4,6},{5,7},{6,4},{7,5},{8,10},{9,11},{10,... | collective-permute-start | bytes 688136 | tf_op jit(solution)/shard_map/ppermute | solution.py:63
  157.4 39.0 %collective-permute-start.12 = (bf16[112,1024]{1,0:T(8,128)(2,1)}, bf16[112,1024]{1,0:T(8,128)(2,1)S(1)}, u32[]{:S(2)}, u32[]{:S(2)}) collective-permute-start(bf16[112,1024]{1,0:T(8,128)(2,1)} %after.22), channel_id=1, source_target_pairs={{0,4},{1,5},{2,6},{3,7},{4,0},{5,1},{6,2},{7,3},{8,12},{9,13},{10,... | collective-permute-start | bytes 688136 | tf_op jit(solution)/shard_map/ppermute | solution.py:63
  157.7 38.7 %collective-permute-start.13 = (bf16[112,1024]{1,0:T(8,128)(2,1)}, bf16[112,1024]{1,0:T(8,128)(2,1)S(1)}, u32[]{:S(2)}, u32[]{:S(2)}) collective-permute-start(bf16[112,1024]{1,0:T(8,128)(2,1)} %after.22), channel_id=1, source_target_pairs={{0,6},{1,7},{2,4},{3,5},{4,2},{5,3},{6,0},{7,1},{8,14},{9,15},{10,... | collective-permute-start | bytes 688136 | tf_op jit(solution)/shard_map/ppermute | solution.py:63
  161.3 36.2 %collective-permute-start.15 = (bf16[112,1024]{1,0:T(8,128)(2,1)S(1)}, bf16[112,1024]{1,0:T(8,128)(2,1)S(1)}, u32[]{:S(2)}, u32[]{:S(2)}) collective-permute-start(bf16[112,1024]{1,0:T(8,128)(2,1)S(1)} %get-tuple-element.360), channel_id=1, source_target_pairs={{0,2},{1,3},{2,0},{3,1},{4,6},{5,7},{6,4},{7,5},{8,10},{9,11},{10,... | collective-permute-start | bytes 688136 | tf_op jit(solution)/shard_map/ppermute | solution.py:63
  162.1 35.3 %collective-permute-start.16 = (bf16[112,1024]{1,0:T(8,128)(2,1)S(1)}, bf16[112,1024]{1,0:T(8,128)(2,1)S(1)}, u32[]{:S(2)}, u32[]{:S(2)}) collective-permute-start(bf16[112,1024]{1,0:T(8,128)(2,1)S(1)} %get-tuple-element.359), channel_id=1, source_target_pairs={{0,4},{1,5},{2,6},{3,7},{4,0},{5,1},{6,2},{7,3},{8,12},{9,13},{10,... | collective-permute-start | bytes 688136 | tf_op jit(solution)/shard_map/ppermute | solution.py:63
  167.1 30.4 %collective-permute-start.17 = (bf16[112,1024]{1,0:T(8,128)(2,1)S(1)}, bf16[112,1024]{1,0:T(8,128)(2,1)S(1)}, u32[]{:S(2)}, u32[]{:S(2)}) collective-permute-start(bf16[112,1024]{1,0:T(8,128)(2,1)S(1)} %get-tuple-element.358), channel_id=1, source_target_pairs={{0,6},{1,7},{2,4},{3,5},{4,2},{5,3},{6,0},{7,1},{8,14},{9,15},{10,... | collective-permute-start | bytes 688136 | tf_op jit(solution)/shard_map/ppermute | solution.py:63
  197.4 36.0 %collective-permute-start.14 = (bf16[4,112,1024]{2,1,0:T(8,128)(2,1)}, bf16[4,112,1024]{2,1,0:T(8,128)(2,1)S(1)}, u32[]{:S(2)}, u32[]{:S(2)}) collective-permute-start(bf16[4,112,1024]{2,1,0:T(8,128)(2,1)} %get-tuple-element.362), channel_id=1, source_target_pairs={{0,1},{1,0},{2,3},{3,2},{4,5},{5,4},{6,7},{7,6},{8,9},{9,8},{10,11... | collective-permute-start | bytes 2752520 | tf_op jit(solution)/shard_map/ppermute | solution.py:63
  203.9 20.6 %collective-permute-start.18 = (bf16[112,1024]{1,0:T(8,128)(2,1)S(1)}, bf16[112,1024]{1,0:T(8,128)(2,1)S(1)}, u32[]{:S(2)}, u32[]{:S(2)}) collective-permute-start(bf16[112,1024]{1,0:T(8,128)(2,1)S(1)} %bitcast.556), channel_id=1, source_target_pairs={{0,2},{1,3},{2,0},{3,1},{4,6},{5,7},{6,4},{7,5},{8,10},{9,11},{10,... | collective-permute-start | bytes 688136 | tf_op jit(solution)/shard_map/ppermute | solution.py:63
  207.5 18.7 %collective-permute-start.19 = (bf16[112,1024]{1,0:T(8,128)(2,1)S(1)}, bf16[112,1024]{1,0:T(8,128)(2,1)S(1)}, u32[]{:S(2)}, u32[]{:S(2)}) collective-permute-start(bf16[112,1024]{1,0:T(8,128)(2,1)S(1)} %bitcast.557), channel_id=1, source_target_pairs={{0,4},{1,5},{2,6},{3,7},{4,0},{5,1},{6,2},{7,3},{8,12},{9,13},{10,... | collective-permute-start | bytes 688136 | tf_op jit(solution)/shard_map/ppermute | solution.py:63
  207.5 18.7 %collective-permute-start.20 = (bf16[112,1024]{1,0:T(8,128)(2,1)S(1)}, bf16[112,1024]{1,0:T(8,128)(2,1)S(1)}, u32[]{:S(2)}, u32[]{:S(2)}) collective-permute-start(bf16[112,1024]{1,0:T(8,128)(2,1)S(1)} %bitcast.558), channel_id=1, source_target_pairs={{0,6},{1,7},{2,4},{3,5},{4,2},{5,3},{6,0},{7,1},{8,14},{9,15},{10,... | collective-permute-start | bytes 688136 | tf_op jit(solution)/shard_map/ppermute | solution.py:63
  229.5 6.4 %collective-permute-start.21 = (bf16[4,112,1024]{2,1,0:T(8,128)(2,1)}, bf16[4,112,1024]{2,1,0:T(8,128)(2,1)}, u32[]{:S(2)}, u32[]{:S(2)}) collective-permute-start(bf16[4,112,1024]{2,1,0:T(8,128)(2,1)} %get-tuple-element.357), channel_id=1, source_target_pairs={{0,1},{1,0},{2,3},{3,2},{4,5},{5,4},{6,7},{7,6},{8,9},{9,8},{10,11... | collective-permute-start | bytes 2752520 | tf_op jit(solution)/shard_map/ppermute | solution.py:63
  247.1 271.0 %reduce-scatter.8.cloned.1.call-start = ((), (), s32[]{:S(2)}) async-start(), calls=%async_computation.6 | async-start | bytes 3932160 | tf_op jit(solution)/shard_map/reduce_scatter | solution.py:809
  253.8 3.7 collective-permute-start.22
  254.7 85.1 %copy-start.11 = (bf16[640,768]{1,0:T(8,128)(2,1)}, bf16[640,768]{1,0:T(8,128)(2,1)S(1)}, u32[]{:S(2)}) copy-start(bf16[640,768]{1,0:T(8,128)(2,1)S(1)} %fusion.16.refs_1_) | copy-start | bytes 2949124
  259.0 39.2 %collective-permute-start.23 = (bf16[112,1024]{1,0:T(8,128)(2,1)S(1)}, bf16[112,1024]{1,0:T(8,128)(2,1)S(1)}, u32[]{:S(2)}, u32[]{:S(2)}) collective-permute-start(bf16[112,1024]{1,0:T(8,128)(2,1)S(1)} %get-tuple-element.355), channel_id=1, source_target_pairs={{0,2},{1,3},{2,0},{3,1},{4,6},{5,7},{6,4},{7,5},{8,10},{9,11},{10,... | collective-permute-start | bytes 688136 | tf_op jit(solution)/shard_map/ppermute | solution.py:63
  263.0 35.3 %collective-permute-start.24 = (bf16[112,1024]{1,0:T(8,128)(2,1)S(1)}, bf16[112,1024]{1,0:T(8,128)(2,1)S(1)}, u32[]{:S(2)}, u32[]{:S(2)}) collective-permute-start(bf16[112,1024]{1,0:T(8,128)(2,1)S(1)} %get-tuple-element.354), channel_id=1, source_target_pairs={{0,4},{1,5},{2,6},{3,7},{4,0},{5,1},{6,2},{7,3},{8,12},{9,13},{10,... | collective-permute-start | bytes 688136 | tf_op jit(solution)/shard_map/ppermute | solution.py:63
  263.0 35.3 %collective-permute-start.25 = (bf16[112,1024]{1,0:T(8,128)(2,1)S(1)}, bf16[112,1024]{1,0:T(8,128)(2,1)S(1)}, u32[]{:S(2)}, u32[]{:S(2)}) collective-permute-start(bf16[112,1024]{1,0:T(8,128)(2,1)S(1)} %get-tuple-element.353), channel_id=1, source_target_pairs={{0,6},{1,7},{2,4},{3,5},{4,2},{5,3},{6,0},{7,1},{8,14},{9,15},{10,... | collective-permute-start | bytes 688136 | tf_op jit(solution)/shard_map/ppermute | solution.py:63
  302.7 57.6 %collective-permute-start.27 = (bf16[112,1024]{1,0:T(8,128)(2,1)S(1)}, bf16[112,1024]{1,0:T(8,128)(2,1)S(1)}, u32[]{:S(2)}, u32[]{:S(2)}) collective-permute-start(bf16[112,1024]{1,0:T(8,128)(2,1)S(1)} %convolution_convert_fusion.9.refs_16_), channel_id=1, source_target_pairs={{0,2},{1,3},{2,0},{3,1},{4,6},{5,7},{6,4},{7,5},{8,10},{9,11},{10,... | collective-permute-start | bytes 688136 | tf_op jit(solution)/shard_map/ppermute | solution.py:63
  303.8 56.5 %collective-permute-start.28 = (bf16[112,1024]{1,0:T(8,128)(2,1)S(1)}, bf16[112,1024]{1,0:T(8,128)(2,1)}, u32[]{:S(2)}, u32[]{:S(2)}) collective-permute-start(bf16[112,1024]{1,0:T(8,128)(2,1)S(1)} %convolution_convert_fusion.9.refs_16_), channel_id=1, source_target_pairs={{0,4},{1,5},{2,6},{3,7},{4,0},{5,1},{6,2},{7,3},{8,12},{9,13},{10,... | collective-permute-start | bytes 688136 | tf_op jit(solution)/shard_map/ppermute | solution.py:63
  304.7 55.6 %collective-permute-start.29 = (bf16[112,1024]{1,0:T(8,128)(2,1)S(1)}, bf16[112,1024]{1,0:T(8,128)(2,1)}, u32[]{:S(2)}, u32[]{:S(2)}) collective-permute-start(bf16[112,1024]{1,0:T(8,128)(2,1)S(1)} %convolution_convert_fusion.9.refs_16_), channel_id=1, source_target_pairs={{0,6},{1,7},{2,4},{3,5},{4,2},{5,3},{6,0},{7,1},{8,14},{9,15},{10,... | collective-permute-start | bytes 688136 | tf_op jit(solution)/shard_map/ppermute | solution.py:63
  310.5 271.8 %reduce-scatter.10.cloned.1.call-start = ((), (), s32[]{:S(2)}) async-start(), calls=%async_computation.9 | async-start | bytes 6285312
  363.2 7.0 %collective-permute-start.30 = (bf16[4,112,1024]{2,1,0:T(8,128)(2,1)S(1)}, bf16[4,112,1024]{2,1,0:T(8,128)(2,1)S(1)}, u32[]{:S(2)}, u32[]{:S(2)}) collective-permute-start(bf16[4,112,1024]{2,1,0:T(8,128)(2,1)S(1)} %get-tuple-element.352), channel_id=1, source_target_pairs={{0,1},{1,0},{2,3},{3,2},{4,5},{5,4},{6,7},{7,6},{8,9},{9,8},{10,11... | collective-permute-start | bytes 2752520 | tf_op jit(solution)/shard_map/ppermute | solution.py:63
  367.2 33.8 %collective-permute-start.26 = (bf16[4,4,24,4096]{3,2,1,0:T(8,128)(2,1)}, bf16[4,4,24,4096]{3,2,1,0:T(8,128)(2,1)}, u32[]{:S(2)}, u32[]{:S(2)}) collective-permute-start(bf16[4,4,24,4096]{3,2,1,0:T(8,128)(2,1)} %dynamic-slice_bitcast_fusion), channel_id=1, source_target_pairs={{0,1},{1,0},{2,3},{3,2},{4,5},{5,4},{6,7},{7,6},{8,9},{9,8},{10,11... | collective-permute-start | bytes 9437192 | tf_op jit(solution)/shard_map/ppermute | solution.py:63
  394.3 56.4 %collective-permute-start.34 = (bf16[4,4,32,1664]{3,2,1,0:T(8,128)(2,1)}, bf16[4,4,32,1664]{3,2,1,0:T(8,128)(2,1)}, u32[]{:S(2)}, u32[]{:S(2)}) collective-permute-start(bf16[4,4,32,1664]{3,2,1,0:T(8,128)(2,1)} %dynamic-slice_bitcast_fusion.1), channel_id=1, source_target_pairs={{0,1},{1,0},{2,3},{3,2},{4,5},{5,4},{6,7},{7,6},{8,9},{9,8},{10,11... | collective-permute-start | bytes 5111816 | tf_op jit(solution)/shard_map/ppermute | solution.py:63
  399.2 103.6 %collective-permute-start.41 = (bf16[4,112,1024]{2,1,0:T(8,128)(2,1)}, bf16[4,112,1024]{2,1,0:T(8,128)(2,1)}, u32[]{:S(2)}, u32[]{:S(2)}) collective-permute-start(bf16[4,112,1024]{2,1,0:T(8,128)(2,1)} %slice_bitcast_fusion), channel_id=1, source_target_pairs={{0,1},{1,0},{2,3},{3,2},{4,5},{5,4},{6,7},{7,6},{8,9},{9,8},{10,11... | collective-permute-start | bytes 2752520 | tf_op jit(solution)/shard_map/ppermute | solution.py:63
  407.5 43.3 %collective-permute-start.31 = (bf16[4,24,4096]{2,1,0:T(8,128)(2,1)}, bf16[4,24,4096]{2,1,0:T(8,128)(2,1)S(1)}, u32[]{:S(2)}, u32[]{:S(2)}) collective-permute-start(bf16[4,24,4096]{2,1,0:T(8,128)(2,1)} %get-tuple-element.337), channel_id=1, source_target_pairs={{0,8},{8,0},{16,24},{24,16},{1,9},{9,1},{17,25},{25,17},{2,10},{10... | collective-permute-start | bytes 2359304 | tf_op jit(solution)/shard_map/ppermute | solution.py:63
  414.1 36.7 %collective-permute-start.32 = (bf16[4,24,4096]{2,1,0:T(8,128)(2,1)}, bf16[4,24,4096]{2,1,0:T(8,128)(2,1)S(1)}, u32[]{:S(2)}, u32[]{:S(2)}) collective-permute-start(bf16[4,24,4096]{2,1,0:T(8,128)(2,1)} %get-tuple-element.336), channel_id=1, source_target_pairs={{0,16},{8,24},{16,0},{24,8},{1,17},{9,25},{17,1},{25,9},{2,18},{10... | collective-permute-start | bytes 2359304 | tf_op jit(solution)/shard_map/ppermute | solution.py:63
  414.8 36.0 %collective-permute-start.33 = (bf16[4,24,4096]{2,1,0:T(8,128)(2,1)S(1)}, bf16[4,24,4096]{2,1,0:T(8,128)(2,1)S(1)}, u32[]{:S(2)}, u32[]{:S(2)}) collective-permute-start(bf16[4,24,4096]{2,1,0:T(8,128)(2,1)S(1)} %get-tuple-element.335), channel_id=1, source_target_pairs={{0,24},{8,16},{16,8},{24,0},{1,25},{9,17},{17,9},{25,1},{2,26},{10... | collective-permute-start | bytes 2359304 | tf_op jit(solution)/shard_map/ppermute | solution.py:63
  455.6 30.6 %collective-permute-start.36 = (bf16[4,32,1664]{2,1,0:T(8,128)(2,1)}, bf16[4,32,1664]{2,1,0:T(8,128)(2,1)S(1)}, u32[]{:S(2)}, u32[]{:S(2)}) collective-permute-start(bf16[4,32,1664]{2,1,0:T(8,128)(2,1)} %get-tuple-element.342), channel_id=1, source_target_pairs={{0,8},{8,0},{16,24},{24,16},{1,9},{9,1},{17,25},{25,17},{2,10},{10... | collective-permute-start | bytes 1277960 | tf_op jit(solution)/shard_map/ppermute | solution.py:63
  457.7 28.6 %collective-permute-start.37 = (bf16[4,32,1664]{2,1,0:T(8,128)(2,1)S(1)}, bf16[4,32,1664]{2,1,0:T(8,128)(2,1)S(1)}, u32[]{:S(2)}, u32[]{:S(2)}) collective-permute-start(bf16[4,32,1664]{2,1,0:T(8,128)(2,1)S(1)} %get-tuple-element.341), channel_id=1, source_target_pairs={{0,16},{8,24},{16,0},{24,8},{1,17},{9,25},{17,1},{25,9},{2,18},{10... | collective-permute-start | bytes 1277960 | tf_op jit(solution)/shard_map/ppermute | solution.py:63
  458.3 28.7 %collective-permute-start.38 = (bf16[4,32,1664]{2,1,0:T(8,128)(2,1)S(1)}, bf16[4,32,1664]{2,1,0:T(8,128)(2,1)}, u32[]{:S(2)}, u32[]{:S(2)}) collective-permute-start(bf16[4,32,1664]{2,1,0:T(8,128)(2,1)S(1)} %get-tuple-element.340), channel_id=1, source_target_pairs={{0,24},{8,16},{16,8},{24,0},{1,25},{9,17},{17,9},{25,1},{2,26},{10... | collective-permute-start | bytes 1277960 | tf_op jit(solution)/shard_map/ppermute | solution.py:63
  461.8 24.5 %collective-permute-start.35 = (bf16[2,24,4096]{2,1,0:T(8,128)(2,1)}, bf16[2,24,4096]{2,1,0:T(8,128)(2,1)S(1)}, u32[]{:S(2)}, u32[]{:S(2)}) collective-permute-start(bf16[2,24,4096]{2,1,0:T(8,128)(2,1)} %dynamic-slice_bitcast_fusion.9), channel_id=1, source_target_pairs={{0,2},{1,3},{2,0},{3,1},{4,6},{5,7},{6,4},{7,5},{8,10},{9,11},{10,... | collective-permute-start | bytes 1179656 | tf_op jit(solution)/shard_map/ppermute | solution.py:63
  489.4 21.6 %collective-permute-start.40 = (bf16[2,32,1664]{2,1,0:T(8,128)(2,1)S(1)}, bf16[2,32,1664]{2,1,0:T(8,128)(2,1)S(1)}, u32[]{:S(2)}, u32[]{:S(2)}) collective-permute-start(bf16[2,32,1664]{2,1,0:T(8,128)(2,1)S(1)} %dynamic-slice_bitcast_fusion.13), channel_id=1, source_target_pairs={{0,2},{1,3},{2,0},{3,1},{4,6},{5,7},{6,4},{7,5},{8,10},{9,11},{10,... | collective-permute-start | bytes 638984 | tf_op jit(solution)/shard_map/ppermute | solution.py:63
  490.6 20.4 %collective-permute-start.39 = (bf16[1,24,4096]{2,1,0:T(8,128)(2,1)S(1)}, bf16[1,24,4096]{2,1,0:T(8,128)(2,1)S(1)}, u32[]{:S(2)}, u32[]{:S(2)}) collective-permute-start(bf16[1,24,4096]{2,1,0:T(8,128)(2,1)S(1)} %constant_dynamic-slice_fusion.2), channel_id=1, source_target_pairs={{0,4},{1,5},{2,6},{3,7},{4,0},{5,1},{6,2},{7,3},{8,12},{9,13},{10,... | collective-permute-start | bytes 589832 | tf_op jit(solution)/shard_map/ppermute | solution.py:63
  502.7 23.6 %collective-permute-start.46 = (bf16[4,4,24,1536]{3,2,1,0:T(8,128)(2,1)}, bf16[4,4,24,1536]{3,2,1,0:T(8,128)(2,1)}, u32[]{:S(2)}, u32[]{:S(2)}) collective-permute-start(bf16[4,4,24,1536]{3,2,1,0:T(8,128)(2,1)} %dynamic-slice_bitcast_fusion.2), channel_id=1, source_target_pairs={{0,1},{1,0},{2,3},{3,2},{4,5},{5,4},{6,7},{7,6},{8,9},{9,8},{10,11... | collective-permute-start | bytes 3538952 | tf_op jit(solution)/shard_map/ppermute | solution.py:63
  513.4 13.0 %collective-permute-start.45 = (bf16[1,32,1664]{2,1,0:T(8,128)(2,1)S(1)}, bf16[1,32,1664]{2,1,0:T(8,128)(2,1)S(1)}, u32[]{:S(2)}, u32[]{:S(2)}) collective-permute-start(bf16[1,32,1664]{2,1,0:T(8,128)(2,1)S(1)} %constant_dynamic-slice_fusion.1), channel_id=1, source_target_pairs={{0,4},{1,5},{2,6},{3,7},{4,0},{5,1},{6,2},{7,3},{8,12},{9,13},{10,... | collective-permute-start | bytes 319496 | tf_op jit(solution)/shard_map/ppermute | solution.py:63
  521.9 56.4 %all-to-all-start.1 = ((bf16[8,32,1024]{2,1,0:T(8,128)(2,1)}), bf16[8,32,1024]{2,1,0:T(8,128)(2,1)}, u32[]{:S(2)}, u32[]{:S(2)}) async-start(bf16[8,32,1024]{2,1,0:T(8,128)(2,1)} %bitcast.212), calls=%async_computation.3 | async-start | bytes 1048576 | tf_op jit(solution)/shard_map/all_to_all | solution.py:902
  532.5 26.7 %collective-permute-start.47 = (bf16[4,24,1536]{2,1,0:T(8,128)(2,1)}, bf16[4,24,1536]{2,1,0:T(8,128)(2,1)}, u32[]{:S(2)}, u32[]{:S(2)}) collective-permute-start(bf16[4,24,1536]{2,1,0:T(8,128)(2,1)} %get-tuple-element.345), channel_id=1, source_target_pairs={{0,8},{8,0},{16,24},{24,16},{1,9},{9,1},{17,25},{25,17},{2,10},{10... | collective-permute-start | bytes 884744 | tf_op jit(solution)/shard_map/ppermute | solution.py:63
  535.1 24.1 %collective-permute-start.48 = (bf16[4,24,1536]{2,1,0:T(8,128)(2,1)}, bf16[4,24,1536]{2,1,0:T(8,128)(2,1)}, u32[]{:S(2)}, u32[]{:S(2)}) collective-permute-start(bf16[4,24,1536]{2,1,0:T(8,128)(2,1)} %get-tuple-element.344), channel_id=1, source_target_pairs={{0,16},{8,24},{16,0},{24,8},{1,17},{9,25},{17,1},{25,9},{2,18},{10... | collective-permute-start | bytes 884744 | tf_op jit(solution)/shard_map/ppermute | solution.py:63
  537.3 21.9 %collective-permute-start.49 = (bf16[4,24,1536]{2,1,0:T(8,128)(2,1)}, bf16[4,24,1536]{2,1,0:T(8,128)(2,1)}, u32[]{:S(2)}, u32[]{:S(2)}) collective-permute-start(bf16[4,24,1536]{2,1,0:T(8,128)(2,1)} %get-tuple-element.343), channel_id=1, source_target_pairs={{0,24},{8,16},{16,8},{24,0},{1,25},{9,17},{17,9},{25,1},{2,26},{10... | collective-permute-start | bytes 884744 | tf_op jit(solution)/shard_map/ppermute | solution.py:63
  538.3 23.4 %collective-permute-start.42 = (bf16[112,1024]{1,0:T(8,128)(2,1)}, bf16[112,1024]{1,0:T(8,128)(2,1)}, u32[]{:S(2)}, u32[]{:S(2)}) collective-permute-start(bf16[112,1024]{1,0:T(8,128)(2,1)} %get-tuple-element.348), channel_id=1, source_target_pairs={{0,2},{1,3},{2,0},{3,1},{4,6},{5,7},{6,4},{7,5},{8,10},{9,11},{10,... | collective-permute-start | bytes 688136 | tf_op jit(solution)/shard_map/ppermute | solution.py:63
  540.3 21.4 %collective-permute-start.43 = (bf16[112,1024]{1,0:T(8,128)(2,1)}, bf16[112,1024]{1,0:T(8,128)(2,1)}, u32[]{:S(2)}, u32[]{:S(2)}) collective-permute-start(bf16[112,1024]{1,0:T(8,128)(2,1)} %get-tuple-element.350), channel_id=1, source_target_pairs={{0,4},{1,5},{2,6},{3,7},{4,0},{5,1},{6,2},{7,3},{8,12},{9,13},{10,... | collective-permute-start | bytes 688136 | tf_op jit(solution)/shard_map/ppermute | solution.py:63
  559.2 9.8 %collective-permute-start.44 = (bf16[112,1024]{1,0:T(8,128)(2,1)S(1)}, bf16[112,1024]{1,0:T(8,128)(2,1)S(1)}, u32[]{:S(2)}, u32[]{:S(2)}) collective-permute-start(bf16[112,1024]{1,0:T(8,128)(2,1)S(1)} %copy-done.118), channel_id=1, source_target_pairs={{0,6},{1,7},{2,4},{3,5},{4,2},{5,3},{6,0},{7,1},{8,14},{9,15},{10,... | collective-permute-start | bytes 688136 | tf_op jit(solution)/shard_map/ppermute | solution.py:63
  560.8 9.6 %collective-permute-start.50 = (bf16[2,24,1536]{2,1,0:T(8,128)(2,1)S(1)}, bf16[2,24,1536]{2,1,0:T(8,128)(2,1)S(1)}, u32[]{:S(2)}, u32[]{:S(2)}) collective-permute-start(bf16[2,24,1536]{2,1,0:T(8,128)(2,1)S(1)} %dynamic-slice_bitcast_fusion.14), channel_id=1, source_target_pairs={{0,2},{1,3},{2,0},{3,1},{4,6},{5,7},{6,4},{7,5},{8,10},{9,11},{10,... | collective-permute-start | bytes 442376 | tf_op jit(solution)/shard_map/ppermute | solution.py:63
  570.5 5.8 collective-permute-start.51
  (150 other events, 757.1 us)
Sparse Core Ops, SparseCore 0:
  11.5 127.5 all-gather.4
  141.0 42.2 all-gather.6
  247.2 46.7 reduce-scatter.5
  310.6 45.7 reduce-scatter.7
  434.5 127.9 reduce-scatter.9
